TPU v7x, 32 devices: a whole 2x2x4 slice. The times are simulated.
32 devices in a mesh: row: 4 (over y, core), col: 8 (over z, x).
Axes of the slice: x: 2, y: 2, z: 4, core: 2. Of those that a mesh axis runs over, the one named last changes fastest.
Arguments:
- river_lower: float32 [64, 2, 2, 8192], P('row', None, None, 'col'), may hold values from -1.3 to 0.6, as said below
- river_main: float32 [64, 2, 2, 8192], P('row', None, None, 'col'), may hold values from -0.9 to 2.01
- river_upper: float32 [64, 2, 2, 8192], P('row', None, None, 'col'), may hold values from -1.3 to 0.6
- river_rhs: float32 [64, 2, 8192], P('row', None, 'col'), may hold values from -0.08 to 0.08
- weir_crest: float32 [64, 8192], P('row', 'col'), may hold values from -1 to 1
- weir_regime: int32 [64, 8192], P('row', 'col'), may hold values from 0 to 2
- weir_tile: int32 [4, 8, 16, 1024, 1], P('row', 'col'), may hold values from 0 to 31; in each aligned block of 16384 rows (0 to 16383, 16384 to 32767, ..., all dimensions but the last counted through in order) at most 1024 rows name the same one
- weir_row: int32 [64, 8192], P('row', 'col'), may hold values from 0 to 31
- weir_col: int32 [64, 8192], P('row', 'col'), may hold values from 0 to 511
- bed_level: float32 [128, 4096], P('row', 'col'), may hold values from -1 to 0
- water_depth: float32 [128, 4096], P('row', 'col'), may hold values from 0.02 to 1.5
- flux_first: float32 [128, 4096], P('row', 'col'), may hold values from -2.4 to 2.4
- flux_second: float32 [128, 4096], P('row', 'col'), may hold values from -2.4 to 2.4
- wet_mask: int32 [128, 4096], P('row', 'col'), may hold values 0 or 1
Outputs:
- river_state: float32 [64, 2, 8192], P('row', None, 'col')
- depth_out: float32 [128, 4096], P('row', 'col')
- first_out: float32 [128, 4096], P('row', 'col')
- second_out: float32 [128, 4096], P('row', 'col')
Inputs may be any that keep to these rules, and one draw needn't show every extreme that they name: `river_lower`: together with river_main and river_upper, the block matrix of each chain has a positive definite symmetric part. Of the weirs in one device's block weir_tile[r, c], at most 1024 feed the same tile, and in some device's block a tile is fed by exactly 1024.
All inputs are finite; a program needn't handle non-finite values. No bound on the sum of `wet_mask` on one device may be relied on, other than what follows from the above.
Results may differ from a plain program's by a relative error of at most 0.0003.
Values sent between devices are 32-bit elements; how exact they have to be, the bound alone decides.
No kernel may reach another device: no remote copies, remote signals or barrier semaphores. Data moves between devices by JAX's collectives and lax.ppermute only.
A program may use at most 64 MiB of HBM per device.

v0:
```python
import functools

import jax
import jax.numpy as jnp
from jax import lax
from jax.experimental import pallas as pl
from jax.experimental.pallas import tpu as pltpu
from jax.sharding import PartitionSpec as P

GRAVITY = 9.81
TIME_STEP = 1.0
CELL_WIDTH = 10.0
MANNING_SQ = 0.0009
DEPTH_FLOOR = 0.05
WEIR_GAIN = 0.5
FREE_COEF = 0.5
SUB_COEF = 0.4
SUB_OFFSET = 0.25
GATE_COEF = 0.2

F32 = jnp.float32
BF16 = jnp.bfloat16
LANES = 128
LOW = 256
VMEM = pl.BlockSpec(memory_space=pltpu.VMEM)
SMEM = pl.BlockSpec(memory_space=pltpu.SMEM)
PARAMS = pltpu.CompilerParams(vmem_limit_bytes=40 * 2**20)


def mat_mat(a, b):
    return [[a[i][0] * b[0][j] + a[i][1] * b[1][j] for j in range(2)] for i in range(2)]


def mat_vec(a, v):
    return [a[i][0] * v[0] + a[i][1] * v[1] for i in range(2)]


def mat_sub(a, b):
    return [[a[i][j] - b[i][j] for j in range(2)] for i in range(2)]


def mat_neg(a):
    return [[-a[i][j] for j in range(2)] for i in range(2)]


def mat_inv(m):
    scale = 1.0 / (m[0][0] * m[1][1] - m[0][1] * m[1][0])
    return [[m[1][1] * scale, -m[0][1] * scale], [-m[1][0] * scale, m[0][0] * scale]]


def solve_kernel(sections, lower_ref, main_ref, upper_ref, rhs_ref, solved_ref, packed_ref):
    def block(ref, k):
        return [[ref[pl.ds(k * 32 + i * 16 + j, 8, stride=2), :] for j in range(2)] for i in range(2)]

    couples = []
    for k in range(sections):
        lower = block(lower_ref, k)
        main = block(main_ref, k)
        upper = block(upper_ref, k)
        right = [rhs_ref[pl.ds(k * 16 + j, 8, stride=2), :] for j in range(2)]
        if k == 0:
            inverse = mat_inv(main)
            left = mat_neg(mat_mat(inverse, lower))
            value = mat_vec(inverse, right)
        else:
            inverse = mat_inv(mat_sub(main, mat_mat(lower, couples[-1])))
            left = mat_neg(mat_mat(inverse, mat_mat(lower, left)))
            moved = mat_vec(lower, value)
            value = mat_vec(inverse, [right[i] - moved[i] for i in range(2)])
        couples.append(mat_mat(inverse, upper))
        for i in range(2):
            solved_ref[k, i] = value[i]
            for j in range(2):
                solved_ref[k, 2 + 2 * i + j] = left[i][j]
    spike = mat_neg(couples[-1])
    tail = (value, left, spike)
    for i in range(2):
        for j in range(2):
            solved_ref[sections - 1, 6 + 2 * i + j] = spike[i][j]
    for k in range(sections - 2, -1, -1):
        couple = couples[k]
        after = mat_vec(couple, value)
        value = [solved_ref[k, i] - after[i] for i in range(2)]
        after = mat_mat(couple, left)
        left = [[solved_ref[k, 2 + 2 * i + j] - after[i][j] for j in range(2)] for i in range(2)]
        spike = mat_neg(mat_mat(couple, spike))
        for i in range(2):
            solved_ref[k, i] = value[i]
            for j in range(2):
                solved_ref[k, 2 + 2 * i + j] = left[i][j]
                solved_ref[k, 6 + 2 * i + j] = spike[i][j]
    for i in range(2):
        packed_ref[i] = value[i]
        packed_ref[2 + i] = tail[0][i]
        for j in range(2):
            packed_ref[4 + 2 * i + j] = left[i][j]
            packed_ref[8 + 2 * i + j] = tail[1][i][j]
            packed_ref[12 + 2 * i + j] = spike[i][j]
            packed_ref[16 + 2 * i + j] = tail[2][i][j]


def rank_kernel(tiles, capacity, groups, tile_ref, slot_ref):
    table = lax.broadcasted_iota(jnp.int32, (tiles, LANES), 0)
    row_at = lax.broadcasted_iota(jnp.int32, (LANES, 2 * LANES), 0)
    col_at = lax.broadcasted_iota(jnp.int32, (LANES, 2 * LANES), 1)
    earlier = jnp.where(row_at < col_at, 1.0, 0.0).astype(BF16)

    def body(g, offset):
        ids = tile_ref[pl.ds((g // 8) * 64 + g % 8, 8, stride=8), :]
        hits = [ids[r : r + 1, :] == table for r in range(8)]
        hot = jnp.concatenate([jnp.where(h, 1.0, 0.0).astype(BF16) for h in hits], 0)
        counts = jnp.dot(hot, earlier, preferred_element_type=F32)
        rows = []
        for r in range(8):
            part = counts[r * tiles : (r + 1) * tiles]
            place = jnp.where(hits[r], part[:, :LANES] + offset, 0.0)
            rows.append(jnp.sum(place, axis=0, keepdims=True))
            offset = offset + part[:, LANES:]
        slot_ref[pl.ds(g * 8, 8), :] = jnp.concatenate(rows, 0).astype(jnp.int32)
        return offset

    lax.fori_loop(0, groups, body, table.astype(F32) * capacity)


def rows16(row):
    return jnp.broadcast_to(row, (16, LANES)).astype(BF16)


def table16(count):
    shape = (count // 16, 16, LANES)
    at = lax.broadcasted_iota(jnp.int32, shape, 0) * 16 + lax.broadcasted_iota(jnp.int32, shape, 1)
    return at.astype(F32).astype(BF16)


def halves(value):
    high = value.astype(BF16).astype(F32)
    return high, value - high


def one_hots(high, low, values, high_table, low_table):
    one = jnp.ones((), BF16)
    zero = jnp.zeros((), BF16)
    left, right = [], []
    for r in range(8):
        hit = high_table == rows16(high[r : r + 1])[None]
        left.append(
            jnp.concatenate(
                [jnp.where(hit, rows16(v[r : r + 1])[None], zero).reshape(-1, LANES) for v in values], 0
            )
        )
        hit = low_table == rows16(low[r : r + 1])[None]
        right.append(jnp.where(hit, one, zero).reshape(-1, LANES))
    return jnp.concatenate(left, 1), jnp.concatenate(right, 1)


def product(left, right):
    return lax.dot_general(left, right, (((1,), (1,)), ((), ())), preferred_element_type=F32)


def weir_kernel(
    sections,
    segments,
    tiles,
    capacity,
    row_count,
    position_ref,
    gathered_ref,
    solved_ref,
    crest_ref,
    regime_ref,
    row_ref,
    col_ref,
    slot_ref,
    state_ref,
    out_ref,
    phase_ref,
    total_ref,
):
    def reduced(d):
        at = lambda n: gathered_ref[d, pl.ds(n * 8, 8), :]
        pair = lambda n: [at(n), at(n + 1)]
        square = lambda n: [[at(n), at(n + 1)], [at(n + 2), at(n + 3)]]
        return pair(0), pair(2), square(4), square(8), square(12), square(16)

    eliminated = []
    for d in range(segments):
        head_y, tail_y, head_left, tail_left, head_right, tail_right = reduced(d)
        if d == 0:
            first = (mat_neg(head_right), head_y)
            last = (mat_neg(tail_right), tail_y)
        else:
            couple, value = last
            inner = mat_mat(head_left, couple)
            inner = [[inner[0][0] + 1.0, inner[0][1]], [inner[1][0], inner[1][1] + 1.0]]
            inverse = mat_inv(inner)
            first_couple = mat_neg(mat_mat(inverse, head_right))
            moved = mat_vec(head_left, value)
            first_value = mat_vec(inverse, [head_y[i] + moved[i] for i in range(2)])
            bridge = mat_mat(tail_left, couple)
            through = mat_mat(bridge, first_couple)
            last_couple = [[-tail_right[i][j] - through[i][j] for j in range(2)] for i in range(2)]
            moved = mat_vec(tail_left, value)
            back = mat_vec(bridge, first_value)
            last_value = [tail_y[i] + moved[i] - back[i] for i in range(2)]
            first = (first_couple, first_value)
            last = (last_couple, last_value)
        eliminated.append((first, last))
    position = position_ref[0]
    nothing = [jnp.zeros((8, LANES), F32)] * 2
    upcoming = nothing
    after = nothing
    before = nothing
    for d in range(segments - 1, -1, -1):
        (first_couple, first_value), (last_couple, last_value) = eliminated[d]
        after = [jnp.where(position == d, upcoming[i], after[i]) for i in range(2)]
        moved = mat_vec(last_couple, upcoming)
        last_state = [last_value[i] - moved[i] for i in range(2)]
        before = [jnp.where(position == d + 1, last_state[i], before[i]) for i in range(2)]
        moved = mat_vec(first_couple, upcoming)
        upcoming = [first_value[i] - moved[i] for i in range(2)]
    for k in range(sections):
        for i in range(2):
            state = solved_ref[k, i]
            for j in range(2):
                state = state + solved_ref[k, 2 + 2 * i + j] * before[j]
                state = state + solved_ref[k, 6 + 2 * i + j] * after[j]
            state_ref[pl.ds(k * 16 + i, 8, stride=2), :] = state
            if i == 0:
                phase_ref[pl.ds((k // 8) * 64 + k % 8, 8, stride=8), :] = state

    high_count = tiles * capacity // LOW
    high_table = table16(high_count)
    low_table = table16(LOW)
    total_ref[...] = jnp.zeros_like(total_ref)

    def body(g, carry):
        over = pl.multiple_of((g // 8) * 8, 8)
        along = pl.multiple_of((g % 8) * LANES, LANES)
        at = (pl.ds(over, 8), pl.ds(along, LANES))
        rows = pl.ds(pl.multiple_of(g * 8, 8), 8)
        phase = phase_ref[rows, :]
        regime = regime_ref[at]
        head = jnp.maximum(phase - crest_ref[at], 0.0)
        free = jnp.where(regime == 0, FREE_COEF * head * jnp.sqrt(head), 0.0)
        sub = jnp.where(
            regime == 1,
            SUB_COEF * jnp.sqrt(head + SUB_OFFSET),
            jnp.where(regime == 2, GATE_COEF, 0.0),
        )
        constant = halves(WEIR_GAIN * (free + sub * phase))
        slope = halves(WEIR_GAIN * sub)
        col = col_ref[at]
        cell_high = (col // LOW) * row_count + row_ref[at]
        cell_low = (col % LOW).astype(F32)
        slot = slot_ref[rows, :]
        left, right = one_hots(
            (slot // LOW).astype(F32),
            (slot % LOW).astype(F32),
            [*constant, *slope, cell_high.astype(F32), cell_low],
            high_table,
            low_table,
        )
        total_ref[...] += product(left, right)
        return carry

    lax.fori_loop(0, sections * 8 // 8, body, 0, unroll=2)
    per_tile = capacity // LOW
    for v in range(3):
        scale = float(LOW) if v == 2 else 1.0
        start = 2 * v * high_count
        value = total_ref[pl.ds(start, high_count), :] * scale + total_ref[pl.ds(start + high_count, high_count), :]
        for t in range(tiles):
            for j in range(LOW // LANES):
                out_ref[t, pl.ds((v * (LOW // LANES) + j) * per_tile, per_tile), :] = value[
                    t * per_tile : (t + 1) * per_tile, j * LANES : (j + 1) * LANES
                ]


def apply_kernel(sources, rows_each, row_count, col_count, in_ref, bed_ref, depth_ref, wetted_ref, total_ref):
    high_count = row_count * col_count // LOW
    high_table = table16(high_count)
    low_table = table16(LOW)
    total_ref[...] = jnp.zeros_like(total_ref)
    step = 8 // rows_each if rows_each < 8 else 1

    def body(g, carry):
        def part(v):
            return jnp.concatenate(
                [in_ref[g * step + n, pl.ds(v * rows_each, rows_each), :] for n in range(step)], 0
            )

        constant = halves(part(0))
        slope = halves(part(1))
        cell = part(2).astype(jnp.int32)
        left, right = one_hots(
            (cell // LOW).astype(F32),
            (cell % LOW).astype(F32),
            [*constant, *slope],
            high_table,
            low_table,
        )
        total_ref[...] += product(left, right)
        return carry

    lax.fori_loop(0, sources // step, body, 0, unroll=2)
    for n in range(col_count // LOW):
        def summed(v):
            start = 2 * v * high_count + n * row_count
            return total_ref[pl.ds(start, row_count), :] + total_ref[pl.ds(start + high_count, row_count), :]

        cols = pl.ds(n * LOW, LOW)
        depth = depth_ref[:, cols]
        surface = bed_ref[:, cols] + depth
        wetted_ref[:, cols] = jnp.maximum(depth + (summed(0) - summed(1) * surface), 0.0)


def face_flux(eta_here, eta_next, bed_here, bed_next, old_flux):
    flow_depth = jnp.maximum(
        jnp.maximum(eta_here, eta_next) - jnp.maximum(bed_here, bed_next), DEPTH_FLOOR
    )
    gradient = (eta_next - eta_here) / CELL_WIDTH
    pushed = old_flux - GRAVITY * TIME_STEP * flow_depth * gradient
    friction = jnp.exp((-7.0 / 3.0) * jnp.log(flow_depth))
    return pushed / (1.0 + GRAVITY * TIME_STEP * MANNING_SQ * jnp.abs(old_flux) * friction)


def flood_kernel(row_count, col_count, closed_ref, in_ref, depth_ref, first_ref, second_ref):
    depth, bed, first, second, wet = (in_ref[n] for n in range(5))
    shape = depth.shape
    row_at = lax.broadcasted_iota(jnp.int32, shape, 0) - 8
    col_at = lax.broadcasted_iota(jnp.int32, shape, 1) - LANES
    first_shut = (row_at == closed_ref[0]) | (row_at == closed_ref[1])
    second_shut = (col_at == closed_ref[2]) | (col_at == closed_ref[3])
    down = lambda x: pltpu.roll(x, shape[0] - 1, 0)
    up = lambda x: pltpu.roll(x, 1, 0)
    onward = lambda x: pltpu.roll(x, shape[1] - 1, 1)
    back = lambda x: pltpu.roll(x, 1, 1)
    bed_down = down(bed)
    bed_onward = onward(bed)
    for _ in range(2):
        eta = bed + depth
        first = jnp.where(first_shut, 0.0, face_flux(eta, down(eta), bed, bed_down, first))
        second = jnp.where(second_shut, 0.0, face_flux(eta, onward(eta), bed, bed_onward, second))
        depth = depth + wet * (TIME_STEP / CELL_WIDTH) * (up(first) - first + (back(second) - second))
    here = (slice(8, 8 + row_count), slice(LANES, LANES + col_count))
    depth_ref[...] = depth[here]
    first_ref[...] = first[here]
    second_ref[...] = second[here]


def shifted(block, axis, step):
    count = lax.axis_size(axis)
    return lax.ppermute(block, axis, [(i, (i + step) % count) for i in range(count)])


def with_sides(block, axis, dim, width):
    size = block.shape[dim]
    low = shifted(lax.slice_in_dim(block, size - width, size, axis=dim), axis, 1)
    high = shifted(lax.slice_in_dim(block, 0, width, axis=dim), axis, -1)
    return jnp.concatenate([low, block, high], axis=dim)


def local(
    river_lower,
    river_main,
    river_upper,
    river_rhs,
    weir_crest,
    weir_regime,
    weir_tile,
    weir_row,
    weir_col,
    bed_level,
    water_depth,
    flux_first,
    flux_second,
    wet_mask,
):
    sections, chains = weir_crest.shape
    row_count, col_count = water_depth.shape
    row_size = lax.axis_size("row")
    col_size = lax.axis_size("col")
    row_at = lax.axis_index("row")
    col_at = lax.axis_index("col")
    tiles = row_size * col_size
    weirs = sections * chains
    capacity = 2 * weirs // tiles
    lane_rows = chains // LANES

    def block_rows(array):
        split = array.reshape(sections, 2, 2, lane_rows, LANES)
        return split.transpose(0, 1, 3, 2, 4).reshape(-1, LANES)

    rhs_rows = river_rhs.reshape(sections, 2, lane_rows, LANES).transpose(0, 2, 1, 3).reshape(-1, LANES)
    solved, packed = pl.pallas_call(
        functools.partial(solve_kernel, sections),
        out_shape=(
            jax.ShapeDtypeStruct((sections, 10, lane_rows, LANES), F32),
            jax.ShapeDtypeStruct((20, lane_rows, LANES), F32),
        ),
        in_specs=[VMEM] * 4,
        out_specs=(VMEM, VMEM),
        compiler_params=PARAMS,
        name="solve",
    )(block_rows(river_lower), block_rows(river_main), block_rows(river_upper), rhs_rows)
    slots = pl.pallas_call(
        functools.partial(rank_kernel, tiles, capacity, sections * lane_rows // 8),
        out_shape=jax.ShapeDtypeStruct((weirs // LANES, LANES), jnp.int32),
        in_specs=[VMEM],
        out_specs=VMEM,
        compiler_params=PARAMS,
        name="rank",
    )(weir_tile.reshape(weirs // LANES, LANES))
    gathered = lax.all_gather(packed.reshape(1, -1, LANES), "row", axis=0, tiled=True)
    high_count = tiles * capacity // LOW
    state_rows, outgoing = pl.pallas_call(
        functools.partial(weir_kernel, sections, row_size, tiles, capacity, row_count),
        out_shape=(
            jax.ShapeDtypeStruct((sections * lane_rows * 2, LANES), F32),
            jax.ShapeDtypeStruct((tiles, 3 * capacity // LANES, LANES), F32),
        ),
        in_specs=[SMEM] + [VMEM] * 7,
        out_specs=(VMEM, VMEM),
        scratch_shapes=[
            pltpu.VMEM((weirs // LANES, LANES), F32),
            pltpu.VMEM((6 * high_count, LOW), F32),
        ],
        compiler_params=PARAMS,
        name="weirs",
    )(row_at.reshape(1), gathered, solved, weir_crest, weir_regime, weir_row, weir_col, slots)
    river_state = (
        state_rows.reshape(sections, lane_rows, 2, LANES).transpose(0, 2, 1, 3).reshape(sections, 2, chains)
    )
    arrived = lax.all_to_all(outgoing, ("row", "col"), split_axis=0, concat_axis=0, tiled=True)
    wetted = pl.pallas_call(
        functools.partial(apply_kernel, tiles, capacity // LANES, row_count, col_count),
        out_shape=jax.ShapeDtypeStruct((row_count, col_count), F32),
        in_specs=[VMEM] * 3,
        out_specs=VMEM,
        scratch_shapes=[pltpu.VMEM((4 * row_count * col_count // LOW, LOW), F32)],
        compiler_params=PARAMS,
        name="apply",
    )(arrived, bed_level, water_depth)
    stacked = jnp.stack([wetted, bed_level, flux_first, flux_second, wet_mask.astype(F32)])
    padded = with_sides(with_sides(stacked, "row", 1, 2), "col", 2, 2)
    padded = jnp.pad(padded, ((0, 0), (6, 6), (LANES - 2, LANES - 2)))
    closed = jnp.stack(
        [
            jnp.where(row_at == 0, -1, -9),
            jnp.where(row_at == row_size - 1, row_count - 1, -9),
            jnp.where(col_at == 0, -1, -LANES - 1),
            jnp.where(col_at == col_size - 1, col_count - 1, -LANES - 1),
        ]
    ).astype(jnp.int32)
    tile_out = jax.ShapeDtypeStruct((row_count, col_count), F32)
    depth_out, first_out, second_out = pl.pallas_call(
        functools.partial(flood_kernel, row_count, col_count),
        out_shape=(tile_out, tile_out, tile_out),
        in_specs=[SMEM, VMEM],
        out_specs=(VMEM, VMEM, VMEM),
        compiler_params=PARAMS,
        name="flood",
    )(closed, padded)
    return (river_state, depth_out, first_out, second_out)


def solution(mesh):
    in_specs = (
        P("row", None, None, "col"),
        P("row", None, None, "col"),
        P("row", None, None, "col"),
        P("row", None, "col"),
        P("row", "col"),
        P("row", "col"),
        P("row", "col", None, None, None),
        P("row", "col"),
        P("row", "col"),
        P("row", "col"),
        P("row", "col"),
        P("row", "col"),
        P("row", "col"),
        P("row", "col"),
    )
    out_specs = (P("row", None, "col"), P("row", "col"), P("row", "col"), P("row", "col"))
    return jax.shard_map(local, mesh=mesh, in_specs=in_specs, out_specs=out_specs, check_vma=False)
```

profile of v0, /device:TPU:0, one launch (start us, length us, event | category | flops | bytes accessed | tf_op | source)
XLA Modules:
  0.0 67.1 jit_solution(6881417627259290052)
XLA Ops:
  0.7 0.9 %copy-done.10 = s32[1,1,16,1024,1]{3,4,2,1,0:T(1,128)S(1)} copy-done((s32[1,1,16,1024,1]{3,4,2,1,0:T(1,128)S(1)}, s32[1,1,16,1024,1]{3,4,2,1,0:T(1,128)}, u32[]{:S(2)}) %copy-start.10) | copy-done | bytes 65560
  1.5 3.1 %rank.1.slot_ref = s32[128,128]{1,0:T(8,128)S(1)} custom-call(s32[128,128]{1,0:T(8,128)S(1)} %bitcast.47), custom_call_target="tpu_custom_call" | custom-call | tf_op jit(solution)/shard_map/rank/pallas_call | solution.py:406
  4.6 0.0 copy-start
  4.7 0.9 %copy-done = f32[16,2,2,1024]{3,2,1,0:T(2,128)S(1)} copy-done((f32[16,2,2,1024]{3,2,1,0:T(2,128)S(1)}, f32[16,2,2,1024]{3,2,1,0:T(2,128)}, u32[]{:S(2)}) %copy-start) | copy-done | bytes 262168
  5.6 0.9 %copy-done.1 = f32[16,2,2,1024]{3,2,1,0:T(2,128)S(1)} copy-done((f32[16,2,2,1024]{3,2,1,0:T(2,128)S(1)}, f32[16,2,2,1024]{3,2,1,0:T(2,128)}, u32[]{:S(2)}) %copy-start.1) | copy-done | bytes 262168
  6.5 0.9 %copy-done.2 = f32[16,2,2,1024]{3,2,1,0:T(2,128)S(1)} copy-done((f32[16,2,2,1024]{3,2,1,0:T(2,128)S(1)}, f32[16,2,2,1024]{3,2,1,0:T(2,128)}, u32[]{:S(2)}) %copy-start.2) | copy-done | bytes 262168
  7.5 0.4 solve.1
  7.9 0.0 copy-start.5
  7.9 0.0 copy-start.6
  7.9 0.0 copy-start.7
  7.9 0.0 copy-start.8
  7.9 7.7 %all_gather.3.gathered_ref = f32[4,160,128]{2,1,0:T(8,128)S(1)} all-gather(f32[1,160,128]{2,1,0:T(8,128)S(1)} %bitcast.46), channel_id=1, replica_groups=mesh['row'=4,'col'=8] {'row'}, dimensions={0}, use_global_device_ids=true | all-gather | bytes 409600 | tf_op jit(solution)/shard_map/all_gather | solution.py:414
  15.6 8.4 %weirs.1 = (f32[256,128]{1,0:T(8,128)}, f32[32,24,128]{2,1,0:T(8,128)S(1)}) custom-call(s32[1]{0:T(128)} %bitcast.position_ref, f32[4,160,128]{2,1,0:T(8,128)S(1)} %all_gather.3.gathered_ref, f32[16,10,8,128]{3,2,1,0:T(8,128)S(1)} %get-tuple-element.12.solved_ref, f32[16,1024]{1,0:T(8,128)S(1)} %copy-done.5, s32[16,1024]{1,0:T(8,128)S(1)} %copy-done.6, ...), custom_call_target="tpu_custom_call" | custom-call | tf_op jit(solution)/shard_map/weirs/pallas_call | solution.py:416
  24.1 0.0 copy-start.3
  24.1 19.0 %all_to_all.5.in_ref = f32[32,24,128]{2,1,0:T(8,128)S(1)} all-to-all(f32[32,24,128]{2,1,0:T(8,128)S(1)} %get-tuple-element.14), channel_id=1, replica_groups=mesh['row'=4,'col'=8] {'row','col'}, dimensions={0} | all-to-all | bytes 786432 | tf_op jit(solution)/shard_map/all_to_all | solution.py:434
  43.1 7.8 %apply.1 = f32[32,512]{1,0:T(8,128)S(1)} custom-call(f32[32,24,128]{2,1,0:T(8,128)S(1)} %all_to_all.5.in_ref, f32[32,512]{1,0:T(8,128)S(1)} %copy-done.3, f32[32,512]{1,0:T(8,128)S(1)} %copy-done.9), custom_call_target="tpu_custom_call" | custom-call | tf_op jit(solution)/shard_map/apply/pallas_call | solution.py:435
  51.0 0.0 copy-start.11
  51.0 0.8 %copy-done.11 = f32[32,512]{1,0:T(8,128)S(1)} copy-done((f32[32,512]{1,0:T(8,128)S(1)}, f32[32,512]{1,0:T(8,128)}, u32[]{:S(2)}) %copy-start.11) | copy-done | bytes 65560
  51.8 0.8 %copy-done.12 = f32[32,512]{1,0:T(8,128)S(1)} copy-done((f32[32,512]{1,0:T(8,128)S(1)}, f32[32,512]{1,0:T(8,128)}, u32[]{:S(2)}) %copy-start.12) | copy-done | bytes 65560
  52.7 0.8 %copy-done.13 = s32[32,512]{1,0:T(8,128)S(1)} copy-done((s32[32,512]{1,0:T(8,128)S(1)}, s32[32,512]{1,0:T(8,128)}, u32[]{:S(2)}) %copy-start.13) | copy-done | bytes 65560
  53.5 0.1 collective-permute-start
  53.6 1.7 %collective-permute-start.1 = (f32[5,2,512]{2,1,0:T(2,128)S(1)}, f32[5,2,512]{2,1,0:T(2,128)S(1)}, u32[]{:S(2)}, u32[]{:S(2)}) collective-permute-start(f32[5,2,512]{2,1,0:T(2,128)S(1)} %get-tuple-element.21), channel_id=1, source_target_pairs={{0,24},{8,0},{16,8},{24,16},{1,25},{9,1},{17,9},{25,17},{2,26},{10... | collective-permute-start | bytes 61448 | tf_op jit(solution)/shard_map/ppermute | solution.py:353
  55.3 1.5 %collective-permute-done = f32[5,2,512]{2,1,0:T(2,128)S(1)} collective-permute-done((f32[5,2,512]{2,1,0:T(2,128)S(1)}, f32[5,2,512]{2,1,0:T(2,128)S(1)}, u32[]{:S(2)}, u32[]{:S(2)}) %collective-permute-start) | collective-permute-done | bytes 20512 | tf_op jit(solution)/shard_map/ppermute | solution.py:353
  56.8 0.0 collective-permute-done.1
  56.8 0.1 pad_maximum_fusion.2
  56.9 0.8 %collective-permute-start.2 = (f32[5,36,2]{2,1,0:T(8,128)S(1)}, f32[5,36,2]{2,1,0:T(8,128)S(1)}, u32[]{:S(2)}, u32[]{:S(2)}) collective-permute-start(f32[5,36,2]{2,1,0:T(8,128)S(1)} %get-tuple-element.18), channel_id=1, source_target_pairs={{0,1},{1,2},{2,3},{3,4},{4,5},{5,6},{6,7},{7,0},{8,9},{9,10},{10,1... | collective-permute-start | bytes 4328 | tf_op jit(solution)/shard_map/ppermute | solution.py:353
  57.8 3.9 %collective-permute-start.3 = (f32[5,36,2]{2,1,0:T(8,128)S(1)}, f32[5,36,2]{2,1,0:T(8,128)S(1)}, u32[]{:S(2)}, u32[]{:S(2)}) collective-permute-start(f32[5,36,2]{2,1,0:T(8,128)S(1)} %get-tuple-element.19), channel_id=1, source_target_pairs={{0,7},{1,0},{2,1},{3,2},{4,3},{5,4},{6,5},{7,6},{8,15},{9,8},{10,9... | collective-permute-start | bytes 4328 | tf_op jit(solution)/shard_map/ppermute | solution.py:353
  61.7 0.1 pad_add_fusion.closed_ref
  61.8 3.3 %collective-permute-done.2 = f32[5,36,2]{2,1,0:T(8,128)S(1)} collective-permute-done((f32[5,36,2]{2,1,0:T(8,128)S(1)}, f32[5,36,2]{2,1,0:T(8,128)S(1)}, u32[]{:S(2)}, u32[]{:S(2)}) %collective-permute-start.2) | collective-permute-done | bytes 1472 | tf_op jit(solution)/shard_map/ppermute | solution.py:353
  65.1 0.1 collective-permute-done.3
  65.2 0.1 select_maximum_fusion.in_ref
  65.4 1.7 %flood.1 = (f32[32,512]{1,0:T(8,128)}, f32[32,512]{1,0:T(8,128)}, f32[32,512]{1,0:T(8,128)}) custom-call(s32[4]{0:T(128)S(1)} %pad_add_fusion.closed_ref, f32[5,48,768]{2,1,0:T(8,128)S(1)} %select_maximum_fusion.in_ref), custom_call_target="tpu_custom_call" | custom-call | tf_op jit(solution)/shard_map/flood/pallas_call | solution.py:456
  (20 shorter events, 0.1 us)
Async XLA Ops:
  0.6 4.0 %copy-start.4 = (f32[16,2,1024]{2,1,0:T(2,128)S(1)}, f32[16,2,1024]{2,1,0:T(2,128)}, u32[]{:S(2)}) copy-start(f32[16,2,1024]{2,1,0:T(2,128)} %param.17) | copy-start | bytes 393220
  0.6 0.9 %copy-start.10 = (s32[1,1,16,1024,1]{3,4,2,1,0:T(1,128)S(1)}, s32[1,1,16,1024,1]{3,4,2,1,0:T(1,128)}, u32[]{:S(2)}) copy-start(s32[1,1,16,1024,1]{3,4,2,1,0:T(1,128)} %param.20) | copy-start | bytes 196612
  4.6 1.0 %copy-start = (f32[16,2,2,1024]{3,2,1,0:T(2,128)S(1)}, f32[16,2,2,1024]{3,2,1,0:T(2,128)}, u32[]{:S(2)}) copy-start(f32[16,2,2,1024]{3,2,1,0:T(2,128)} %param.14) | copy-start | bytes 786436
  5.6 0.9 %copy-start.1 = (f32[16,2,2,1024]{3,2,1,0:T(2,128)S(1)}, f32[16,2,2,1024]{3,2,1,0:T(2,128)}, u32[]{:S(2)}) copy-start(f32[16,2,2,1024]{3,2,1,0:T(2,128)} %param.15) | copy-start | bytes 786436
  6.5 0.9 %copy-start.2 = (f32[16,2,2,1024]{3,2,1,0:T(2,128)S(1)}, f32[16,2,2,1024]{3,2,1,0:T(2,128)}, u32[]{:S(2)}) copy-start(f32[16,2,2,1024]{3,2,1,0:T(2,128)} %param.16) | copy-start | bytes 786436
  7.9 7.8 %copy-start.5 = (f32[16,1024]{1,0:T(8,128)S(1)}, f32[16,1024]{1,0:T(8,128)}, u32[]{:S(2)}) copy-start(f32[16,1024]{1,0:T(8,128)} %crest_ref.1) | copy-start | bytes 196612
  7.9 7.8 %copy-start.6 = (s32[16,1024]{1,0:T(8,128)S(1)}, s32[16,1024]{1,0:T(8,128)}, u32[]{:S(2)}) copy-start(s32[16,1024]{1,0:T(8,128)} %regime_ref.1) | copy-start | bytes 196612
  7.9 7.7 %copy-start.7 = (s32[16,1024]{1,0:T(8,128)S(1)}, s32[16,1024]{1,0:T(8,128)}, u32[]{:S(2)}) copy-start(s32[16,1024]{1,0:T(8,128)} %row_ref.1) | copy-start | bytes 196612
  7.9 7.7 %copy-start.8 = (s32[16,1024]{1,0:T(8,128)S(1)}, s32[16,1024]{1,0:T(8,128)}, u32[]{:S(2)}) copy-start(s32[16,1024]{1,0:T(8,128)} %col_ref.1) | copy-start | bytes 196612
  24.1 19.1 %copy-start.3 = (f32[32,512]{1,0:T(8,128)S(1)}, f32[32,512]{1,0:T(8,128)}, u32[]{:S(2)}) copy-start(f32[32,512]{1,0:T(8,128)} %bed_ref.1) | copy-start | bytes 196612
  24.1 19.1 %copy-start.9 = (f32[32,512]{1,0:T(8,128)S(1)}, f32[32,512]{1,0:T(8,128)}, u32[]{:S(2)}) copy-start(f32[32,512]{1,0:T(8,128)} %depth_ref.1) | copy-start | bytes 196612
  51.0 0.8 %copy-start.11 = (f32[32,512]{1,0:T(8,128)S(1)}, f32[32,512]{1,0:T(8,128)}, u32[]{:S(2)}) copy-start(f32[32,512]{1,0:T(8,128)} %param.25) | copy-start | bytes 196612
  51.8 0.8 %copy-start.12 = (f32[32,512]{1,0:T(8,128)S(1)}, f32[32,512]{1,0:T(8,128)}, u32[]{:S(2)}) copy-start(f32[32,512]{1,0:T(8,128)} %param.26) | copy-start | bytes 196612
  52.7 0.8 %copy-start.13 = (s32[32,512]{1,0:T(8,128)S(1)}, s32[32,512]{1,0:T(8,128)}, u32[]{:S(2)}) copy-start(s32[32,512]{1,0:T(8,128)} %param.27) | copy-start | bytes 196612
  53.5 3.3 %collective-permute-start = (f32[5,2,512]{2,1,0:T(2,128)S(1)}, f32[5,2,512]{2,1,0:T(2,128)S(1)}, u32[]{:S(2)}, u32[]{:S(2)}) collective-permute-start(f32[5,2,512]{2,1,0:T(2,128)S(1)} %get-tuple-element.20), channel_id=1, source_target_pairs={{0,8},{8,16},{16,24},{24,0},{1,9},{9,17},{17,25},{25,1},{2,10},{10... | collective-permute-start | bytes 61448 | tf_op jit(solution)/shard_map/ppermute | solution.py:353
  53.6 3.2 %collective-permute-start.1 = (f32[5,2,512]{2,1,0:T(2,128)S(1)}, f32[5,2,512]{2,1,0:T(2,128)S(1)}, u32[]{:S(2)}, u32[]{:S(2)}) collective-permute-start(f32[5,2,512]{2,1,0:T(2,128)S(1)} %get-tuple-element.21), channel_id=1, source_target_pairs={{0,24},{8,0},{16,8},{24,16},{1,25},{9,1},{17,9},{25,17},{2,26},{10... | collective-permute-start | bytes 61448 | tf_op jit(solution)/shard_map/ppermute | solution.py:353
  56.9 8.2 %collective-permute-start.2 = (f32[5,36,2]{2,1,0:T(8,128)S(1)}, f32[5,36,2]{2,1,0:T(8,128)S(1)}, u32[]{:S(2)}, u32[]{:S(2)}) collective-permute-start(f32[5,36,2]{2,1,0:T(8,128)S(1)} %get-tuple-element.18), channel_id=1, source_target_pairs={{0,1},{1,2},{2,3},{3,4},{4,5},{5,6},{6,7},{7,0},{8,9},{9,10},{10,1... | collective-permute-start | bytes 4328 | tf_op jit(solution)/shard_map/ppermute | solution.py:353
  57.8 7.5 %collective-permute-start.3 = (f32[5,36,2]{2,1,0:T(8,128)S(1)}, f32[5,36,2]{2,1,0:T(8,128)S(1)}, u32[]{:S(2)}, u32[]{:S(2)}) collective-permute-start(f32[5,36,2]{2,1,0:T(8,128)S(1)} %get-tuple-element.19), channel_id=1, source_target_pairs={{0,7},{1,0},{2,1},{3,2},{4,3},{5,4},{6,5},{7,6},{8,15},{9,8},{10,9... | collective-permute-start | bytes 4328 | tf_op jit(solution)/shard_map/ppermute | solution.py:353
where the time goes:
time: 67.6 us; the launch traced here: 67.1 us
  blocking collectives  26.8 us (40%)
  Pallas kernels  21.5 us (32%)
  starting transfers between devices  6.57 us (10%)
  local copies, waits for them, and re-layouts  6.27 us (9%)
  waiting for transfers between devices  4.92 us (7%)
  between operations  0.82 us (1%)
    all_to_all x1, blocking collectives, local(): lax.all_to_all(outgoing, ('row', 'col'), split_axis=0, concat_axis=0, til...  19 us
    pallas_call x1, Pallas kernels, local(): pl.pallas_call(functools.partial(weir_kernel, sections, row_size, tiles,...  8.42 us
    pallas_call x1, Pallas kernels, local(): pl.pallas_call(functools.partial(apply_kernel, tiles, capacity // LANES,...  7.83 us
    all_gather x1, blocking collectives, local(): lax.all_gather(packed.reshape(1, -1, LANES), 'row', axis=0, tiled=True)  7.71 us
    ppermute x4, starting transfers between devices, shifted(): lax.ppermute(block, axis, [(i, (i + step) % count) for i in range(count)])  6.57 us
    unnamed x32, local copies, waits for them, and re-layouts  6.26 us
    ppermute x4, waiting for transfers between devices, shifted(): lax.ppermute(block, axis, [(i, (i + step) % count) for i in range(count)])  4.92 us
    pallas_call x1, Pallas kernels, local(): pl.pallas_call(functools.partial(rank_kernel, tiles, capacity, sections *...  3.1 us
  transfers between devices with their start and end apart: 4, of which 3 were waited for; matrix products, arithmetic and copies ran while one was open for 0% of the time, Pallas kernels for 0%

commit v1 on v0

v1 whole, which is shorter than its diff:
```python
import functools

import jax
import jax.numpy as jnp
from jax import lax
from jax.experimental import pallas as pl
from jax.experimental.pallas import tpu as pltpu
from jax.sharding import PartitionSpec as P

GRAVITY = 9.81
TIME_STEP = 1.0
CELL_WIDTH = 10.0
MANNING_SQ = 0.0009
DEPTH_FLOOR = 0.05
WEIR_GAIN = 0.5
FREE_COEF = 0.5
SUB_COEF = 0.4
SUB_OFFSET = 0.25
GATE_COEF = 0.2

F32 = jnp.float32
BF16 = jnp.bfloat16
LANES = 128
LOW = 256
VMEM = pl.BlockSpec(memory_space=pltpu.VMEM)
SMEM = pl.BlockSpec(memory_space=pltpu.SMEM)
ANY = pl.BlockSpec(memory_space=pl.ANY)
PARAMS = pltpu.CompilerParams(vmem_limit_bytes=40 * 2**20)
WIDE = pltpu.CompilerParams(vmem_limit_bytes=60 * 2**20)


def start_copies(sources, targets, sems):
    copies = [pltpu.make_async_copy(s, t, sems.at[n]) for n, (s, t) in enumerate(zip(sources, targets))]
    for copy in copies:
        copy.start()
    return copies


def mat_mat(a, b):
    return [[a[i][0] * b[0][j] + a[i][1] * b[1][j] for j in range(2)] for i in range(2)]


def mat_vec(a, v):
    return [a[i][0] * v[0] + a[i][1] * v[1] for i in range(2)]


def mat_sub(a, b):
    return [[a[i][j] - b[i][j] for j in range(2)] for i in range(2)]


def mat_neg(a):
    return [[-a[i][j] for j in range(2)] for i in range(2)]


def mat_inv(m):
    scale = 1.0 / (m[0][0] * m[1][1] - m[0][1] * m[1][0])
    return [[m[1][1] * scale, -m[0][1] * scale], [-m[1][0] * scale, m[0][0] * scale]]


def solve_kernel(sections, *refs):
    solved_ref, packed_ref = refs[4:6]
    lower_ref, main_ref, upper_ref, rhs_ref = refs[6:10]
    for copy in start_copies(refs[:4], refs[6:10], refs[10]):
        copy.wait()

    def block(ref, k):
        return [[ref[pl.ds(k * 32 + i * 16 + j, 8, stride=2), :] for j in range(2)] for i in range(2)]

    couples = []
    for k in range(sections):
        lower = block(lower_ref, k)
        main = block(main_ref, k)
        upper = block(upper_ref, k)
        right = [rhs_ref[pl.ds(k * 16 + j, 8, stride=2), :] for j in range(2)]
        if k == 0:
            inverse = mat_inv(main)
            left = mat_neg(mat_mat(inverse, lower))
            value = mat_vec(inverse, right)
        else:
            inverse = mat_inv(mat_sub(main, mat_mat(lower, couples[-1])))
            left = mat_neg(mat_mat(inverse, mat_mat(lower, left)))
            moved = mat_vec(lower, value)
            value = mat_vec(inverse, [right[i] - moved[i] for i in range(2)])
        couples.append(mat_mat(inverse, upper))
        for i in range(2):
            solved_ref[k, i] = value[i]
            for j in range(2):
                solved_ref[k, 2 + 2 * i + j] = left[i][j]
    spike = mat_neg(couples[-1])
    tail = (value, left, spike)
    for i in range(2):
        for j in range(2):
            solved_ref[sections - 1, 6 + 2 * i + j] = spike[i][j]
    for k in range(sections - 2, -1, -1):
        couple = couples[k]
        after = mat_vec(couple, value)
        value = [solved_ref[k, i] - after[i] for i in range(2)]
        after = mat_mat(couple, left)
        left = [[solved_ref[k, 2 + 2 * i + j] - after[i][j] for j in range(2)] for i in range(2)]
        spike = mat_neg(mat_mat(couple, spike))
        for i in range(2):
            solved_ref[k, i] = value[i]
            for j in range(2):
                solved_ref[k, 2 + 2 * i + j] = left[i][j]
                solved_ref[k, 6 + 2 * i + j] = spike[i][j]
    for i in range(2):
        packed_ref[i] = value[i]
        packed_ref[2 + i] = tail[0][i]
        for j in range(2):
            packed_ref[4 + 2 * i + j] = left[i][j]
            packed_ref[8 + 2 * i + j] = tail[1][i][j]
            packed_ref[12 + 2 * i + j] = spike[i][j]
            packed_ref[16 + 2 * i + j] = tail[2][i][j]


def load_pair(ref, n):
    return [ref[n], ref[n + 1]]


def load_square(ref, n):
    return [load_pair(ref, n), load_pair(ref, n + 2)]


def store_all(ref, values):
    flat = []
    for value in values:
        flat += [*value[0], *value[1]] if isinstance(value[0], list) else value
    for n, item in enumerate(flat):
        ref[n] = item


def pick(flag, one, other):
    if isinstance(one, list):
        return [pick(flag, a, b) for a, b in zip(one, other)]
    return jnp.where(flag, one, other)


def add(a, b):
    if isinstance(a, list):
        return [add(x, y) for x, y in zip(a, b)]
    return a + b


def meet(head_y, head_left, tail_y, tail_right):
    inner = mat_mat(head_left, tail_right)
    inverse = mat_inv([[1.0 - inner[0][0], -inner[0][1]], [-inner[1][0], 1.0 - inner[1][1]]])
    return inverse, mat_vec(inverse, add(head_y, mat_vec(head_left, tail_y)))


def merge_kernel(step, first, position_ref, own_ref, other_ref, *refs):
    known_ref = None if first else refs[0]
    group_ref, map_ref, send_ref = refs[-3:]
    position = position_ref[0]
    late = ((position >> step) & 1) == 1

    def group(ref):
        return [load_pair(ref, 0), load_pair(ref, 2)] + [load_square(ref, n) for n in (4, 8, 12, 16)]

    own, other = group(own_ref), group(other_ref)
    head_y, tail_y, head_left, tail_left, head_right, tail_right = pick(late, other, own)
    next_head_y, next_tail_y, next_head_left, next_tail_left, next_head_right, next_tail_right = pick(
        late, own, other
    )
    inverse, head = meet(next_head_y, next_head_left, tail_y, tail_right)
    head_before = mat_mat(inverse, mat_mat(next_head_left, tail_left))
    head_after = mat_mat(inverse, next_head_right)
    tail = add(tail_y, mat_vec(tail_right, head))
    tail_before = add(tail_left, mat_mat(tail_right, head_before))
    tail_after = mat_mat(tail_right, head_after)
    joined = [
        add(head_y, mat_vec(head_right, head)),
        add(next_tail_y, mat_vec(next_tail_left, tail)),
        add(head_left, mat_mat(head_right, head_before)),
        mat_mat(next_tail_left, tail_before),
        mat_mat(head_right, head_after),
        add(next_tail_right, mat_mat(next_tail_left, tail_after)),
    ]
    zero = jnp.zeros(tail[0].shape, F32)
    one = zero + 1.0
    unit, none, nothing = [[one, zero], [zero, one]], [[zero, zero], [zero, zero]], [zero, zero]
    if first:
        maps = [
            [pick(late, tail_before, unit), pick(late, tail_after, none), pick(late, tail, nothing)],
            [pick(late, none, head_before), pick(late, unit, head_after), pick(late, nothing, head)],
        ]
    else:
        maps = []
        for n in range(2):
            by_before = load_square(known_ref, 10 * n)
            by_after = load_square(known_ref, 10 * n + 4)
            value = load_pair(known_ref, 10 * n + 8)
            maps.append(
                [
                    pick(late, mat_mat(by_before, tail_before), add(by_before, mat_mat(by_after, head_before))),
                    pick(late, add(by_after, mat_mat(by_before, tail_after)), mat_mat(by_after, head_after)),
                    pick(late, add(value, mat_vec(by_before, tail)), add(value, mat_vec(by_after, head))),
                ]
            )
    store_all(group_ref, joined)
    store_all(map_ref, maps[0] + maps[1])
    later = ((position >> (step + 1)) & 1) == 1
    store_all(send_ref, [pick(later, joined[0], joined[1]), pick(later, joined[2], joined[5])])


def rows16(row):
    return jnp.broadcast_to(row, (16, LANES)).astype(BF16)


def table16(count):
    shape = (count // 16, 16, LANES)
    at = lax.broadcasted_iota(jnp.int32, shape, 0) * 16 + lax.broadcasted_iota(jnp.int32, shape, 1)
    return at.astype(F32).astype(BF16)


def halves(value):
    high = value.astype(BF16).astype(F32)
    return high, value - high


def one_hots(high, low, values, high_table, low_table):
    one = jnp.ones((), BF16)
    zero = jnp.zeros((), BF16)
    left, right = [], []
    for r in range(8):
        hit = high_table == rows16(high[r : r + 1])[None]
        left.append(
            jnp.concatenate(
                [jnp.where(hit, rows16(v[r : r + 1])[None], zero).reshape(-1, LANES) for v in values], 0
            )
        )
        hit = low_table == rows16(low[r : r + 1])[None]
        right.append(jnp.where(hit, one, zero).reshape(-1, LANES))
    return jnp.concatenate(left, 1), jnp.concatenate(right, 1)


def product(left, right):
    return lax.dot_general(left, right, (((1,), (1,)), ((), ())), preferred_element_type=F32)


def group_at(g):
    over = pl.multiple_of((g // 8) * 8, 8)
    along = pl.multiple_of((g % 8) * LANES, LANES)
    return (pl.ds(over, 8), pl.ds(along, LANES))


def fill_slots(high_count, groups, slot_ref, values, total_ref):
    high_table = table16(high_count)
    low_table = table16(LOW)
    total_ref[...] = jnp.zeros_like(total_ref)

    def body(g, carry):
        slot = slot_ref[pl.ds(pl.multiple_of(g * 8, 8), 8), :]
        left, right = one_hots(
            (slot // LOW).astype(F32), (slot % LOW).astype(F32), values(g), high_table, low_table
        )
        total_ref[...] += product(left, right)
        return carry

    lax.fori_loop(0, groups, body, 0, unroll=8)


def store_slots(tiles, capacity, total_ref, part, scale, out_ref, row):
    high_count = tiles * capacity // LOW
    per_tile = capacity // LOW
    first = total_ref[pl.ds(part * high_count, high_count), :]
    value = first * scale + total_ref[pl.ds((part + 1) * high_count, high_count), :]
    for t in range(tiles):
        for j in range(LOW // LANES):
            out_ref[t, pl.ds(row + j * per_tile, per_tile), :] = value[
                t * per_tile : (t + 1) * per_tile, j * LANES : (j + 1) * LANES
            ]


def rank_kernel(tiles, capacity, groups, tile_in, slot_ref, tile_ref, sems):
    start_copies((tile_in,), (tile_ref,), sems)[0].wait()
    table = lax.broadcasted_iota(jnp.int32, (tiles, LANES), 0)
    row_at = lax.broadcasted_iota(jnp.int32, (LANES, 2 * LANES), 0)
    col_at = lax.broadcasted_iota(jnp.int32, (LANES, 2 * LANES), 1)
    earlier = jnp.where(row_at < col_at, 1.0, 0.0).astype(BF16)

    def body(g, offset):
        ids = tile_ref[pl.ds((g // 8) * 64 + g % 8, 8, stride=8), :]
        hits = [ids[r : r + 1, :] == table for r in range(8)]
        hot = jnp.concatenate([jnp.where(h, 1.0, 0.0).astype(BF16) for h in hits], 0)
        counts = jnp.dot(hot, earlier, preferred_element_type=F32)
        rows = []
        for r in range(8):
            part = counts[r * tiles : (r + 1) * tiles]
            place = jnp.where(hits[r], part[:, :LANES] + offset, 0.0)
            rows.append(jnp.sum(place, axis=0, keepdims=True))
            offset = offset + part[:, LANES:]
        slot_ref[pl.ds(g * 8, 8), :] = jnp.concatenate(rows, 0).astype(jnp.int32)
        return offset

    lax.fori_loop(0, groups, body, table.astype(F32) * capacity, unroll=4)


def cell_kernel(tiles, capacity, groups, row_count, slot_ref, row_in, col_in, after, cells_ref, *refs):
    row_ref, col_ref, total_ref, sems = refs
    for copy in start_copies((row_in, col_in), (row_ref, col_ref), sems):
        copy.wait()

    def values(g):
        col = col_ref[group_at(g)]
        high = (col // LOW) * row_count + row_ref[group_at(g)]
        return [high.astype(F32), (col % LOW).astype(F32)]

    fill_slots(tiles * capacity // LOW, groups, slot_ref, values, total_ref)
    store_slots(tiles, capacity, total_ref, 0, float(LOW), cells_ref, 0)


def weir_kernel(sections, steps, tiles, capacity, *refs):
    position_ref, own_ref, other_ref, map_ref = refs[:4]
    solved_ref, slot_ref, cells_ref, crest_in, regime_in = refs[4:9]
    state_out, out_ref = refs[9:11]
    crest_ref, regime_ref, state_ref, phase_ref, total_ref, sems = refs[11:]
    copies = start_copies((crest_in, regime_in), (crest_ref, regime_ref), sems)
    late = ((position_ref[0] >> (steps - 1)) & 1) == 1
    own = [load_pair(own_ref, 0), load_square(own_ref, 2)]
    other = [load_pair(other_ref, 0), load_square(other_ref, 2)]
    tail_y, tail_right = pick(late, other, own)
    head_y, head_left = pick(late, own, other)
    head = meet(head_y, head_left, tail_y, tail_right)[1]
    tail = add(tail_y, mat_vec(tail_right, head))
    zero = jnp.zeros(tail[0].shape, F32)
    outer_before = pick(late, tail, [zero, zero])
    outer_after = pick(late, [zero, zero], head)
    before, after = (
        add(
            load_pair(map_ref, n + 8),
            add(
                mat_vec(load_square(map_ref, n), outer_before),
                mat_vec(load_square(map_ref, n + 4), outer_after),
            ),
        )
        for n in (0, 10)
    )
    for k in range(sections):
        for i in range(2):
            state = solved_ref[k, i]
            for j in range(2):
                state = state + solved_ref[k, 2 + 2 * i + j] * before[j]
                state = state + solved_ref[k, 6 + 2 * i + j] * after[j]
            state_ref[pl.ds(k * 16 + i, 8, stride=2), :] = state
            if i == 0:
                phase_ref[pl.ds((k // 8) * 64 + k % 8, 8, stride=8), :] = state

    state_copy = pltpu.make_async_copy(state_ref, state_out, sems.at[2])
    state_copy.start()
    for copy in copies:
        copy.wait()

    def values(g):
        phase = phase_ref[pl.ds(pl.multiple_of(g * 8, 8), 8), :]
        regime = regime_ref[group_at(g)]
        head = jnp.maximum(phase - crest_ref[group_at(g)], 0.0)
        free = jnp.where(regime == 0, FREE_COEF * head * jnp.sqrt(head), 0.0)
        sub = jnp.where(
            regime == 1,
            SUB_COEF * jnp.sqrt(head + SUB_OFFSET),
            jnp.where(regime == 2, GATE_COEF, 0.0),
        )
        return [*halves(WEIR_GAIN * (free + sub * phase)), *halves(WEIR_GAIN * sub)]

    fill_slots(tiles * capacity // LOW, sections, slot_ref, values, total_ref)
    rows_each = capacity // LANES
    for v in range(2):
        store_slots(tiles, capacity, total_ref, 2 * v, 1.0, out_ref, v * rows_each)
    out_ref[:, pl.ds(2 * rows_each, rows_each), :] = cells_ref[...]
    state_copy.wait()


def apply_kernel(sources, rows_each, row_count, col_count, *refs):
    in_ref, bed_in, depth_in, first_in, second_in, wet_in = refs[:6]
    tile_ref, top_ref, bottom_ref = refs[6:9]
    depth_ref, wet_ref, total_ref, sems = refs[9:]
    copies = start_copies(
        (bed_in, depth_in, first_in, second_in, wet_in),
        (tile_ref.at[1], depth_ref, tile_ref.at[2], tile_ref.at[3], wet_ref),
        sems,
    )
    high_count = row_count * col_count // LOW
    high_table = table16(high_count)
    low_table = table16(LOW)
    total_ref[...] = jnp.zeros_like(total_ref)
    step = 8 // rows_each if rows_each < 8 else 1

    def body(g, carry):
        def part(v):
            return jnp.concatenate(
                [in_ref[g * step + n, pl.ds(v * rows_each, rows_each), :] for n in range(step)], 0
            )

        cell = part(2).astype(jnp.int32)
        left, right = one_hots(
            (cell // LOW).astype(F32),
            (cell % LOW).astype(F32),
            [*halves(part(0)), *halves(part(1))],
            high_table,
            low_table,
        )
        total_ref[...] += product(left, right)
        return carry

    lax.fori_loop(0, sources // step, body, 0, unroll=8)
    for copy in copies:
        copy.wait()
    tile_ref[4] = wet_ref[...].astype(F32) * (TIME_STEP / CELL_WIDTH)
    for n in range(col_count // LOW):
        def summed(v):
            start = 2 * v * high_count + n * row_count
            return total_ref[pl.ds(start, row_count), :] + total_ref[pl.ds(start + high_count, row_count), :]

        cols = pl.ds(n * LOW, LOW)
        depth = depth_ref[:, cols]
        surface = tile_ref[1, :, cols] + depth
        tile_ref[0, :, cols] = jnp.maximum(depth + (summed(0) - summed(1) * surface), 0.0)
    for out, near, rows in ((top_ref, 0, (0, 1)), (bottom_ref, row_count - 1, (row_count - 2, row_count - 1))):
        for n in range(3):
            for i in range(2):
                out[pl.ds(2 * n + i, 1), :] = tile_ref[n, pl.ds(rows[i], 1), :]
        for n in (3, 4):
            out[pl.ds(3 + n, 1), :] = tile_ref[n, pl.ds(near, 1), :]


def face_flux(eta_here, eta_next, bed_here, bed_next, old_flux):
    flow_depth = jnp.maximum(
        jnp.maximum(eta_here, eta_next) - jnp.maximum(bed_here, bed_next), DEPTH_FLOOR
    )
    gradient = (eta_next - eta_here) / CELL_WIDTH
    pushed = old_flux - GRAVITY * TIME_STEP * flow_depth * gradient
    friction = jnp.exp((-7.0 / 3.0) * jnp.log(flow_depth))
    return pushed / (1.0 + GRAVITY * TIME_STEP * MANNING_SQ * jnp.abs(old_flux) * friction)


def pad_rows(n, tile_ref, above_ref, below_ref, cols):
    at = lax.broadcasted_iota(jnp.int32, (8, 1), 0)
    row = 2 * n if n < 3 else 3 + n
    low = above_ref[pl.ds(row, 1), cols]
    high = below_ref[pl.ds(row, 1), cols]
    if n < 3:
        low_last = above_ref[pl.ds(row + 1, 1), cols]
        high_last = below_ref[pl.ds(row + 1, 1), cols]
    else:
        low_last, high_last = low, high
    low = jnp.where(at == 6, low, jnp.where(at == 7, low_last, 0.0))
    high = jnp.where(at == 0, high, jnp.where(at == 1, high_last, 0.0))
    return jnp.concatenate([low, tile_ref[n, :, cols], high], 0)


def side_lanes(n):
    at = lax.broadcasted_iota(jnp.int32, (8, LANES), 1)
    return (at == 2 * n) | (at == 2 * n + 1)


def sides_kernel(col_count, tile_ref, above_ref, below_ref, left_ref, right_ref):
    left = jnp.zeros(left_ref.shape, F32)
    right = left
    for n in range(5):
        first = pad_rows(n, tile_ref, above_ref, below_ref, pl.ds(0, LANES))
        last = pad_rows(n, tile_ref, above_ref, below_ref, pl.ds(col_count - LANES, LANES))
        for t in range(first.shape[0] // 8):
            at = 5 * t + n
            rows = slice(8 * t, 8 * t + 8)
            left = jnp.where(side_lanes(at), pltpu.roll(first[rows], 2 * at, 1), left)
            right = jnp.where(side_lanes(at), pltpu.roll(last[rows], 2 * at + 2, 1), right)
    left_ref[...] = left
    right_ref[...] = right


def flood_kernel(row_count, col_count, closed_ref, tile_ref, above_ref, below_ref, before_ref, after_ref, *outs):
    arrays = []
    for n in range(5):
        at = [5 * t + n for t in range(row_count // 8 + 2)]
        before = jnp.concatenate([pltpu.roll(before_ref[...], LANES - 2 - 2 * m, 1) for m in at], 0)
        after = jnp.concatenate([pltpu.roll(after_ref[...], (LANES - 2 * m) % LANES, 1) for m in at], 0)
        inner = pad_rows(n, tile_ref, above_ref, below_ref, slice(None))
        arrays.append(jnp.concatenate([before, inner, after], 1))
    depth, bed, first, second, wet = arrays
    shape = depth.shape
    row_at = lax.broadcasted_iota(jnp.int32, shape, 0) - 8
    col_at = lax.broadcasted_iota(jnp.int32, shape, 1) - LANES
    first_shut = (row_at == closed_ref[0]) | (row_at == closed_ref[1])
    second_shut = (col_at == closed_ref[2]) | (col_at == closed_ref[3])
    down = lambda x: pltpu.roll(x, shape[0] - 1, 0)
    up = lambda x: pltpu.roll(x, 1, 0)
    onward = lambda x: pltpu.roll(x, shape[1] - 1, 1)
    back = lambda x: pltpu.roll(x, 1, 1)
    bed_down = down(bed)
    bed_onward = onward(bed)
    for _ in range(2):
        eta = bed + depth
        first = jnp.where(first_shut, 0.0, face_flux(eta, down(eta), bed, bed_down, first))
        second = jnp.where(second_shut, 0.0, face_flux(eta, onward(eta), bed, bed_onward, second))
        depth = depth + wet * (up(first) - first + (back(second) - second))
    here = (slice(8, 8 + row_count), slice(LANES, LANES + col_count))
    for out, value in zip(outs, (depth, first, second)):
        out[...] = value[here]


def shifted(block, axis, step):
    count = lax.axis_size(axis)
    return lax.ppermute(block, axis, [(i, (i + step) % count) for i in range(count)])


def exchanged(block, axis, step):
    return lax.ppermute(block, axis, [(i, i ^ (1 << step)) for i in range(lax.axis_size(axis))])


def swapped(left, right, position, count):
    odd = position % 2 == 1
    inner = [(i, i ^ 1) for i in range(count)]
    outer = [(0, 0), (count - 1, count - 1)]
    for i in range(1, count - 1, 2):
        outer += [(i, i + 1), (i + 1, i)]
    one = lax.ppermute(jnp.where(odd, left, right), "col", inner)
    two = lax.ppermute(jnp.where(odd, right, left), "col", outer)
    return jnp.where(odd, one, two), jnp.where(odd, two, one)


def local(
    river_lower,
    river_main,
    river_upper,
    river_rhs,
    weir_crest,
    weir_regime,
    weir_tile,
    weir_row,
    weir_col,
    bed_level,
    water_depth,
    flux_first,
    flux_second,
    wet_mask,
):
    sections, chains = weir_crest.shape
    row_count, col_count = water_depth.shape
    row_size = lax.axis_size("row")
    col_size = lax.axis_size("col")
    row_at = lax.axis_index("row")
    col_at = lax.axis_index("col")
    tiles = row_size * col_size
    weirs = sections * chains
    capacity = 2 * weirs // tiles
    lane_rows = chains // LANES

    def block_rows(array):
        split = array.reshape(sections, 2, 2, lane_rows, LANES)
        return split.transpose(0, 1, 3, 2, 4).reshape(-1, LANES)

    rhs_rows = river_rhs.reshape(sections, 2, lane_rows, LANES).transpose(0, 2, 1, 3).reshape(-1, LANES)
    rows = weirs // LANES
    high_count = tiles * capacity // LOW
    rows_each = capacity // LANES
    river_block = pltpu.VMEM((sections * 4 * lane_rows, LANES), F32)
    solved, packed = pl.pallas_call(
        functools.partial(solve_kernel, sections),
        out_shape=(
            jax.ShapeDtypeStruct((sections, 10, lane_rows, LANES), F32),
            jax.ShapeDtypeStruct((20, lane_rows, LANES), F32),
        ),
        in_specs=[ANY] * 4,
        out_specs=(VMEM, VMEM),
        scratch_shapes=[
            river_block,
            river_block,
            river_block,
            pltpu.VMEM((sections * 2 * lane_rows, LANES), F32),
            pltpu.SemaphoreType.DMA((4,)),
        ],
        compiler_params=WIDE,
        name="solve",
    )(block_rows(river_lower), block_rows(river_main), block_rows(river_upper), rhs_rows)
    steps = row_size.bit_length() - 1
    slots = pl.pallas_call(
        functools.partial(rank_kernel, tiles, capacity, sections * lane_rows // 8),
        out_shape=jax.ShapeDtypeStruct((rows, LANES), jnp.int32),
        in_specs=[ANY],
        out_specs=VMEM,
        scratch_shapes=[pltpu.VMEM((rows, LANES), jnp.int32), pltpu.SemaphoreType.DMA((1,))],
        compiler_params=PARAMS,
        cost_estimate=pl.CostEstimate(flops=2 * tiles * weirs * LOW, bytes_accessed=2**17, transcendentals=0),
        name="rank",
    )(weir_tile.reshape(rows, LANES))
    group, known = packed, ()
    for step in range(steps - 1):
        other = exchanged(group, "row", step)
        twenty = jax.ShapeDtypeStruct((20, lane_rows, LANES), F32)
        group, own_map, sent = pl.pallas_call(
            functools.partial(merge_kernel, step, step == 0),
            out_shape=(twenty, twenty, jax.ShapeDtypeStruct((6, lane_rows, LANES), F32)),
            in_specs=[SMEM] + [VMEM] * (2 + len(known)),
            out_specs=(VMEM, VMEM, VMEM),
            compiler_params=PARAMS,
            name="merge",
        )(row_at.reshape(1), group, other, *known)
        known = (own_map,)
    met = exchanged(sent, "row", steps - 1)
    cells = pl.pallas_call(
        functools.partial(cell_kernel, tiles, capacity, sections * lane_rows // 8, row_count),
        out_shape=jax.ShapeDtypeStruct((tiles, rows_each, LANES), F32),
        in_specs=[VMEM] + [ANY] * 3,
        out_specs=VMEM,
        scratch_shapes=[
            pltpu.VMEM((sections, chains), jnp.int32),
            pltpu.VMEM((sections, chains), jnp.int32),
            pltpu.VMEM((2 * high_count, LOW), F32),
            pltpu.SemaphoreType.DMA((2,)),
        ],
        compiler_params=PARAMS,
        cost_estimate=pl.CostEstimate(flops=4 * high_count * LOW * weirs, bytes_accessed=2**18, transcendentals=0),
        name="cells",
    )(slots, weir_row, weir_col, sent)
    state_shape = jax.ShapeDtypeStruct((sections * lane_rows * 2, LANES), F32)
    state_rows, outgoing = pl.pallas_call(
        functools.partial(weir_kernel, sections, steps, tiles, capacity),
        out_shape=(state_shape, jax.ShapeDtypeStruct((tiles, 3 * rows_each, LANES), F32)),
        in_specs=[SMEM] + [VMEM] * 6 + [ANY] * 2,
        out_specs=(ANY, VMEM),
        scratch_shapes=[
            pltpu.VMEM((sections, chains), F32),
            pltpu.VMEM((sections, chains), jnp.int32),
            pltpu.VMEM(state_shape.shape, F32),
            pltpu.VMEM((rows, LANES), F32),
            pltpu.VMEM((4 * high_count, LOW), F32),
            pltpu.SemaphoreType.DMA((3,)),
        ],
        compiler_params=PARAMS,
        name="weirs",
    )(row_at.reshape(1), sent, met, own_map, solved, slots, cells, weir_crest, weir_regime)
    river_state = (
        state_rows.reshape(sections, lane_rows, 2, LANES).transpose(0, 2, 1, 3).reshape(sections, 2, chains)
    )
    arrived = lax.all_to_all(outgoing, ("row", "col"), split_axis=0, concat_axis=0, tiled=True)
    strip = jax.ShapeDtypeStruct((8, col_count), F32)
    tile, top, bottom = pl.pallas_call(
        functools.partial(apply_kernel, tiles, rows_each, row_count, col_count),
        out_shape=(jax.ShapeDtypeStruct((5, row_count, col_count), F32), strip, strip),
        in_specs=[VMEM] + [ANY] * 5,
        out_specs=(VMEM, VMEM, VMEM),
        scratch_shapes=[
            pltpu.VMEM((row_count, col_count), F32),
            pltpu.VMEM((row_count, col_count), jnp.int32),
            pltpu.VMEM((4 * row_count * col_count // LOW, LOW), F32),
            pltpu.SemaphoreType.DMA((5,)),
        ],
        compiler_params=PARAMS,
        name="apply",
    )(arrived, bed_level, water_depth, flux_first, flux_second, wet_mask)
    above = shifted(bottom, "row", 1)
    below = shifted(top, "row", -1)
    side = jax.ShapeDtypeStruct((8, LANES), F32)
    left, right = pl.pallas_call(
        functools.partial(sides_kernel, col_count),
        out_shape=(side, side),
        in_specs=[VMEM] * 3,
        out_specs=(VMEM, VMEM),
        compiler_params=PARAMS,
        name="sides",
    )(tile, above, below)
    before, after = swapped(left, right, col_at, col_size)
    closed = jnp.stack(
        [
            jnp.where(row_at == 0, -1, -9),
            jnp.where(row_at == row_size - 1, row_count - 1, -9),
            jnp.where(col_at == 0, -1, -LANES - 1),
            jnp.where(col_at == col_size - 1, col_count - 1, -LANES - 1),
        ]
    ).astype(jnp.int32)
    tile_out = jax.ShapeDtypeStruct((row_count, col_count), F32)
    depth_out, first_out, second_out = pl.pallas_call(
        functools.partial(flood_kernel, row_count, col_count),
        out_shape=(tile_out, tile_out, tile_out),
        in_specs=[SMEM] + [VMEM] * 5,
        out_specs=(VMEM, VMEM, VMEM),
        compiler_params=PARAMS,
        name="flood",
    )(closed, tile, above, below, before, after)
    return (river_state, depth_out, first_out, second_out)


def solution(mesh):
    in_specs = (
        P("row", None, None, "col"),
        P("row", None, None, "col"),
        P("row", None, None, "col"),
        P("row", None, "col"),
        P("row", "col"),
        P("row", "col"),
        P("row", "col", None, None, None),
        P("row", "col"),
        P("row", "col"),
        P("row", "col"),
        P("row", "col"),
        P("row", "col"),
        P("row", "col"),
        P("row", "col"),
    )
    out_specs = (P("row", None, "col"), P("row", "col"), P("row", "col"), P("row", "col"))
    return jax.shard_map(local, mesh=mesh, in_specs=in_specs, out_specs=out_specs, check_vma=False)
```

time: 67.6 us -> 51.6 us (0.76)
  the two profiles are of different devices: /device:TPU:0 before, /device:TPU:2 now
where the time goes in v1:
time: 51.6 us; the launch traced here: 51.4 us
  Pallas kernels  20 us (39%)
  blocking collectives  18.1 us (35%)
  starting transfers between devices  6.72 us (13%)
  waiting for transfers between devices  5.66 us (11%)
  between operations  0.83 us (2%)
    all_to_all x1, blocking collectives, local(): lax.all_to_all(outgoing, ('row', 'col'), split_axis=0, concat_axis=0, til...  18.1 us
    pallas_call x1, Pallas kernels, local(): pl.pallas_call(functools.partial(apply_kernel, tiles, rows_each, row_coun...  5.72 us
    pallas_call x1, Pallas kernels, local(): pl.pallas_call(functools.partial(weir_kernel, sections, steps, tiles, cap...  5.08 us
    ppermute x1, waiting for transfers between devices, swapped(): two = lax.ppermute(jnp.where(odd, right, left), 'col', outer)  3.91 us
    pallas_call x1, Pallas kernels, local(): pl.pallas_call(functools.partial(cell_kernel, tiles, capacity, sections *...  2.78 us
    pallas_call x1, Pallas kernels, local(): pl.pallas_call(functools.partial(solve_kernel, sections), out_shape=(jax....  2.43 us
    ppermute x1, starting transfers between devices, swapped(): two = lax.ppermute(jnp.where(odd, right, left), 'col', outer)  2.14 us
    ppermute x2, starting transfers between devices, shifted(): lax.ppermute(block, axis, [(i, (i + step) % count) for i in range(count)])  1.8 us
  transfers between devices with their start and end apart: 6, of which 4 were waited for; matrix products, arithmetic and copies ran while one was open for 0% of the time, Pallas kernels for 8%

profile of v1, /device:TPU:2, one launch (start us, length us, event | category | flops | bytes accessed | tf_op | source)
XLA Modules:
  0.0 51.4 jit_solution(10969596940023236060)
XLA Ops:
  0.6 0.0 copy-start.9
  0.6 2.4 %solve.1 = (f32[16,10,8,128]{3,2,1,0:T(8,128)}, f32[20,8,128]{2,1,0:T(8,128)}) custom-call(f32[512,128]{1,0:T(8,128)} %bitcast.32, f32[512,128]{1,0:T(8,128)} %bitcast.33, f32[512,128]{1,0:T(8,128)} %bitcast.34, f32[256,128]{1,0:T(8,128)} %bitcast.35), custom_call_target="tpu_custom_call" | custom-call | tf_op jit(solution)/shard_map/solve/pallas_call | solution.py:557
  3.1 0.1 collective-permute-start
  3.2 0.0 copy-done.9
  3.2 0.0 copy-start.1
  3.2 1.4 %rank.1.slot_ref.refs_5_ = s32[128,128]{1,0:T(8,128)S(1)} custom-call(s32[128,128]{1,0:T(8,128)S(1)} %bitcast.31), custom_call_target="tpu_custom_call" | custom-call | flops 268435456 | bytes 131072 | tf_op jit(solution)/shard_map/rank/pallas_call | solution.py:576
  4.6 0.1 collective-permute-done.other_ref
  4.6 0.0 copy-done.1
  4.6 0.7 %merge.1 = (f32[20,8,128]{2,1,0:T(8,128)}, f32[20,8,128]{2,1,0:T(8,128)S(1)}, f32[6,8,128]{2,1,0:T(8,128)S(1)}) custom-call(s32[1]{0:T(128)} %bitcast.position_ref.refs_0_, f32[20,8,128]{2,1,0:T(8,128)S(1)} %copy-done.1, f32[20,8,128]{2,1,0:T(8,128)S(1)} %collective-permute-done.other_ref), custom_call_target="tpu_custom_call" | custom-call | tf_op jit(solution)/shard_map/merge/pallas_call | solution.py:590
  5.3 1.5 %collective-permute-start.1 = (f32[6,8,128]{2,1,0:T(8,128)S(1)}, f32[6,8,128]{2,1,0:T(8,128)S(1)}, u32[]{:S(2)}, u32[]{:S(2)}) collective-permute-start(f32[6,8,128]{2,1,0:T(8,128)S(1)} %get-tuple-element.19.after.refs_1_), channel_id=1, source_target_pairs={{0,16},{8,24},{16,0},{24,8},{1,17},{9,25},{17,1},{25,9},{2,18},{10... | collective-permute-start | bytes 73736 | tf_op jit(solution)/shard_map/ppermute | solution.py:507
  6.9 0.0 copy-done.10
  6.9 2.8 %cells.1.refs_6_ = f32[32,8,128]{2,1,0:T(8,128)S(1)} custom-call(s32[128,128]{1,0:T(8,128)S(1)} %rank.1.slot_ref.refs_5_, s32[16,1024]{1,0:T(8,128)S(1)} %copy-done.10, s32[16,1024]{1,0:T(8,128)S(1)} %copy-done.11, f32[6,8,128]{2,1,0:T(8,128)S(1)} %get-tuple-element.19.after.refs_1_), custom_call_target="tpu_custom_call" | custom-call | flops 2147483648 | bytes 262144 | tf_op jit(solution)/shard_map/cells/pallas_call | solution.py:600
  9.6 0.0 collective-permute-done.1.refs_2_
  9.7 5.1 %weirs.1 = (f32[256,128]{1,0:T(8,128)}, f32[32,24,128]{2,1,0:T(8,128)S(1)}) custom-call(s32[1]{0:T(128)} %bitcast.position_ref.refs_0_, f32[6,8,128]{2,1,0:T(8,128)S(1)} %get-tuple-element.19.after.refs_1_, f32[6,8,128]{2,1,0:T(8,128)S(1)} %collective-permute-done.1.refs_2_, f32[20,8,128]{2,1,0:T(8,128)S(1)} %get-tuple-element.20.refs_3_, ...), custom_call_target="tpu_custom_call" | custom-call | tf_op jit(solution)/shard_map/weirs/pallas_call | solution.py:616
  14.8 0.0 copy-start.4
  14.8 0.0 copy-start.5
  14.8 0.0 copy-start.6
  14.8 0.0 copy-start.7
  14.8 0.0 copy-start.8
  14.8 18.1 %all_to_all.5.refs_0_ = f32[32,24,128]{2,1,0:T(8,128)S(1)} all-to-all(f32[32,24,128]{2,1,0:T(8,128)S(1)} %get-tuple-element.23), channel_id=1, replica_groups=mesh['row'=4,'col'=8] {'row','col'}, dimensions={0} | all-to-all | bytes 786432 | tf_op jit(solution)/shard_map/all_to_all | solution.py:635
  33.0 5.7 %apply.1 = (f32[5,32,512]{2,1,0:T(8,128)S(1)}, f32[8,512]{1,0:T(8,128)S(1)}, f32[8,512]{1,0:T(8,128)S(1)}) custom-call(f32[32,24,128]{2,1,0:T(8,128)S(1)} %all_to_all.5.refs_0_, f32[32,512]{1,0:T(8,128)S(1)} %copy-done.4, f32[32,512]{1,0:T(8,128)S(1)} %copy-done.5, f32[32,512]{1,0:T(8,128)S(1)} %copy-done.6, f32[32,512]{1,0:T(8,128)S(1)} %copy-done.7, ...), custom_call_target="tpu_custom_call" | custom-call | tf_op jit(solution)/shard_map/apply/pallas_call | solution.py:637
  38.7 0.2 collective-permute-start.2
  38.9 1.6 %collective-permute-start.3 = (f32[8,512]{1,0:T(8,128)S(1)}, f32[8,512]{1,0:T(8,128)S(1)}, u32[]{:S(2)}, u32[]{:S(2)}) collective-permute-start(f32[8,512]{1,0:T(8,128)S(1)} %get-tuple-element.26), channel_id=1, source_target_pairs={{0,24},{8,0},{16,8},{24,16},{1,25},{9,1},{17,9},{25,17},{2,26},{10... | collective-permute-start | bytes 49160 | tf_op jit(solution)/shard_map/ppermute | solution.py:503
  40.5 1.4 %collective-permute-done.2.above_ref = f32[8,512]{1,0:T(8,128)S(1)} collective-permute-done((f32[8,512]{1,0:T(8,128)S(1)}, f32[8,512]{1,0:T(8,128)S(1)}, u32[]{:S(2)}, u32[]{:S(2)}) %collective-permute-start.2) | collective-permute-done | bytes 16416 | tf_op jit(solution)/shard_map/ppermute | solution.py:503
  41.9 0.0 collective-permute-done.3.below_ref
  41.9 0.1 sides.1
  42.1 1.2 %collective-permute-start.4 = (f32[8,128]{1,0:T(8,128)S(1)}, f32[8,128]{1,0:T(8,128)S(1)}, u32[]{:S(2)}, u32[]{:S(2)}) collective-permute-start(f32[8,128]{1,0:T(8,128)S(1)} %get-tuple-element.35), channel_id=1, source_target_pairs={{0,1},{1,0},{2,3},{3,2},{4,5},{5,4},{6,7},{7,6},{8,9},{9,8},{10,11... | collective-permute-start | bytes 12296 | tf_op jit(solution)/shard_map/ppermute | solution.py:516
  43.3 2.1 %collective-permute-start.5 = (f32[8,128]{1,0:T(8,128)S(1)}, f32[8,128]{1,0:T(8,128)S(1)}, u32[]{:S(2)}, u32[]{:S(2)}) collective-permute-start(f32[8,128]{1,0:T(8,128)S(1)} %get-tuple-element.34), channel_id=1, source_target_pairs={{0,0},{7,7},{1,2},{2,1},{3,4},{4,3},{5,6},{6,5},{8,8},{15,15},{9,1... | collective-permute-start | bytes 12296 | tf_op jit(solution)/shard_map/ppermute | solution.py:517
  45.4 0.1 pad_add_fusion.closed_ref
  45.5 0.2 collective-permute-done.4
  45.7 3.9 %collective-permute-done.5 = f32[8,128]{1,0:T(8,128)S(1)} collective-permute-done((f32[8,128]{1,0:T(8,128)S(1)}, f32[8,128]{1,0:T(8,128)S(1)}, u32[]{:S(2)}, u32[]{:S(2)}) %collective-permute-start.5) | collective-permute-done | bytes 4128 | tf_op jit(solution)/shard_map/ppermute | solution.py:517
  49.7 1.7 %flood.1 = (f32[32,512]{1,0:T(8,128)}, f32[32,512]{1,0:T(8,128)}, f32[32,512]{1,0:T(8,128)}) custom-call(s32[4]{0:T(128)S(1)} %pad_add_fusion.closed_ref, f32[5,32,512]{2,1,0:T(8,128)S(1)} %get-tuple-element.24.tile_ref, f32[8,512]{1,0:T(8,128)S(1)} %collective-permute-done.2.above_ref, f32[8,512]{1,0:T(8,128)S(1)} %collective-permute-done.3.below_ref, ...), custom_call_target="tpu_custom_call" | custom-call | tf_op jit(solution)/shard_map/flood/pallas_call | solution.py:672
  (16 shorter events, 0.0 us)
Async XLA Ops:
  0.6 2.5 %copy-start.9 = (s32[1,1,16,1024,1]{3,4,2,1,0:T(1,128)S(1)}, s32[1,1,16,1024,1]{3,4,2,1,0:T(1,128)}, u32[]{:S(2)}) copy-start(s32[1,1,16,1024,1]{3,4,2,1,0:T(1,128)} %param.20) | copy-start | bytes 196612
  3.1 1.6 %collective-permute-start = (f32[20,8,128]{2,1,0:T(8,128)}, f32[20,8,128]{2,1,0:T(8,128)S(1)}, u32[]{:S(2)}, u32[]{:S(2)}) collective-permute-start(f32[20,8,128]{2,1,0:T(8,128)} %get-tuple-element.18.own_ref), channel_id=1, source_target_pairs={{0,8},{8,0},{16,24},{24,16},{1,9},{9,1},{17,25},{25,17},{2,10},{10... | collective-permute-start | bytes 245768 | tf_op jit(solution)/shard_map/ppermute | solution.py:507
  3.2 1.5 %copy-start.1 = (f32[20,8,128]{2,1,0:T(8,128)S(1)}, f32[20,8,128]{2,1,0:T(8,128)}, u32[]{:S(2)}) copy-start(f32[20,8,128]{2,1,0:T(8,128)} %get-tuple-element.18.own_ref) | copy-start | bytes 245764
  4.6 2.2 %copy-start.10 = (s32[16,1024]{1,0:T(8,128)S(1)}, s32[16,1024]{1,0:T(8,128)}, u32[]{:S(2)}) copy-start(s32[16,1024]{1,0:T(8,128)} %row_in.1) | copy-start | bytes 196612
  4.6 2.2 %copy-start.11 = (s32[16,1024]{1,0:T(8,128)S(1)}, s32[16,1024]{1,0:T(8,128)}, u32[]{:S(2)}) copy-start(s32[16,1024]{1,0:T(8,128)} %col_in.1) | copy-start | bytes 196612
  5.3 4.3 %copy-start = (f32[16,10,8,128]{3,2,1,0:T(8,128)S(1)}, f32[16,10,8,128]{3,2,1,0:T(8,128)}, u32[]{:S(2)}) copy-start(f32[16,10,8,128]{3,2,1,0:T(8,128)} %get-tuple-element.21.refs_4_) | copy-start | bytes 1966084
  5.3 4.3 %copy-start.2 = (f32[16,1024]{1,0:T(8,128)S(1)}, f32[16,1024]{1,0:T(8,128)}, u32[]{:S(2)}) copy-start(f32[16,1024]{1,0:T(8,128)} %refs_7_.1) | copy-start | bytes 196612
  5.3 4.4 %copy-start.3 = (s32[16,1024]{1,0:T(8,128)S(1)}, s32[16,1024]{1,0:T(8,128)}, u32[]{:S(2)}) copy-start(s32[16,1024]{1,0:T(8,128)} %refs_8_.1) | copy-start | bytes 196612
  5.3 4.3 %collective-permute-start.1 = (f32[6,8,128]{2,1,0:T(8,128)S(1)}, f32[6,8,128]{2,1,0:T(8,128)S(1)}, u32[]{:S(2)}, u32[]{:S(2)}) collective-permute-start(f32[6,8,128]{2,1,0:T(8,128)S(1)} %get-tuple-element.19.after.refs_1_), channel_id=1, source_target_pairs={{0,16},{8,24},{16,0},{24,8},{1,17},{9,25},{17,1},{25,9},{2,18},{10... | collective-permute-start | bytes 73736 | tf_op jit(solution)/shard_map/ppermute | solution.py:507
  14.8 18.1 %copy-start.4 = (f32[32,512]{1,0:T(8,128)S(1)}, f32[32,512]{1,0:T(8,128)}, u32[]{:S(2)}) copy-start(f32[32,512]{1,0:T(8,128)} %refs_1_.1) | copy-start | bytes 196612
  14.8 18.1 %copy-start.5 = (f32[32,512]{1,0:T(8,128)S(1)}, f32[32,512]{1,0:T(8,128)}, u32[]{:S(2)}) copy-start(f32[32,512]{1,0:T(8,128)} %refs_2_.1) | copy-start | bytes 196612
  14.8 18.1 %copy-start.6 = (f32[32,512]{1,0:T(8,128)S(1)}, f32[32,512]{1,0:T(8,128)}, u32[]{:S(2)}) copy-start(f32[32,512]{1,0:T(8,128)} %refs_3_.1) | copy-start | bytes 196612
  14.8 18.1 %copy-start.7 = (f32[32,512]{1,0:T(8,128)S(1)}, f32[32,512]{1,0:T(8,128)}, u32[]{:S(2)}) copy-start(f32[32,512]{1,0:T(8,128)} %refs_4_.1) | copy-start | bytes 196612
  14.8 18.1 %copy-start.8 = (s32[32,512]{1,0:T(8,128)S(1)}, s32[32,512]{1,0:T(8,128)}, u32[]{:S(2)}) copy-start(s32[32,512]{1,0:T(8,128)} %refs_5_.1) | copy-start | bytes 196612
  38.7 3.2 %collective-permute-start.2 = (f32[8,512]{1,0:T(8,128)S(1)}, f32[8,512]{1,0:T(8,128)S(1)}, u32[]{:S(2)}, u32[]{:S(2)}) collective-permute-start(f32[8,512]{1,0:T(8,128)S(1)} %get-tuple-element.25), channel_id=1, source_target_pairs={{0,8},{8,16},{16,24},{24,0},{1,9},{9,17},{17,25},{25,1},{2,10},{10... | collective-permute-start | bytes 49160 | tf_op jit(solution)/shard_map/ppermute | solution.py:503
  38.9 3.1 %collective-permute-start.3 = (f32[8,512]{1,0:T(8,128)S(1)}, f32[8,512]{1,0:T(8,128)S(1)}, u32[]{:S(2)}, u32[]{:S(2)}) collective-permute-start(f32[8,512]{1,0:T(8,128)S(1)} %get-tuple-element.26), channel_id=1, source_target_pairs={{0,24},{8,0},{16,8},{24,16},{1,25},{9,1},{17,9},{25,17},{2,26},{10... | collective-permute-start | bytes 49160 | tf_op jit(solution)/shard_map/ppermute | solution.py:503
  42.1 3.7 %collective-permute-start.4 = (f32[8,128]{1,0:T(8,128)S(1)}, f32[8,128]{1,0:T(8,128)S(1)}, u32[]{:S(2)}, u32[]{:S(2)}) collective-permute-start(f32[8,128]{1,0:T(8,128)S(1)} %get-tuple-element.35), channel_id=1, source_target_pairs={{0,1},{1,0},{2,3},{3,2},{4,5},{5,4},{6,7},{7,6},{8,9},{9,8},{10,11... | collective-permute-start | bytes 12296 | tf_op jit(solution)/shard_map/ppermute | solution.py:516
  43.3 6.4 %collective-permute-start.5 = (f32[8,128]{1,0:T(8,128)S(1)}, f32[8,128]{1,0:T(8,128)S(1)}, u32[]{:S(2)}, u32[]{:S(2)}) collective-permute-start(f32[8,128]{1,0:T(8,128)S(1)} %get-tuple-element.34), channel_id=1, source_target_pairs={{0,0},{7,7},{1,2},{2,1},{3,4},{4,3},{5,6},{6,5},{8,8},{15,15},{9,1... | collective-permute-start | bytes 12296 | tf_op jit(solution)/shard_map/ppermute | solution.py:517

commit v2 on v1

--- a/solution.py
+++ b/solution.py
@@ -60,14 +60,19 @@
 def solve_kernel(sections, *refs):
     solved_ref, packed_ref = refs[4:6]
     lower_ref, main_ref, upper_ref, rhs_ref = refs[6:10]
-    for copy in start_copies(refs[:4], refs[6:10], refs[10]):
-        copy.wait()
+    pieces = []
+    for n in range(4):
+        parts = [[r.at[pl.ds(n * r.shape[0] // 4, r.shape[0] // 4)] for r in group] for group in (refs[:4], refs[6:10])]
+        pieces.append(start_copies(*parts, refs[10].at[n]))
 
     def block(ref, k):
         return [[ref[pl.ds(k * 32 + i * 16 + j, 8, stride=2), :] for j in range(2)] for i in range(2)]
 
     couples = []
     for k in range(sections):
+        if k % (sections // 4) == 0:
+            for copy in pieces[k // (sections // 4)]:
+                copy.wait()
         lower = block(lower_ref, k)
         main = block(main_ref, k)
         upper = block(upper_ref, k)
@@ -243,30 +248,41 @@
     return (pl.ds(over, 8), pl.ds(along, LANES))
 
 
-def fill_slots(high_count, groups, slot_ref, values, total_ref):
+def fill_slots(high_count, groups, slot_ref, values, total_ref, side=None):
+    if side is not None:
+        capacity, side_code, side_ref = side
+        tile_table = table16(high_count * LOW // capacity)
+        side_table = table16(LANES)
+        side_ref[...] = jnp.zeros_like(side_ref)
     high_table = table16(high_count)
     low_table = table16(LOW)
     total_ref[...] = jnp.zeros_like(total_ref)
 
     def body(g, carry):
         slot = slot_ref[pl.ds(pl.multiple_of(g * 8, 8), 8), :]
+        value = values(g)
         left, right = one_hots(
-            (slot // LOW).astype(F32), (slot % LOW).astype(F32), values(g), high_table, low_table
+            (slot // LOW).astype(F32), (slot % LOW).astype(F32), value, high_table, low_table
         )
         total_ref[...] += product(left, right)
+        if side is not None:
+            left, right = one_hots(
+                (slot // capacity).astype(F32), side_code(g).astype(F32), value, tile_table, side_table
+            )
+            side_ref[...] += product(left, right)
         return carry
 
     lax.fori_loop(0, groups, body, 0, unroll=8)
 
 
-def store_slots(tiles, capacity, total_ref, part, scale, out_ref, row):
+def store_slots(tiles, capacity, total_ref, part, scale, out_ref, pitch, row):
     high_count = tiles * capacity // LOW
     per_tile = capacity // LOW
     first = total_ref[pl.ds(part * high_count, high_count), :]
     value = first * scale + total_ref[pl.ds((part + 1) * high_count, high_count), :]
     for t in range(tiles):
         for j in range(LOW // LANES):
-            out_ref[t, pl.ds(row + j * per_tile, per_tile), :] = value[
+            out_ref[pl.ds(t * pitch + row + j * per_tile, per_tile), :] = value[
                 t * per_tile : (t + 1) * per_tile, j * LANES : (j + 1) * LANES
             ]
 
@@ -306,15 +322,15 @@
         return [high.astype(F32), (col % LOW).astype(F32)]
 
     fill_slots(tiles * capacity // LOW, groups, slot_ref, values, total_ref)
-    store_slots(tiles, capacity, total_ref, 0, float(LOW), cells_ref, 0)
-
-
-def weir_kernel(sections, steps, tiles, capacity, *refs):
+    store_slots(tiles, capacity, total_ref, 0, float(LOW), cells_ref, capacity // LANES, 0)
+
+
+def weir_kernel(sections, steps, tiles, capacity, row_count, col_count, *refs):
     position_ref, own_ref, other_ref, map_ref = refs[:4]
-    solved_ref, slot_ref, cells_ref, crest_in, regime_in = refs[4:9]
-    state_out, out_ref = refs[9:11]
-    crest_ref, regime_ref, state_ref, phase_ref, total_ref, sems = refs[11:]
-    copies = start_copies((crest_in, regime_in), (crest_ref, regime_ref), sems)
+    solved_ref, slot_ref, cells_ref = refs[4:7]
+    state_out, out_ref = refs[11:13]
+    crest_ref, regime_ref, row_ref, col_ref, state_ref, phase_ref, total_ref, side_ref, sems = refs[13:]
+    copies = start_copies(refs[7:11], (crest_ref, regime_ref, row_ref, col_ref), sems)
     late = ((position_ref[0] >> (steps - 1)) & 1) == 1
     own = [load_pair(own_ref, 0), load_square(own_ref, 2)]
     other = [load_pair(other_ref, 0), load_square(other_ref, 2)]
@@ -345,7 +361,7 @@
             if i == 0:
                 phase_ref[pl.ds((k // 8) * 64 + k % 8, 8, stride=8), :] = state
 
-    state_copy = pltpu.make_async_copy(state_ref, state_out, sems.at[2])
+    state_copy = pltpu.make_async_copy(state_ref, state_out, sems.at[4])
     state_copy.start()
     for copy in copies:
         copy.wait()
@@ -362,23 +378,59 @@
         )
         return [*halves(WEIR_GAIN * (free + sub * phase)), *halves(WEIR_GAIN * sub)]
 
-    fill_slots(tiles * capacity // LOW, sections, slot_ref, values, total_ref)
+    def side_code(g):
+        col = col_ref[group_at(g)]
+        place = jnp.where(col < 2, col, jnp.where(col >= col_count - 2, col - (col_count - 4), -1))
+        return jnp.where(place >= 0, place * row_count + row_ref[group_at(g)], -1)
+
+    side = (capacity, side_code, side_ref)
+    fill_slots(tiles * capacity // LOW, sections, slot_ref, values, total_ref, side)
     rows_each = capacity // LANES
+    pitch = 3 * rows_each + 2
+    at = lax.broadcasted_iota(jnp.int32, (tiles, LANES), 1)
+    first_cols = at < 2 * row_count
     for v in range(2):
-        store_slots(tiles, capacity, total_ref, 2 * v, 1.0, out_ref, v * rows_each)
-    out_ref[:, pl.ds(2 * rows_each, rows_each), :] = cells_ref[...]
+        store_slots(tiles, capacity, total_ref, 2 * v, 1.0, out_ref, pitch, v * rows_each)
+        sums = side_ref[pl.ds(2 * v * tiles, tiles), :] + side_ref[pl.ds((2 * v + 1) * tiles, tiles), :]
+        beside = jnp.where(first_cols, pltpu.roll(sums, tiles - 1, 0), pltpu.roll(sums, 1, 0))
+        out_ref[pl.ds(3 * rows_each + v, tiles, stride=pitch), :] = beside
+    for t in range(tiles):
+        out_ref[pl.ds(t * pitch + 2 * rows_each, rows_each), :] = cells_ref[pl.ds(t * rows_each, rows_each), :]
     state_copy.wait()
 
 
+def side_lanes(n):
+    at = lax.broadcasted_iota(jnp.int32, (8, LANES), 1)
+    return (at == 2 * n) | (at == 2 * n + 1)
+
+
+def stage_kernel(row_count, col_count, *refs):
+    tile_ref, left_ref, right_ref, wet_ref, sems = refs[6:]
+    for copy in start_copies(refs[:5], [tile_ref.at[n] for n in range(4)] + [wet_ref], sems):
+        copy.wait()
+    tile_ref[4] = wet_ref[...].astype(F32) * (TIME_STEP / CELL_WIDTH)
+    left = jnp.zeros(left_ref.shape, F32)
+    right = left
+    for t in range(row_count // 8):
+        for n in range(5):
+            at = 5 * t + n
+            first = tile_ref[n, pl.ds(8 * t, 8), pl.ds(0, LANES)]
+            last = tile_ref[n, pl.ds(8 * t, 8), pl.ds(col_count - LANES, LANES)]
+            left = jnp.where(side_lanes(at), pltpu.roll(first, 2 * at, 1), left)
+            right = jnp.where(side_lanes(at), pltpu.roll(last, 2 * at + 2, 1), right)
+    left_ref[...] = left
+    right_ref[...] = right
+
+
+def unpacked(strip, n, rows, lane):
+    parts = [pltpu.roll(strip, (lane - 2 * (5 * t + n)) % LANES, 1) for t in range(rows // 8)]
+    return jnp.concatenate(parts, 0)
+
+
 def apply_kernel(sources, rows_each, row_count, col_count, *refs):
-    in_ref, bed_in, depth_in, first_in, second_in, wet_in = refs[:6]
-    tile_ref, top_ref, bottom_ref = refs[6:9]
-    depth_ref, wet_ref, total_ref, sems = refs[9:]
-    copies = start_copies(
-        (bed_in, depth_in, first_in, second_in, wet_in),
-        (tile_ref.at[1], depth_ref, tile_ref.at[2], tile_ref.at[3], wet_ref),
-        sems,
-    )
+    in_ref, tile_ref, before_ref, after_ref = refs[:4]
+    depth_ref, top_ref, bottom_ref, left_ref, right_ref, total_ref = refs[4:]
+    pitch = 3 * rows_each + 2
     high_count = row_count * col_count // LOW
     high_table = table16(high_count)
     low_table = table16(LOW)
@@ -388,7 +440,7 @@
     def body(g, carry):
         def part(v):
             return jnp.concatenate(
-                [in_ref[g * step + n, pl.ds(v * rows_each, rows_each), :] for n in range(step)], 0
+                [in_ref[pl.ds((g * step + n) * pitch + v * rows_each, rows_each), :] for n in range(step)], 0
             )
 
         cell = part(2).astype(jnp.int32)
@@ -403,24 +455,54 @@
         return carry
 
     lax.fori_loop(0, sources // step, body, 0, unroll=8)
-    for copy in copies:
-        copy.wait()
-    tile_ref[4] = wet_ref[...].astype(F32) * (TIME_STEP / CELL_WIDTH)
     for n in range(col_count // LOW):
         def summed(v):
             start = 2 * v * high_count + n * row_count
             return total_ref[pl.ds(start, row_count), :] + total_ref[pl.ds(start + high_count, row_count), :]
 
         cols = pl.ds(n * LOW, LOW)
-        depth = depth_ref[:, cols]
+        depth = tile_ref[0, :, cols]
         surface = tile_ref[1, :, cols] + depth
-        tile_ref[0, :, cols] = jnp.maximum(depth + (summed(0) - summed(1) * surface), 0.0)
-    for out, near, rows in ((top_ref, 0, (0, 1)), (bottom_ref, row_count - 1, (row_count - 2, row_count - 1))):
-        for n in range(3):
-            for i in range(2):
-                out[pl.ds(2 * n + i, 1), :] = tile_ref[n, pl.ds(rows[i], 1), :]
+        depth_ref[:, cols] = jnp.maximum(depth + (summed(0) - summed(1) * surface), 0.0)
+    row_at = lax.broadcasted_iota(jnp.int32, (row_count, LANES), 0)
+    col_at = lax.broadcasted_iota(jnp.int32, (row_count, LANES), 1)
+
+    def columns(v, lane, place):
+        sums = jnp.sum(in_ref[pl.ds(3 * rows_each + v, sources, stride=pitch), :], axis=0, keepdims=True)
+        result = jnp.zeros((row_count, LANES), F32)
+        for i in range(2):
+            wanted = col_at == (place + i) * row_count + row_at
+            column = jnp.sum(jnp.where(wanted, sums, 0.0), axis=1, keepdims=True)
+            result = jnp.where(col_at == lane + i, column, result)
+        return result
+
+    edges = ((top_ref, 0, (0, 1)), (bottom_ref, row_count - 1, (row_count - 2, row_count - 1)))
+    lane_at = lax.broadcasted_iota(jnp.int32, (1, LANES), 1)
+    corners = {(i, j): jnp.zeros((1, LANES), F32) for i in range(2) for j in range(2)}
+    for out, strip_ref, lane, place in ((left_ref, before_ref, LANES - 2, 2), (right_ref, after_ref, 0, 0)):
+        strip = strip_ref[...]
+        arrays = [unpacked(strip, n, row_count, lane) for n in range(5)]
+        surface = arrays[1] + arrays[0]
+        constant, slope = columns(0, lane, place), columns(1, lane, place)
+        arrays[0] = jnp.maximum(arrays[0] + (constant - slope * surface), 0.0)
+        for n in range(5):
+            out[n] = arrays[n]
+            start = 2 * n + (LANES // 2 if place == 0 else 0)
+            mine = (lane_at == start) | (lane_at == start + 1)
+            for i, (_, _, rows) in enumerate(edges):
+                for j in range(2):
+                    moved = pltpu.roll(arrays[n][rows[j] : rows[j] + 1], (start - lane) % LANES, 1)
+                    corners[i, j] = jnp.where(mine, moved, corners[i, j])
+    cols = pl.ds(0, col_count)
+    for i, (out, near, rows) in enumerate(edges):
+        for j in range(2):
+            out[pl.ds(j, 1), cols] = depth_ref[pl.ds(rows[j], 1), :]
+            for n in (1, 2):
+                out[pl.ds(2 * n + j, 1), cols] = tile_ref[n, pl.ds(rows[j], 1), :]
+            out[pl.ds(j, 1), pl.ds(col_count, LANES)] = corners[i, j]
         for n in (3, 4):
-            out[pl.ds(3 + n, 1), :] = tile_ref[n, pl.ds(near, 1), :]
+            out[pl.ds(3 + n, 1), cols] = tile_ref[n, pl.ds(near, 1), :]
+        out[pl.ds(2, 6), pl.ds(col_count, LANES)] = jnp.zeros((6, LANES), F32)
 
 
 def face_flux(eta_here, eta_next, bed_here, bed_next, old_flux):
@@ -433,49 +515,40 @@
     return pushed / (1.0 + GRAVITY * TIME_STEP * MANNING_SQ * jnp.abs(old_flux) * friction)
 
 
-def pad_rows(n, tile_ref, above_ref, below_ref, cols):
+def halo_rows(n, ref, start, cols):
     at = lax.broadcasted_iota(jnp.int32, (8, 1), 0)
     row = 2 * n if n < 3 else 3 + n
-    low = above_ref[pl.ds(row, 1), cols]
-    high = below_ref[pl.ds(row, 1), cols]
-    if n < 3:
-        low_last = above_ref[pl.ds(row + 1, 1), cols]
-        high_last = below_ref[pl.ds(row + 1, 1), cols]
-    else:
-        low_last, high_last = low, high
-    low = jnp.where(at == 6, low, jnp.where(at == 7, low_last, 0.0))
-    high = jnp.where(at == 0, high, jnp.where(at == 1, high_last, 0.0))
-    return jnp.concatenate([low, tile_ref[n, :, cols], high], 0)
-
-
-def side_lanes(n):
-    at = lax.broadcasted_iota(jnp.int32, (8, LANES), 1)
-    return (at == 2 * n) | (at == 2 * n + 1)
-
-
-def sides_kernel(col_count, tile_ref, above_ref, below_ref, left_ref, right_ref):
-    left = jnp.zeros(left_ref.shape, F32)
-    right = left
-    for n in range(5):
-        first = pad_rows(n, tile_ref, above_ref, below_ref, pl.ds(0, LANES))
-        last = pad_rows(n, tile_ref, above_ref, below_ref, pl.ds(col_count - LANES, LANES))
-        for t in range(first.shape[0] // 8):
-            at = 5 * t + n
-            rows = slice(8 * t, 8 * t + 8)
-            left = jnp.where(side_lanes(at), pltpu.roll(first[rows], 2 * at, 1), left)
-            right = jnp.where(side_lanes(at), pltpu.roll(last[rows], 2 * at + 2, 1), right)
-    left_ref[...] = left
-    right_ref[...] = right
-
-
-def flood_kernel(row_count, col_count, closed_ref, tile_ref, above_ref, below_ref, before_ref, after_ref, *outs):
+    one = ref[pl.ds(row, 1), cols]
+    two = ref[pl.ds(row + 1, 1), cols] if n < 3 else one
+    return jnp.where(at == start, one, jnp.where(at == start + 1, two, 0.0))
+
+
+def corner_rows(n, ref, start, cols, lane, place):
+    at = lax.broadcasted_iota(jnp.int32, (8, 1), 0)
+    shift = (lane - 2 * n - place) % LANES
+    one, two = (pltpu.roll(ref[pl.ds(j, 1), cols], shift, 1) for j in range(2))
+    return jnp.where(at == start, one, jnp.where(at == start + 1, two, 0.0))
+
+
+def flood_kernel(row_count, col_count, *refs):
+    closed_ref, tile_ref, depth_ref, left_ref, right_ref, above_ref, below_ref = refs[:7]
+    outs = refs[7:]
+    inner = pl.ds(0, col_count)
+    outer = pl.ds(col_count, LANES)
     arrays = []
     for n in range(5):
-        at = [5 * t + n for t in range(row_count // 8 + 2)]
-        before = jnp.concatenate([pltpu.roll(before_ref[...], LANES - 2 - 2 * m, 1) for m in at], 0)
-        after = jnp.concatenate([pltpu.roll(after_ref[...], (LANES - 2 * m) % LANES, 1) for m in at], 0)
-        inner = pad_rows(n, tile_ref, above_ref, below_ref, slice(None))
-        arrays.append(jnp.concatenate([before, inner, after], 1))
+        columns = []
+        for ref, lane, place in ((left_ref, LANES - 2, 0), (None, 0, 0), (right_ref, 0, LANES // 2)):
+            if ref is None:
+                low = halo_rows(n, above_ref, 6, inner)
+                own = depth_ref[...] if n == 0 else tile_ref[n]
+                high = halo_rows(n, below_ref, 0, inner)
+            else:
+                low = corner_rows(n, above_ref, 6, outer, lane, place)
+                own = ref[n]
+                high = corner_rows(n, below_ref, 0, outer, lane, place)
+            columns.append(jnp.concatenate([low, own, high], 0))
+        arrays.append(jnp.concatenate(columns, 1))
     depth, bed, first, second, wet = arrays
     shape = depth.shape
     row_at = lax.broadcasted_iota(jnp.int32, shape, 0) - 8
@@ -553,6 +626,7 @@
     rows = weirs // LANES
     high_count = tiles * capacity // LOW
     rows_each = capacity // LANES
+    pitch = 3 * rows_each + 2
     river_block = pltpu.VMEM((sections * 4 * lane_rows, LANES), F32)
     solved, packed = pl.pallas_call(
         functools.partial(solve_kernel, sections),
@@ -567,7 +641,7 @@
             river_block,
             river_block,
             pltpu.VMEM((sections * 2 * lane_rows, LANES), F32),
-            pltpu.SemaphoreType.DMA((4,)),
+            pltpu.SemaphoreType.DMA((4, 4)),
         ],
         compiler_params=WIDE,
         name="solve",
@@ -599,7 +673,7 @@
     met = exchanged(sent, "row", steps - 1)
     cells = pl.pallas_call(
         functools.partial(cell_kernel, tiles, capacity, sections * lane_rows // 8, row_count),
-        out_shape=jax.ShapeDtypeStruct((tiles, rows_each, LANES), F32),
+        out_shape=jax.ShapeDtypeStruct((tiles * rows_each, LANES), F32),
         in_specs=[VMEM] + [ANY] * 3,
         out_specs=VMEM,
         scratch_shapes=[
@@ -614,52 +688,55 @@
     )(slots, weir_row, weir_col, sent)
     state_shape = jax.ShapeDtypeStruct((sections * lane_rows * 2, LANES), F32)
     state_rows, outgoing = pl.pallas_call(
-        functools.partial(weir_kernel, sections, steps, tiles, capacity),
-        out_shape=(state_shape, jax.ShapeDtypeStruct((tiles, 3 * rows_each, LANES), F32)),
-        in_specs=[SMEM] + [VMEM] * 6 + [ANY] * 2,
+        functools.partial(weir_kernel, sections, steps, tiles, capacity, row_count, col_count),
+        out_shape=(state_shape, jax.ShapeDtypeStruct((tiles * pitch, LANES), F32)),
+        in_specs=[SMEM] + [VMEM] * 6 + [ANY] * 4,
         out_specs=(ANY, VMEM),
         scratch_shapes=[
             pltpu.VMEM((sections, chains), F32),
             pltpu.VMEM((sections, chains), jnp.int32),
+            pltpu.VMEM((sections, chains), jnp.int32),
+            pltpu.VMEM((sections, chains), jnp.int32),
             pltpu.VMEM(state_shape.shape, F32),
             pltpu.VMEM((rows, LANES), F32),
             pltpu.VMEM((4 * high_count, LOW), F32),
-            pltpu.SemaphoreType.DMA((3,)),
+            pltpu.VMEM((4 * tiles, LANES), F32),
+            pltpu.SemaphoreType.DMA((5,)),
         ],
         compiler_params=PARAMS,
         name="weirs",
-    )(row_at.reshape(1), sent, met, own_map, solved, slots, cells, weir_crest, weir_regime)
+    )(row_at.reshape(1), sent, met, own_map, solved, slots, cells, weir_crest, weir_regime, weir_row, weir_col)
     river_state = (
         state_rows.reshape(sections, lane_rows, 2, LANES).transpose(0, 2, 1, 3).reshape(sections, 2, chains)
     )
-    arrived = lax.all_to_all(outgoing, ("row", "col"), split_axis=0, concat_axis=0, tiled=True)
-    strip = jax.ShapeDtypeStruct((8, col_count), F32)
-    tile, top, bottom = pl.pallas_call(
+    messages = outgoing.reshape(tiles, pitch, 1, LANES)
+    arrived = lax.all_to_all(messages, ("row", "col"), split_axis=0, concat_axis=0, tiled=True)
+    tile_stack = jax.ShapeDtypeStruct((5, row_count, col_count), F32)
+    side = jax.ShapeDtypeStruct((8, LANES), F32)
+    tile, left, right = pl.pallas_call(
+        functools.partial(stage_kernel, row_count, col_count),
+        out_shape=(tile_stack, side, side),
+        in_specs=[ANY] * 6,
+        out_specs=(VMEM, VMEM, VMEM),
+        scratch_shapes=[pltpu.VMEM((row_count, col_count), jnp.int32), pltpu.SemaphoreType.DMA((5,))],
+        compiler_params=PARAMS,
+        name="stage",
+    )(water_depth, bed_level, flux_first, flux_second, wet_mask, outgoing)
+    before, after = swapped(left, right, col_at, col_size)
+    tile_out = jax.ShapeDtypeStruct((row_count, col_count), F32)
+    edge = jax.ShapeDtypeStruct((8, col_count + LANES), F32)
+    flank = jax.ShapeDtypeStruct((5, row_count, LANES), F32)
+    wetted, top, bottom, left, right = pl.pallas_call(
         functools.partial(apply_kernel, tiles, rows_each, row_count, col_count),
-        out_shape=(jax.ShapeDtypeStruct((5, row_count, col_count), F32), strip, strip),
-        in_specs=[VMEM] + [ANY] * 5,
-        out_specs=(VMEM, VMEM, VMEM),
-        scratch_shapes=[
-            pltpu.VMEM((row_count, col_count), F32),
-            pltpu.VMEM((row_count, col_count), jnp.int32),
-            pltpu.VMEM((4 * row_count * col_count // LOW, LOW), F32),
-            pltpu.SemaphoreType.DMA((5,)),
-        ],
+        out_shape=(tile_out, edge, edge, flank, flank),
+        in_specs=[VMEM] * 4,
+        out_specs=(VMEM,) * 5,
+        scratch_shapes=[pltpu.VMEM((4 * row_count * col_count // LOW, LOW), F32)],
         compiler_params=PARAMS,
         name="apply",
-    )(arrived, bed_level, water_depth, flux_first, flux_second, wet_mask)
+    )(arrived.reshape(tiles * pitch, LANES), tile, before, after)
     above = shifted(bottom, "row", 1)
     below = shifted(top, "row", -1)
-    side = jax.ShapeDtypeStruct((8, LANES), F32)
-    left, right = pl.pallas_call(
-        functools.partial(sides_kernel, col_count),
-        out_shape=(side, side),
-        in_specs=[VMEM] * 3,
-        out_specs=(VMEM, VMEM),
-        compiler_params=PARAMS,
-        name="sides",
-    )(tile, above, below)
-    before, after = swapped(left, right, col_at, col_size)
     closed = jnp.stack(
         [
             jnp.where(row_at == 0, -1, -9),
@@ -668,15 +745,14 @@
             jnp.where(col_at == col_size - 1, col_count - 1, -LANES - 1),
         ]
     ).astype(jnp.int32)
-    tile_out = jax.ShapeDtypeStruct((row_count, col_count), F32)
     depth_out, first_out, second_out = pl.pallas_call(
         functools.partial(flood_kernel, row_count, col_count),
         out_shape=(tile_out, tile_out, tile_out),
-        in_specs=[SMEM] + [VMEM] * 5,
+        in_specs=[SMEM] + [VMEM] * 6,
         out_specs=(VMEM, VMEM, VMEM),
         compiler_params=PARAMS,
         name="flood",
-    )(closed, tile, above, below, before, after)
+    )(closed, tile, wetted, left, right, above, below)
     return (river_state, depth_out, first_out, second_out)
 
 

time: 51.6 us -> 49 us (0.950)
  the two profiles are of different devices: /device:TPU:2 before, /device:TPU:0 now
where the time goes in v2:
time: 49 us; the launch traced here: 48.5 us
  Pallas kernels  22.3 us (46%)
  starting transfers between devices  15.4 us (31%)
  waiting for transfers between devices  9.76 us (20%)
  between operations  0.88 us (2%)
    pallas_call x1, Pallas kernels, local(): pl.pallas_call(functools.partial(weir_kernel, sections, steps, tiles, cap...  7.26 us
    all_to_all x1, waiting for transfers between devices, local(): lax.all_to_all(messages, ('row', 'col'), split_axis=0, concat_axis=0, til...  6.72 us
    pallas_call x1, Pallas kernels, local(): pl.pallas_call(functools.partial(apply_kernel, tiles, rows_each, row_coun...  5.51 us
    all_to_all x1, starting transfers between devices, local(): lax.all_to_all(messages, ('row', 'col'), split_axis=0, concat_axis=0, til...  5.33 us
    ppermute x1, starting transfers between devices, swapped(): one = lax.ppermute(jnp.where(odd, left, right), 'col', inner)  4.55 us
    ppermute x2, starting transfers between devices, exchanged(): lax.ppermute(block, axis, [(i, i ^ 1 << step) for i in range(lax.axis_siz...  3.09 us
    pallas_call x1, Pallas kernels, local(): pl.pallas_call(functools.partial(cell_kernel, tiles, capacity, sections *...  2.79 us
    pallas_call x1, Pallas kernels, local(): pl.pallas_call(functools.partial(solve_kernel, sections), out_shape=(jax....  2.37 us
  transfers between devices with their start and end apart: 7, of which 3 were waited for; matrix products, arithmetic and copies ran while one was open for 0% of the time, Pallas kernels for 10%

profile of v2, /device:TPU:0, one launch (start us, length us, event | category | flops | bytes accessed | tf_op | source)
XLA Modules:
  0.0 48.5 jit_solution(12145662740323328348)
XLA Ops:
  0.6 0.0 copy-start.11
  0.6 2.4 %solve.1 = (f32[16,10,8,128]{3,2,1,0:T(8,128)}, f32[20,8,128]{2,1,0:T(8,128)}) custom-call(f32[512,128]{1,0:T(8,128)} %bitcast.35, f32[512,128]{1,0:T(8,128)} %bitcast.36, f32[512,128]{1,0:T(8,128)} %bitcast.37, f32[256,128]{1,0:T(8,128)} %bitcast.38), custom_call_target="tpu_custom_call" | custom-call | tf_op jit(solution)/shard_map/solve/pallas_call | solution.py:631
  3.0 0.5 %collective-permute-start = (f32[20,8,128]{2,1,0:T(8,128)}, f32[20,8,128]{2,1,0:T(8,128)S(1)}, u32[]{:S(2)}, u32[]{:S(2)}) collective-permute-start(f32[20,8,128]{2,1,0:T(8,128)} %get-tuple-element.21.own_ref), channel_id=1, source_target_pairs={{0,8},{8,0},{16,24},{24,16},{1,9},{9,1},{17,25},{25,17},{2,10},{10... | collective-permute-start | bytes 245768 | tf_op jit(solution)/shard_map/ppermute | solution.py:580
  3.5 1.4 %rank.1.slot_ref.refs_5_ = s32[128,128]{1,0:T(8,128)S(1)} custom-call(s32[128,128]{1,0:T(8,128)S(1)} %bitcast.34), custom_call_target="tpu_custom_call" | custom-call | flops 268435456 | bytes 131072 | tf_op jit(solution)/shard_map/rank/pallas_call | solution.py:650
  4.9 0.0 collective-permute-done.other_ref
  4.9 0.0 copy-start.2
  5.0 0.0 copy-start.3
  5.0 0.7 %merge.1 = (f32[20,8,128]{2,1,0:T(8,128)}, f32[20,8,128]{2,1,0:T(8,128)S(1)}, f32[6,8,128]{2,1,0:T(8,128)S(1)}) custom-call(s32[1]{0:T(128)} %bitcast.position_ref.refs_0_, f32[20,8,128]{2,1,0:T(8,128)S(1)} %copy-done.1, f32[20,8,128]{2,1,0:T(8,128)S(1)} %collective-permute-done.other_ref), custom_call_target="tpu_custom_call" | custom-call | tf_op jit(solution)/shard_map/merge/pallas_call | solution.py:664
  5.7 2.6 %collective-permute-start.1 = (f32[6,8,128]{2,1,0:T(8,128)S(1)}, f32[6,8,128]{2,1,0:T(8,128)S(1)}, u32[]{:S(2)}, u32[]{:S(2)}) collective-permute-start(f32[6,8,128]{2,1,0:T(8,128)S(1)} %get-tuple-element.22.after.refs_1_), channel_id=1, source_target_pairs={{0,16},{8,24},{16,0},{24,8},{1,17},{9,25},{17,1},{25,9},{2,18},{10... | collective-permute-start | bytes 73736 | tf_op jit(solution)/shard_map/ppermute | solution.py:580
  8.2 0.0 copy-done.2
  8.2 2.8 %cells.1.refs_6_ = f32[256,128]{1,0:T(8,128)S(1)} custom-call(s32[128,128]{1,0:T(8,128)S(1)} %rank.1.slot_ref.refs_5_, s32[16,1024]{1,0:T(8,128)S(1)} %copy-done.2, s32[16,1024]{1,0:T(8,128)S(1)} %copy-done.3, f32[6,8,128]{2,1,0:T(8,128)S(1)} %get-tuple-element.22.after.refs_1_), custom_call_target="tpu_custom_call" | custom-call | flops 2147483648 | bytes 262144 | tf_op jit(solution)/shard_map/cells/pallas_call | solution.py:674
  11.0 0.0 collective-permute-done.1.refs_2_
  11.1 7.3 %weirs.1 = (f32[256,128]{1,0:T(8,128)}, f32[832,128]{1,0:T(8,128)}) custom-call(s32[1]{0:T(128)} %bitcast.position_ref.refs_0_, f32[6,8,128]{2,1,0:T(8,128)S(1)} %get-tuple-element.22.after.refs_1_, f32[6,8,128]{2,1,0:T(8,128)S(1)} %collective-permute-done.1.refs_2_, f32[20,8,128]{2,1,0:T(8,128)S(1)} %get-tuple-element.23.refs_3_, ...), custom_call_target="tpu_custom_call" | custom-call | tf_op jit(solution)/shard_map/weirs/pallas_call | solution.py:690
  18.3 0.0 copy-start.6
  18.3 0.0 copy-start.7
  18.4 0.0 copy-start.8
  18.4 0.0 copy-start.9
  18.4 0.0 copy-start.10
  18.4 5.3 %all-to-all-start = ((f32[32,26,1,128]{3,2,1,0:T(1,128)}), f32[32,26,1,128]{3,2,1,0:T(1,128)S(1)}, u32[]{:S(2)}, u32[]{:S(2)}) async-start(f32[32,26,1,128]{3,2,1,0:T(1,128)} %bitcast.21), calls=%async_computation | async-start | bytes 851968 | tf_op jit(solution)/shard_map/all_to_all | solution.py:713
  23.8 0.6 %stage.1 = (f32[5,32,512]{2,1,0:T(8,128)S(1)}, f32[8,128]{1,0:T(8,128)S(1)}, f32[8,128]{1,0:T(8,128)S(1)}) custom-call(f32[32,512]{1,0:T(8,128)S(1)} %copy-done.6, f32[32,512]{1,0:T(8,128)S(1)} %copy-done.7, f32[32,512]{1,0:T(8,128)S(1)} %copy-done.8, f32[32,512]{1,0:T(8,128)S(1)} %copy-done.9, s32[32,512]{1,0:T(8,128)S(1)} %copy-done.10, ...), custom_call_target="tpu_custom_call" | custom-call | tf_op jit(solution)/shard_map/stage/pallas_call | solution.py:716
  24.4 0.7 %collective-permute-start.3 = (f32[8,128]{1,0:T(8,128)S(1)}, f32[8,128]{1,0:T(8,128)S(1)}, u32[]{:S(2)}, u32[]{:S(2)}) collective-permute-start(f32[8,128]{1,0:T(8,128)S(1)} %get-tuple-element.40), channel_id=1, source_target_pairs={{0,0},{7,7},{1,2},{2,1},{3,4},{4,3},{5,6},{6,5},{8,8},{15,15},{9,1... | collective-permute-start | bytes 12296 | tf_op jit(solution)/shard_map/ppermute | solution.py:590
  25.1 4.5 %collective-permute-start.2 = (f32[8,128]{1,0:T(8,128)S(1)}, f32[8,128]{1,0:T(8,128)S(1)}, u32[]{:S(2)}, u32[]{:S(2)}) collective-permute-start(f32[8,128]{1,0:T(8,128)S(1)} %get-tuple-element.41), channel_id=1, source_target_pairs={{0,1},{1,0},{2,3},{3,2},{4,5},{5,4},{6,7},{7,6},{8,9},{9,8},{10,11... | collective-permute-start | bytes 12296 | tf_op jit(solution)/shard_map/ppermute | solution.py:589
  29.6 0.0 collective-permute-done.3
  29.6 1.6 %collective-permute-done.2 = f32[8,128]{1,0:T(8,128)S(1)} collective-permute-done((f32[8,128]{1,0:T(8,128)S(1)}, f32[8,128]{1,0:T(8,128)S(1)}, u32[]{:S(2)}, u32[]{:S(2)}) %collective-permute-start.2) | collective-permute-done | bytes 4128 | tf_op jit(solution)/shard_map/ppermute | solution.py:589
  31.3 6.7 %all-to-all-done = f32[32,26,1,128]{3,2,1,0:T(1,128)S(1)} async-done(((f32[32,26,1,128]{3,2,1,0:T(1,128)}), f32[32,26,1,128]{3,2,1,0:T(1,128)S(1)}, u32[]{:S(2)}, u32[]{:S(2)}) %all-to-all-start) | async-done | bytes 426016 | tf_op jit(solution)/shard_map/all_to_all | solution.py:713
  38.0 5.5 %apply.1 = (f32[32,512]{1,0:T(8,128)S(1)}, f32[8,640]{1,0:T(8,128)S(1)}, f32[8,640]{1,0:T(8,128)S(1)}, f32[5,32,128]{2,1,0:T(8,128)S(1)}, f32[5,32,128]{2,1,0:T(8,128)S(1)}) custom-call(f32[832,128]{1,0:T(8,128)S(1)} %bitcast.33, f32[5,32,512]{2,1,0:T(8,128)S(1)} %get-tuple-element.27.refs_1_, f32[8,128]{1,0:T(8,128)S(1)} %get-tuple-element.39.refs_2_, ...), custom_call_target="tpu_custom_call" | custom-call | tf_op jit(solution)/shard_map/apply/pallas_call | solution.py:729
  43.5 0.1 collective-permute-start.4
  43.6 1.7 %collective-permute-start.5 = (f32[8,640]{1,0:T(8,128)S(1)}, f32[8,640]{1,0:T(8,128)S(1)}, u32[]{:S(2)}, u32[]{:S(2)}) collective-permute-start(f32[8,640]{1,0:T(8,128)S(1)} %get-tuple-element.34), channel_id=1, source_target_pairs={{0,24},{8,0},{16,8},{24,16},{1,25},{9,1},{17,9},{25,17},{2,26},{10... | collective-permute-start | bytes 61448 | tf_op jit(solution)/shard_map/ppermute | solution.py:576
  45.3 0.1 pad_add_fusion.refs_0_
  45.4 1.4 %collective-permute-done.4.refs_5_ = f32[8,640]{1,0:T(8,128)S(1)} collective-permute-done((f32[8,640]{1,0:T(8,128)S(1)}, f32[8,640]{1,0:T(8,128)S(1)}, u32[]{:S(2)}, u32[]{:S(2)}) %collective-permute-start.4) | collective-permute-done | bytes 20512 | tf_op jit(solution)/shard_map/ppermute | solution.py:576
  46.7 0.0 collective-permute-done.5.refs_6_
  46.8 1.8 %flood.1 = (f32[32,512]{1,0:T(8,128)}, f32[32,512]{1,0:T(8,128)}, f32[32,512]{1,0:T(8,128)}) custom-call(s32[4]{0:T(128)S(1)} %pad_add_fusion.refs_0_, f32[5,32,512]{2,1,0:T(8,128)S(1)} %get-tuple-element.27.refs_1_, f32[32,512]{1,0:T(8,128)S(1)} %get-tuple-element.30.refs_2_, f32[5,32,128]{2,1,0:T(8,128)S(1)} %get-tuple-element.31.refs_3_, ...), custom_call_target="tpu_custom_call" | custom-call | tf_op jit(solution)/shard_map/flood/pallas_call | solution.py:748
  (17 shorter events, 0.0 us)
Async XLA Ops:
  0.6 2.9 %copy-start.11 = (s32[1,1,16,1024,1]{3,4,2,1,0:T(1,128)S(1)}, s32[1,1,16,1024,1]{3,4,2,1,0:T(1,128)}, u32[]{:S(2)}) copy-start(s32[1,1,16,1024,1]{3,4,2,1,0:T(1,128)} %param.20) | copy-start | bytes 196612
  3.0 1.9 %collective-permute-start = (f32[20,8,128]{2,1,0:T(8,128)}, f32[20,8,128]{2,1,0:T(8,128)S(1)}, u32[]{:S(2)}, u32[]{:S(2)}) collective-permute-start(f32[20,8,128]{2,1,0:T(8,128)} %get-tuple-element.21.own_ref), channel_id=1, source_target_pairs={{0,8},{8,0},{16,24},{24,16},{1,9},{9,1},{17,25},{25,17},{2,10},{10... | collective-permute-start | bytes 245768 | tf_op jit(solution)/shard_map/ppermute | solution.py:580
  3.5 1.4 %copy-start.1 = (f32[20,8,128]{2,1,0:T(8,128)S(1)}, f32[20,8,128]{2,1,0:T(8,128)}, u32[]{:S(2)}) copy-start(f32[20,8,128]{2,1,0:T(8,128)} %get-tuple-element.21.own_ref) | copy-start | bytes 245764
  4.9 3.3 %copy-start.2 = (s32[16,1024]{1,0:T(8,128)S(1)}, s32[16,1024]{1,0:T(8,128)}, u32[]{:S(2)}) copy-start(s32[16,1024]{1,0:T(8,128)} %refs_9_.1) | copy-start | bytes 196612
  5.0 3.3 %copy-start.3 = (s32[16,1024]{1,0:T(8,128)S(1)}, s32[16,1024]{1,0:T(8,128)}, u32[]{:S(2)}) copy-start(s32[16,1024]{1,0:T(8,128)} %refs_10_.1) | copy-start | bytes 196612
  5.6 5.4 %copy-start = (f32[16,10,8,128]{3,2,1,0:T(8,128)S(1)}, f32[16,10,8,128]{3,2,1,0:T(8,128)}, u32[]{:S(2)}) copy-start(f32[16,10,8,128]{3,2,1,0:T(8,128)} %get-tuple-element.24.refs_4_) | copy-start | bytes 1966084
  5.6 5.4 %copy-start.4 = (f32[16,1024]{1,0:T(8,128)S(1)}, f32[16,1024]{1,0:T(8,128)}, u32[]{:S(2)}) copy-start(f32[16,1024]{1,0:T(8,128)} %refs_7_.1) | copy-start | bytes 196612
  5.7 5.4 %copy-start.5 = (s32[16,1024]{1,0:T(8,128)S(1)}, s32[16,1024]{1,0:T(8,128)}, u32[]{:S(2)}) copy-start(s32[16,1024]{1,0:T(8,128)} %refs_8_.1) | copy-start | bytes 196612
  5.7 5.4 %collective-permute-start.1 = (f32[6,8,128]{2,1,0:T(8,128)S(1)}, f32[6,8,128]{2,1,0:T(8,128)S(1)}, u32[]{:S(2)}, u32[]{:S(2)}) collective-permute-start(f32[6,8,128]{2,1,0:T(8,128)S(1)} %get-tuple-element.22.after.refs_1_), channel_id=1, source_target_pairs={{0,16},{8,24},{16,0},{24,8},{1,17},{9,25},{17,1},{25,9},{2,18},{10... | collective-permute-start | bytes 73736 | tf_op jit(solution)/shard_map/ppermute | solution.py:580
  18.3 5.4 %copy-start.6 = (f32[32,512]{1,0:T(8,128)S(1)}, f32[32,512]{1,0:T(8,128)}, u32[]{:S(2)}) copy-start(f32[32,512]{1,0:T(8,128)} %refs_0_.1) | copy-start | bytes 196612
  18.3 5.4 %copy-start.7 = (f32[32,512]{1,0:T(8,128)S(1)}, f32[32,512]{1,0:T(8,128)}, u32[]{:S(2)}) copy-start(f32[32,512]{1,0:T(8,128)} %refs_1_.1) | copy-start | bytes 196612
  18.4 5.4 %copy-start.8 = (f32[32,512]{1,0:T(8,128)S(1)}, f32[32,512]{1,0:T(8,128)}, u32[]{:S(2)}) copy-start(f32[32,512]{1,0:T(8,128)} %refs_2_.1) | copy-start | bytes 196612
  18.4 5.4 %copy-start.9 = (f32[32,512]{1,0:T(8,128)S(1)}, f32[32,512]{1,0:T(8,128)}, u32[]{:S(2)}) copy-start(f32[32,512]{1,0:T(8,128)} %refs_3_.1) | copy-start | bytes 196612
  18.4 5.4 %copy-start.10 = (s32[32,512]{1,0:T(8,128)S(1)}, s32[32,512]{1,0:T(8,128)}, u32[]{:S(2)}) copy-start(s32[32,512]{1,0:T(8,128)} %refs_4_.1) | copy-start | bytes 196612
  18.4 19.6 %all-to-all-start = ((f32[32,26,1,128]{3,2,1,0:T(1,128)}), f32[32,26,1,128]{3,2,1,0:T(1,128)S(1)}, u32[]{:S(2)}, u32[]{:S(2)}) async-start(f32[32,26,1,128]{3,2,1,0:T(1,128)} %bitcast.21), calls=%async_computation | async-start | bytes 851968 | tf_op jit(solution)/shard_map/all_to_all | solution.py:713
  24.4 5.2 %collective-permute-start.3 = (f32[8,128]{1,0:T(8,128)S(1)}, f32[8,128]{1,0:T(8,128)S(1)}, u32[]{:S(2)}, u32[]{:S(2)}) collective-permute-start(f32[8,128]{1,0:T(8,128)S(1)} %get-tuple-element.40), channel_id=1, source_target_pairs={{0,0},{7,7},{1,2},{2,1},{3,4},{4,3},{5,6},{6,5},{8,8},{15,15},{9,1... | collective-permute-start | bytes 12296 | tf_op jit(solution)/shard_map/ppermute | solution.py:590
  25.1 6.2 %collective-permute-start.2 = (f32[8,128]{1,0:T(8,128)S(1)}, f32[8,128]{1,0:T(8,128)S(1)}, u32[]{:S(2)}, u32[]{:S(2)}) collective-permute-start(f32[8,128]{1,0:T(8,128)S(1)} %get-tuple-element.41), channel_id=1, source_target_pairs={{0,1},{1,0},{2,3},{3,2},{4,5},{5,4},{6,7},{7,6},{8,9},{9,8},{10,11... | collective-permute-start | bytes 12296 | tf_op jit(solution)/shard_map/ppermute | solution.py:589
  43.5 3.3 %collective-permute-start.4 = (f32[8,640]{1,0:T(8,128)S(1)}, f32[8,640]{1,0:T(8,128)S(1)}, u32[]{:S(2)}, u32[]{:S(2)}) collective-permute-start(f32[8,640]{1,0:T(8,128)S(1)} %get-tuple-element.33), channel_id=1, source_target_pairs={{0,8},{8,16},{16,24},{24,0},{1,9},{9,17},{17,25},{25,1},{2,10},{10... | collective-permute-start | bytes 61448 | tf_op jit(solution)/shard_map/ppermute | solution.py:576
  43.6 3.2 %collective-permute-start.5 = (f32[8,640]{1,0:T(8,128)S(1)}, f32[8,640]{1,0:T(8,128)S(1)}, u32[]{:S(2)}, u32[]{:S(2)}) collective-permute-start(f32[8,640]{1,0:T(8,128)S(1)} %get-tuple-element.34), channel_id=1, source_target_pairs={{0,24},{8,0},{16,8},{24,16},{1,25},{9,1},{17,9},{25,17},{2,26},{10... | collective-permute-start | bytes 61448 | tf_op jit(solution)/shard_map/ppermute | solution.py:576

commit v3 on v2

--- a/solution.py
+++ b/solution.py
@@ -22,6 +22,7 @@
 BF16 = jnp.bfloat16
 LANES = 128
 LOW = 256
+BLOCK = 2
 VMEM = pl.BlockSpec(memory_space=pltpu.VMEM)
 SMEM = pl.BlockSpec(memory_space=pltpu.SMEM)
 ANY = pl.BlockSpec(memory_space=pl.ANY)
@@ -57,13 +58,54 @@
     return [[m[1][1] * scale, -m[0][1] * scale], [-m[1][0] * scale, m[0][0] * scale]]
 
 
+def rank_kernel(tiles, capacity, blocks, tile_ref, slot_ref, base_ref, flag_ref, whole_ref):
+    table = lax.broadcasted_iota(jnp.int32, (tiles, LANES), 0)
+    first_slot = table.astype(F32) * capacity
+    row_at = lax.broadcasted_iota(jnp.int32, (LANES, 2 * LANES), 0)
+    col_at = lax.broadcasted_iota(jnp.int32, (LANES, 2 * LANES), 1)
+    earlier = jnp.where(row_at < col_at, 1.0, 0.0).astype(BF16)
+
+    def body(b, carry):
+        rank, most = carry
+        base = jnp.floor(rank * (1.0 / LOW))
+        base_ref[b] = base
+        offset = first_slot + (rank - base * LOW)
+        start = offset
+        for n in range(BLOCK):
+            g = b * BLOCK + n
+            ids = tile_ref[pl.ds((g // 8) * 64 + g % 8, 8, stride=8), :]
+            hits = [ids[r : r + 1, :] == table for r in range(8)]
+            hot = jnp.concatenate([jnp.where(h, 1.0, 0.0).astype(BF16) for h in hits], 0)
+            counts = jnp.dot(hot, earlier, preferred_element_type=F32)
+            rows, bases = [], []
+            for r in range(8):
+                part = counts[r * tiles : (r + 1) * tiles]
+                place = jnp.where(hits[r], part[:, :LANES] + offset, 0.0)
+                rows.append(jnp.sum(place, axis=0, keepdims=True))
+                bases.append(jnp.sum(jnp.where(hits[r], base * LOW, 0.0), axis=0, keepdims=True))
+                offset = offset + part[:, LANES:]
+            slots = jnp.concatenate(rows, 0)
+            at = pl.ds(pl.multiple_of(g * 8, 8), 8)
+            slot_ref[at, :] = slots.astype(jnp.int32)
+            whole_ref[at, :] = (slots + jnp.concatenate(bases, 0)).astype(jnp.int32)
+        last = jnp.floor((offset - first_slot - 1.0) * (1.0 / LOW))
+        return rank + (offset - start), jnp.maximum(most, last)
+
+    nothing = jnp.zeros((tiles, LANES), F32)
+    most = lax.fori_loop(0, blocks, body, (nothing, nothing), unroll=8)[1]
+    flag_ref[0] = jnp.max(most).astype(jnp.int32)
+
+
 def solve_kernel(sections, *refs):
-    solved_ref, packed_ref = refs[4:6]
-    lower_ref, main_ref, upper_ref, rhs_ref = refs[6:10]
+    inputs, later = refs[:4], refs[4:8]
+    solved_ref, packed_ref = refs[8:10]
+    fetched = refs[10:14]
+    lower_ref, main_ref, upper_ref, rhs_ref, sems, later_sems = refs[14:]
     pieces = []
     for n in range(4):
-        parts = [[r.at[pl.ds(n * r.shape[0] // 4, r.shape[0] // 4)] for r in group] for group in (refs[:4], refs[6:10])]
-        pieces.append(start_copies(*parts, refs[10].at[n]))
+        parts = [[r.at[pl.ds(n * r.shape[0] // 4, r.shape[0] // 4)] for r in group] for group in (inputs, refs[14:18])]
+        pieces.append(start_copies(*parts, sems.at[n]))
+    copies = start_copies(later, fetched, later_sems)
 
     def block(ref, k):
         return [[ref[pl.ds(k * 32 + i * 16 + j, 8, stride=2), :] for j in range(2)] for i in range(2)]
@@ -116,6 +158,8 @@
             packed_ref[8 + 2 * i + j] = tail[1][i][j]
             packed_ref[12 + 2 * i + j] = spike[i][j]
             packed_ref[16 + 2 * i + j] = tail[2][i][j]
+    for copy in copies:
+        copy.wait()
 
 
 def load_pair(ref, n):
@@ -226,7 +270,7 @@
     one = jnp.ones((), BF16)
     zero = jnp.zeros((), BF16)
     left, right = [], []
-    for r in range(8):
+    for r in range(high.shape[0]):
         hit = high_table == rows16(high[r : r + 1])[None]
         left.append(
             jnp.concatenate(
@@ -248,89 +292,98 @@
     return (pl.ds(over, 8), pl.ds(along, LANES))
 
 
-def fill_slots(high_count, groups, slot_ref, values, total_ref, side=None):
+def fill_slots(tiles, capacity, start, stop, most, slot_ref, base_ref, flag_ref, values, total_ref, side=None):
+    windows = capacity // LOW
+    taken = min(most, windows)
+    window_table = table16(taken * tiles)
+    low_table = table16(LOW)
     if side is not None:
-        capacity, side_code, side_ref = side
-        tile_table = table16(high_count * LOW // capacity)
+        side_code, side_ref = side
+        tile_table = table16(tiles)
         side_table = table16(LANES)
         side_ref[...] = jnp.zeros_like(side_ref)
-    high_table = table16(high_count)
+
+    def block_values(b):
+        groups = [values(b * BLOCK + n) for n in range(BLOCK)]
+        return [jnp.concatenate([g[v] for g in groups], 0) for v in range(len(groups[0]))]
+
+    def add_block(b, first, with_side):
+        rows = pl.ds(pl.multiple_of(b * (8 * BLOCK), 8 * BLOCK), 8 * BLOCK)
+        slot = slot_ref[rows, :]
+        value = block_values(b)
+        tile = slot // capacity
+        window = slot % capacity // LOW - first
+        code = jnp.where((window >= 0) & (window < taken), window * tiles + tile, -1)
+        left, right = one_hots(code.astype(F32), (slot % LOW).astype(F32), value, window_table, low_table)
+        found = product(left, right)
+        base = base_ref[b] + first
+        base = jnp.concatenate([base, base], 1)
+        for v in range(len(value)):
+            parts = [found[(v * taken + i) * tiles : (v * taken + i + 1) * tiles] for i in range(taken)]
+            for q in range(windows):
+                put = jnp.where(base == q, parts[0], 0.0)
+                for i in range(1, taken):
+                    put = jnp.where(base == q - i, parts[i], put)
+                total_ref[pl.ds((v * windows + q) * tiles, tiles), :] += put
+        if with_side:
+            code = jnp.concatenate([side_code(b * BLOCK + n) for n in range(BLOCK)], 0)
+            left, right = one_hots(tile.astype(F32), code.astype(F32), value, tile_table, side_table)
+            side_ref[...] += product(left, right)
+
+    def body(b, carry):
+        add_block(b, 0, side is not None)
+        return carry
+
+    lax.fori_loop(start, stop, body, 0, unroll=4)
+    for first in range(taken, windows, taken):
+
+        @pl.when(flag_ref[0] >= first)
+        def _(first=first):
+            def rest(b, carry):
+                add_block(b, first, False)
+                return carry
+
+            lax.fori_loop(start, stop, rest, 0)
+
+
+def store_slots(tiles, capacity, total_ref, part, scale, out_ref, pitch, row):
+    windows = capacity // LOW
+    for q in range(windows):
+        first = total_ref[pl.ds((part * windows + q) * tiles, tiles), :]
+        value = first * scale + total_ref[pl.ds(((part + 1) * windows + q) * tiles, tiles), :]
+        for j in range(LOW // LANES):
+            at = pl.ds(row + j * windows + q, tiles, stride=pitch)
+            out_ref[at, :] = value[:, j * LANES : (j + 1) * LANES]
+
+
+def cell_kernel(tiles, capacity, groups, row_count, *refs):
+    slot_ref, row_ref, col_ref, _, out_ref = refs
+    high_table = table16(tiles * capacity // LOW)
     low_table = table16(LOW)
-    total_ref[...] = jnp.zeros_like(total_ref)
+    out_ref[...] = jnp.zeros_like(out_ref)
 
     def body(g, carry):
         slot = slot_ref[pl.ds(pl.multiple_of(g * 8, 8), 8), :]
-        value = values(g)
-        left, right = one_hots(
-            (slot // LOW).astype(F32), (slot % LOW).astype(F32), value, high_table, low_table
-        )
-        total_ref[...] += product(left, right)
-        if side is not None:
-            left, right = one_hots(
-                (slot // capacity).astype(F32), side_code(g).astype(F32), value, tile_table, side_table
-            )
-            side_ref[...] += product(left, right)
-        return carry
-
-    lax.fori_loop(0, groups, body, 0, unroll=8)
-
-
-def store_slots(tiles, capacity, total_ref, part, scale, out_ref, pitch, row):
-    high_count = tiles * capacity // LOW
-    per_tile = capacity // LOW
-    first = total_ref[pl.ds(part * high_count, high_count), :]
-    value = first * scale + total_ref[pl.ds((part + 1) * high_count, high_count), :]
-    for t in range(tiles):
-        for j in range(LOW // LANES):
-            out_ref[pl.ds(t * pitch + row + j * per_tile, per_tile), :] = value[
-                t * per_tile : (t + 1) * per_tile, j * LANES : (j + 1) * LANES
-            ]
-
-
-def rank_kernel(tiles, capacity, groups, tile_in, slot_ref, tile_ref, sems):
-    start_copies((tile_in,), (tile_ref,), sems)[0].wait()
-    table = lax.broadcasted_iota(jnp.int32, (tiles, LANES), 0)
-    row_at = lax.broadcasted_iota(jnp.int32, (LANES, 2 * LANES), 0)
-    col_at = lax.broadcasted_iota(jnp.int32, (LANES, 2 * LANES), 1)
-    earlier = jnp.where(row_at < col_at, 1.0, 0.0).astype(BF16)
-
-    def body(g, offset):
-        ids = tile_ref[pl.ds((g // 8) * 64 + g % 8, 8, stride=8), :]
-        hits = [ids[r : r + 1, :] == table for r in range(8)]
-        hot = jnp.concatenate([jnp.where(h, 1.0, 0.0).astype(BF16) for h in hits], 0)
-        counts = jnp.dot(hot, earlier, preferred_element_type=F32)
-        rows = []
-        for r in range(8):
-            part = counts[r * tiles : (r + 1) * tiles]
-            place = jnp.where(hits[r], part[:, :LANES] + offset, 0.0)
-            rows.append(jnp.sum(place, axis=0, keepdims=True))
-            offset = offset + part[:, LANES:]
-        slot_ref[pl.ds(g * 8, 8), :] = jnp.concatenate(rows, 0).astype(jnp.int32)
-        return offset
-
-    lax.fori_loop(0, groups, body, table.astype(F32) * capacity, unroll=4)
-
-
-def cell_kernel(tiles, capacity, groups, row_count, slot_ref, row_in, col_in, after, cells_ref, *refs):
-    row_ref, col_ref, total_ref, sems = refs
-    for copy in start_copies((row_in, col_in), (row_ref, col_ref), sems):
-        copy.wait()
-
-    def values(g):
         col = col_ref[group_at(g)]
         high = (col // LOW) * row_count + row_ref[group_at(g)]
-        return [high.astype(F32), (col % LOW).astype(F32)]
-
-    fill_slots(tiles * capacity // LOW, groups, slot_ref, values, total_ref)
-    store_slots(tiles, capacity, total_ref, 0, float(LOW), cells_ref, capacity // LANES, 0)
+        left, right = one_hots(
+            (slot % capacity // LOW * tiles + slot // capacity).astype(F32),
+            (slot % LOW).astype(F32),
+            [high.astype(F32), (col % LOW).astype(F32)],
+            high_table,
+            low_table,
+        )
+        out_ref[...] += product(left, right)
+        return carry
+
+    lax.fori_loop(0, groups, body, 0, unroll=8)
 
 
 def weir_kernel(sections, steps, tiles, capacity, row_count, col_count, *refs):
     position_ref, own_ref, other_ref, map_ref = refs[:4]
-    solved_ref, slot_ref, cells_ref = refs[4:7]
-    state_out, out_ref = refs[11:13]
-    crest_ref, regime_ref, row_ref, col_ref, state_ref, phase_ref, total_ref, side_ref, sems = refs[13:]
-    copies = start_copies(refs[7:11], (crest_ref, regime_ref, row_ref, col_ref), sems)
+    solved_ref, slot_ref, base_ref, flag_ref, cells_ref = refs[4:9]
+    crest_ref, regime_ref, row_ref, col_ref = refs[9:13]
+    state_out, out_ref, state_ref, phase_ref, total_ref, side_ref, sems = refs[13:]
     late = ((position_ref[0] >> (steps - 1)) & 1) == 1
     own = [load_pair(own_ref, 0), load_square(own_ref, 2)]
     other = [load_pair(other_ref, 0), load_square(other_ref, 2)]
@@ -361,10 +414,8 @@
             if i == 0:
                 phase_ref[pl.ds((k // 8) * 64 + k % 8, 8, stride=8), :] = state
 
-    state_copy = pltpu.make_async_copy(state_ref, state_out, sems.at[4])
+    state_copy = pltpu.make_async_copy(state_ref, state_out, sems.at[0])
     state_copy.start()
-    for copy in copies:
-        copy.wait()
 
     def values(g):
         phase = phase_ref[pl.ds(pl.multiple_of(g * 8, 8), 8), :]
@@ -383,8 +434,9 @@
         place = jnp.where(col < 2, col, jnp.where(col >= col_count - 2, col - (col_count - 4), -1))
         return jnp.where(place >= 0, place * row_count + row_ref[group_at(g)], -1)
 
-    side = (capacity, side_code, side_ref)
-    fill_slots(tiles * capacity // LOW, sections, slot_ref, values, total_ref, side)
+    total_ref[...] = jnp.zeros_like(total_ref)
+    side = (side_code, side_ref)
+    fill_slots(tiles, capacity, 0, sections // BLOCK, 2, slot_ref, base_ref, flag_ref, values, total_ref, side)
     rows_each = capacity // LANES
     pitch = 3 * rows_each + 2
     at = lax.broadcasted_iota(jnp.int32, (tiles, LANES), 1)
@@ -394,8 +446,7 @@
         sums = side_ref[pl.ds(2 * v * tiles, tiles), :] + side_ref[pl.ds((2 * v + 1) * tiles, tiles), :]
         beside = jnp.where(first_cols, pltpu.roll(sums, tiles - 1, 0), pltpu.roll(sums, 1, 0))
         out_ref[pl.ds(3 * rows_each + v, tiles, stride=pitch), :] = beside
-    for t in range(tiles):
-        out_ref[pl.ds(t * pitch + 2 * rows_each, rows_each), :] = cells_ref[pl.ds(t * rows_each, rows_each), :]
+    store_slots(tiles, capacity, cells_ref, 0, float(LOW), out_ref, pitch, 2 * rows_each)
     state_copy.wait()
 
 
@@ -429,7 +480,7 @@
 
 def apply_kernel(sources, rows_each, row_count, col_count, *refs):
     in_ref, tile_ref, before_ref, after_ref = refs[:4]
-    depth_ref, top_ref, bottom_ref, left_ref, right_ref, total_ref = refs[4:]
+    depth_ref, top_ref, bottom_ref, side_ref, total_ref = refs[4:]
     pitch = 3 * rows_each + 2
     high_count = row_count * col_count // LOW
     high_table = table16(high_count)
@@ -454,7 +505,7 @@
         total_ref[...] += product(left, right)
         return carry
 
-    lax.fori_loop(0, sources // step, body, 0, unroll=8)
+    lax.fori_loop(0, sources // step, body, 0, unroll=16)
     for n in range(col_count // LOW):
         def summed(v):
             start = 2 * v * high_count + n * row_count
@@ -467,42 +518,31 @@
     row_at = lax.broadcasted_iota(jnp.int32, (row_count, LANES), 0)
     col_at = lax.broadcasted_iota(jnp.int32, (row_count, LANES), 1)
 
-    def columns(v, lane, place):
+    def columns(v):
         sums = jnp.sum(in_ref[pl.ds(3 * rows_each + v, sources, stride=pitch), :], axis=0, keepdims=True)
         result = jnp.zeros((row_count, LANES), F32)
-        for i in range(2):
-            wanted = col_at == (place + i) * row_count + row_at
+        for place, lane in enumerate((0, 1, LANES - 2, LANES - 1)):
+            wanted = col_at == place * row_count + row_at
             column = jnp.sum(jnp.where(wanted, sums, 0.0), axis=1, keepdims=True)
-            result = jnp.where(col_at == lane + i, column, result)
+            result = jnp.where(col_at == lane, column, result)
         return result
 
-    edges = ((top_ref, 0, (0, 1)), (bottom_ref, row_count - 1, (row_count - 2, row_count - 1)))
-    lane_at = lax.broadcasted_iota(jnp.int32, (1, LANES), 1)
-    corners = {(i, j): jnp.zeros((1, LANES), F32) for i in range(2) for j in range(2)}
-    for out, strip_ref, lane, place in ((left_ref, before_ref, LANES - 2, 2), (right_ref, after_ref, 0, 0)):
-        strip = strip_ref[...]
-        arrays = [unpacked(strip, n, row_count, lane) for n in range(5)]
-        surface = arrays[1] + arrays[0]
-        constant, slope = columns(0, lane, place), columns(1, lane, place)
-        arrays[0] = jnp.maximum(arrays[0] + (constant - slope * surface), 0.0)
+    before, after = before_ref[...], after_ref[...]
+    for n in range(5):
+        right = unpacked(after, n, row_count, 0)
+        left = unpacked(before, n, row_count, LANES - 2)
+        side_ref[n] = jnp.where(col_at < LANES // 2, right, left)
+    depth = side_ref[0]
+    surface = side_ref[1] + depth
+    side_ref[0] = jnp.maximum(depth + (columns(0) - columns(1) * surface), 0.0)
+    inner, outer = pl.ds(0, col_count), pl.ds(col_count, LANES)
+    for out, near, rows in ((top_ref, 0, (0, 1)), (bottom_ref, row_count - 1, (row_count - 2, row_count - 1))):
         for n in range(5):
-            out[n] = arrays[n]
-            start = 2 * n + (LANES // 2 if place == 0 else 0)
-            mine = (lane_at == start) | (lane_at == start + 1)
-            for i, (_, _, rows) in enumerate(edges):
-                for j in range(2):
-                    moved = pltpu.roll(arrays[n][rows[j] : rows[j] + 1], (start - lane) % LANES, 1)
-                    corners[i, j] = jnp.where(mine, moved, corners[i, j])
-    cols = pl.ds(0, col_count)
-    for i, (out, near, rows) in enumerate(edges):
-        for j in range(2):
-            out[pl.ds(j, 1), cols] = depth_ref[pl.ds(rows[j], 1), :]
-            for n in (1, 2):
-                out[pl.ds(2 * n + j, 1), cols] = tile_ref[n, pl.ds(rows[j], 1), :]
-            out[pl.ds(j, 1), pl.ds(col_count, LANES)] = corners[i, j]
-        for n in (3, 4):
-            out[pl.ds(3 + n, 1), cols] = tile_ref[n, pl.ds(near, 1), :]
-        out[pl.ds(2, 6), pl.ds(col_count, LANES)] = jnp.zeros((6, LANES), F32)
+            for j in range(2 if n < 3 else 1):
+                row = pl.ds(rows[j] if n < 3 else near, 1)
+                at = pl.ds(2 * n + j if n < 3 else 3 + n, 1)
+                out[at, inner] = depth_ref[row, :] if n == 0 else tile_ref[n, row, :]
+                out[at, outer] = side_ref[n, row, :]
 
 
 def face_flux(eta_here, eta_next, bed_here, bed_next, old_flux):
@@ -515,44 +555,24 @@
     return pushed / (1.0 + GRAVITY * TIME_STEP * MANNING_SQ * jnp.abs(old_flux) * friction)
 
 
-def halo_rows(n, ref, start, cols):
+def flood_kernel(row_count, col_count, *refs):
+    closed_ref, tile_ref, depth_ref, side_ref, above_ref, below_ref = refs[:6]
+    outs, kept, sems = refs[6:9], refs[9], refs[10]
     at = lax.broadcasted_iota(jnp.int32, (8, 1), 0)
-    row = 2 * n if n < 3 else 3 + n
-    one = ref[pl.ds(row, 1), cols]
-    two = ref[pl.ds(row + 1, 1), cols] if n < 3 else one
-    return jnp.where(at == start, one, jnp.where(at == start + 1, two, 0.0))
-
-
-def corner_rows(n, ref, start, cols, lane, place):
-    at = lax.broadcasted_iota(jnp.int32, (8, 1), 0)
-    shift = (lane - 2 * n - place) % LANES
-    one, two = (pltpu.roll(ref[pl.ds(j, 1), cols], shift, 1) for j in range(2))
-    return jnp.where(at == start, one, jnp.where(at == start + 1, two, 0.0))
-
-
-def flood_kernel(row_count, col_count, *refs):
-    closed_ref, tile_ref, depth_ref, left_ref, right_ref, above_ref, below_ref = refs[:7]
-    outs = refs[7:]
-    inner = pl.ds(0, col_count)
-    outer = pl.ds(col_count, LANES)
     arrays = []
     for n in range(5):
-        columns = []
-        for ref, lane, place in ((left_ref, LANES - 2, 0), (None, 0, 0), (right_ref, 0, LANES // 2)):
-            if ref is None:
-                low = halo_rows(n, above_ref, 6, inner)
-                own = depth_ref[...] if n == 0 else tile_ref[n]
-                high = halo_rows(n, below_ref, 0, inner)
-            else:
-                low = corner_rows(n, above_ref, 6, outer, lane, place)
-                own = ref[n]
-                high = corner_rows(n, below_ref, 0, outer, lane, place)
-            columns.append(jnp.concatenate([low, own, high], 0))
-        arrays.append(jnp.concatenate(columns, 1))
+        own = jnp.concatenate([depth_ref[...] if n == 0 else tile_ref[n], side_ref[n]], 1)
+        first_row = 2 * n if n < 3 else 3 + n
+        second_row = first_row + 1 if n < 3 else first_row
+        halo = jnp.where(at == 0, below_ref[pl.ds(first_row, 1), :], 0.0)
+        halo = jnp.where(at == 1, below_ref[pl.ds(second_row, 1), :], halo)
+        halo = jnp.where(at == 6, above_ref[pl.ds(first_row, 1), :], halo)
+        halo = jnp.where(at == 7, above_ref[pl.ds(second_row, 1), :], halo)
+        arrays.append(jnp.concatenate([own, halo], 0))
     depth, bed, first, second, wet = arrays
     shape = depth.shape
-    row_at = lax.broadcasted_iota(jnp.int32, shape, 0) - 8
-    col_at = lax.broadcasted_iota(jnp.int32, shape, 1) - LANES
+    row_at = lax.broadcasted_iota(jnp.int32, shape, 0)
+    col_at = lax.broadcasted_iota(jnp.int32, shape, 1)
     first_shut = (row_at == closed_ref[0]) | (row_at == closed_ref[1])
     second_shut = (col_at == closed_ref[2]) | (col_at == closed_ref[3])
     down = lambda x: pltpu.roll(x, shape[0] - 1, 0)
@@ -561,33 +581,40 @@
     back = lambda x: pltpu.roll(x, 1, 1)
     bed_down = down(bed)
     bed_onward = onward(bed)
-    for _ in range(2):
+    copies = []
+
+    def finish(n, value):
+        kept[n] = value[:row_count, :col_count]
+        copies.append(pltpu.make_async_copy(kept.at[n], outs[n], sems.at[n]))
+        copies[-1].start()
+
+    for step in range(2):
         eta = bed + depth
         first = jnp.where(first_shut, 0.0, face_flux(eta, down(eta), bed, bed_down, first))
+        if step == 1:
+            finish(1, first)
         second = jnp.where(second_shut, 0.0, face_flux(eta, onward(eta), bed, bed_onward, second))
+        if step == 1:
+            finish(2, second)
         depth = depth + wet * (up(first) - first + (back(second) - second))
-    here = (slice(8, 8 + row_count), slice(LANES, LANES + col_count))
-    for out, value in zip(outs, (depth, first, second)):
-        out[...] = value[here]
-
-
-def shifted(block, axis, step):
-    count = lax.axis_size(axis)
-    return lax.ppermute(block, axis, [(i, (i + step) % count) for i in range(count)])
+    finish(0, depth)
+    for copy in copies:
+        copy.wait()
 
 
 def exchanged(block, axis, step):
     return lax.ppermute(block, axis, [(i, i ^ (1 << step)) for i in range(lax.axis_size(axis))])
 
 
-def swapped(left, right, position, count):
-    odd = position % 2 == 1
+def swapped(first, last, axis, ring):
+    count = lax.axis_size(axis)
+    odd = lax.axis_index(axis) % 2 == 1
     inner = [(i, i ^ 1) for i in range(count)]
-    outer = [(0, 0), (count - 1, count - 1)]
-    for i in range(1, count - 1, 2):
-        outer += [(i, i + 1), (i + 1, i)]
-    one = lax.ppermute(jnp.where(odd, left, right), "col", inner)
-    two = lax.ppermute(jnp.where(odd, right, left), "col", outer)
+    outer = [] if ring else [(0, 0), (count - 1, count - 1)]
+    for i in range(1, count if ring else count - 1, 2):
+        outer += [(i, (i + 1) % count), ((i + 1) % count, i)]
+    two = lax.ppermute(jnp.where(odd, last, first), axis, outer)
+    one = lax.ppermute(jnp.where(odd, first, last), axis, inner)
     return jnp.where(odd, one, two), jnp.where(odd, two, one)
 
 
@@ -628,31 +655,52 @@
     rows_each = capacity // LANES
     pitch = 3 * rows_each + 2
     river_block = pltpu.VMEM((sections * 4 * lane_rows, LANES), F32)
-    solved, packed = pl.pallas_call(
+    blocks = sections // BLOCK
+    steps = row_size.bit_length() - 1
+    weir_shape = (sections, chains)
+    whole = jax.ShapeDtypeStruct(weir_shape, jnp.int32)
+    solved, packed, crest, regime, weir_rows, weir_cols = pl.pallas_call(
         functools.partial(solve_kernel, sections),
         out_shape=(
             jax.ShapeDtypeStruct((sections, 10, lane_rows, LANES), F32),
             jax.ShapeDtypeStruct((20, lane_rows, LANES), F32),
+            jax.ShapeDtypeStruct(weir_shape, F32),
+            whole,
+            whole,
+            whole,
         ),
-        in_specs=[ANY] * 4,
-        out_specs=(VMEM, VMEM),
+        in_specs=[ANY] * 8,
+        out_specs=(VMEM,) * 6,
         scratch_shapes=[
             river_block,
             river_block,
             river_block,
             pltpu.VMEM((sections * 2 * lane_rows, LANES), F32),
             pltpu.SemaphoreType.DMA((4, 4)),
+            pltpu.SemaphoreType.DMA((4,)),
         ],
         compiler_params=WIDE,
         name="solve",
-    )(block_rows(river_lower), block_rows(river_main), block_rows(river_upper), rhs_rows)
-    steps = row_size.bit_length() - 1
-    slots = pl.pallas_call(
-        functools.partial(rank_kernel, tiles, capacity, sections * lane_rows // 8),
-        out_shape=jax.ShapeDtypeStruct((rows, LANES), jnp.int32),
-        in_specs=[ANY],
-        out_specs=VMEM,
-        scratch_shapes=[pltpu.VMEM((rows, LANES), jnp.int32), pltpu.SemaphoreType.DMA((1,))],
+    )(
+        block_rows(river_lower),
+        block_rows(river_main),
+        block_rows(river_upper),
+        rhs_rows,
+        weir_crest,
+        weir_regime,
+        weir_row,
+        weir_col,
+    )
+    *places, whole_slots = pl.pallas_call(
+        functools.partial(rank_kernel, tiles, capacity, blocks),
+        out_shape=(
+            jax.ShapeDtypeStruct((rows, LANES), jnp.int32),
+            jax.ShapeDtypeStruct((blocks, tiles, LANES), F32),
+            jax.ShapeDtypeStruct((1,), jnp.int32),
+            jax.ShapeDtypeStruct((rows, LANES), jnp.int32),
+        ),
+        in_specs=[VMEM],
+        out_specs=(VMEM, VMEM, SMEM, VMEM),
         compiler_params=PARAMS,
         cost_estimate=pl.CostEstimate(flops=2 * tiles * weirs * LOW, bytes_accessed=2**17, transcendentals=0),
         name="rank",
@@ -672,40 +720,30 @@
         known = (own_map,)
     met = exchanged(sent, "row", steps - 1)
     cells = pl.pallas_call(
-        functools.partial(cell_kernel, tiles, capacity, sections * lane_rows // 8, row_count),
-        out_shape=jax.ShapeDtypeStruct((tiles * rows_each, LANES), F32),
-        in_specs=[VMEM] + [ANY] * 3,
+        functools.partial(cell_kernel, tiles, capacity, rows // 8, row_count),
+        out_shape=jax.ShapeDtypeStruct((2 * high_count, LOW), F32),
+        in_specs=[VMEM, VMEM, VMEM, ANY],
         out_specs=VMEM,
-        scratch_shapes=[
-            pltpu.VMEM((sections, chains), jnp.int32),
-            pltpu.VMEM((sections, chains), jnp.int32),
-            pltpu.VMEM((2 * high_count, LOW), F32),
-            pltpu.SemaphoreType.DMA((2,)),
-        ],
         compiler_params=PARAMS,
         cost_estimate=pl.CostEstimate(flops=4 * high_count * LOW * weirs, bytes_accessed=2**18, transcendentals=0),
         name="cells",
-    )(slots, weir_row, weir_col, sent)
+    )(whole_slots, weir_rows, weir_cols, sent)
     state_shape = jax.ShapeDtypeStruct((sections * lane_rows * 2, LANES), F32)
     state_rows, outgoing = pl.pallas_call(
         functools.partial(weir_kernel, sections, steps, tiles, capacity, row_count, col_count),
         out_shape=(state_shape, jax.ShapeDtypeStruct((tiles * pitch, LANES), F32)),
-        in_specs=[SMEM] + [VMEM] * 6 + [ANY] * 4,
+        in_specs=[SMEM] + [VMEM] * 5 + [VMEM, SMEM] + [VMEM] * 5,
         out_specs=(ANY, VMEM),
         scratch_shapes=[
-            pltpu.VMEM((sections, chains), F32),
-            pltpu.VMEM((sections, chains), jnp.int32),
-            pltpu.VMEM((sections, chains), jnp.int32),
-            pltpu.VMEM((sections, chains), jnp.int32),
             pltpu.VMEM(state_shape.shape, F32),
             pltpu.VMEM((rows, LANES), F32),
             pltpu.VMEM((4 * high_count, LOW), F32),
             pltpu.VMEM((4 * tiles, LANES), F32),
-            pltpu.SemaphoreType.DMA((5,)),
+            pltpu.SemaphoreType.DMA((1,)),
         ],
         compiler_params=PARAMS,
         name="weirs",
-    )(row_at.reshape(1), sent, met, own_map, solved, slots, cells, weir_crest, weir_regime, weir_row, weir_col)
+    )(row_at.reshape(1), sent, met, own_map, solved, *places, cells, crest, regime, weir_rows, weir_cols)
     river_state = (
         state_rows.reshape(sections, lane_rows, 2, LANES).transpose(0, 2, 1, 3).reshape(sections, 2, chains)
     )
@@ -722,37 +760,37 @@
         compiler_params=PARAMS,
         name="stage",
     )(water_depth, bed_level, flux_first, flux_second, wet_mask, outgoing)
-    before, after = swapped(left, right, col_at, col_size)
+    before, after = swapped(left, right, "col", False)
     tile_out = jax.ShapeDtypeStruct((row_count, col_count), F32)
     edge = jax.ShapeDtypeStruct((8, col_count + LANES), F32)
     flank = jax.ShapeDtypeStruct((5, row_count, LANES), F32)
-    wetted, top, bottom, left, right = pl.pallas_call(
+    wetted, top, bottom, side = pl.pallas_call(
         functools.partial(apply_kernel, tiles, rows_each, row_count, col_count),
-        out_shape=(tile_out, edge, edge, flank, flank),
+        out_shape=(tile_out, edge, edge, flank),
         in_specs=[VMEM] * 4,
-        out_specs=(VMEM,) * 5,
+        out_specs=(VMEM,) * 4,
         scratch_shapes=[pltpu.VMEM((4 * row_count * col_count // LOW, LOW), F32)],
         compiler_params=PARAMS,
         name="apply",
     )(arrived.reshape(tiles * pitch, LANES), tile, before, after)
-    above = shifted(bottom, "row", 1)
-    below = shifted(top, "row", -1)
+    above, below = swapped(top, bottom, "row", True)
     closed = jnp.stack(
         [
-            jnp.where(row_at == 0, -1, -9),
-            jnp.where(row_at == row_size - 1, row_count - 1, -9),
-            jnp.where(col_at == 0, -1, -LANES - 1),
-            jnp.where(col_at == col_size - 1, col_count - 1, -LANES - 1),
+            jnp.where(row_at == 0, row_count + 7, -1),
+            jnp.where(row_at == row_size - 1, row_count - 1, -1),
+            jnp.where(col_at == 0, col_count + LANES - 1, -1),
+            jnp.where(col_at == col_size - 1, col_count - 1, -1),
         ]
     ).astype(jnp.int32)
     depth_out, first_out, second_out = pl.pallas_call(
         functools.partial(flood_kernel, row_count, col_count),
         out_shape=(tile_out, tile_out, tile_out),
-        in_specs=[SMEM] + [VMEM] * 6,
-        out_specs=(VMEM, VMEM, VMEM),
+        in_specs=[SMEM] + [VMEM] * 5,
+        out_specs=(ANY, ANY, ANY),
+        scratch_shapes=[pltpu.VMEM((3, row_count, col_count), F32), pltpu.SemaphoreType.DMA((3,))],
         compiler_params=PARAMS,
         name="flood",
-    )(closed, tile, wetted, left, right, above, below)
+    )(closed, tile, wetted, side, above, below)
     return (river_state, depth_out, first_out, second_out)
 
 

time: 49 us -> 47 us (0.959)
  waiting for transfers between devices: 9.76 us -> 13.6 us
  starting transfers between devices: 15.4 us -> 11.8 us
  Pallas kernels: 22.3 us -> 20.2 us
    ppermute x4, starting transfers between devices: 7 us -> 3.2 us  [the longest x2 1.9 us: swapped(): one = lax.ppermute(jnp.where(odd, first, last), axis, inner)]
    all_to_all x1, waiting for transfers between devices: 6.72 us -> 9.79 us  [local(): lax.all_to_all(messages, ('row', 'col'), split_axis=0, concat_axis=0, til...]
    pallas_call x1, Pallas kernels: 7.26 us -> 5.31 us  [local(): pl.pallas_call(functools.partial(weir_kernel, sections, steps, tiles, cap...]
    ppermute x4, waiting for transfers between devices: 3.04 us -> 3.81 us  [the longest x2 2.1 us: swapped(): two = lax.ppermute(jnp.where(odd, last, first), axis, outer)]
    pallas_call x1, Pallas kernels: 5.51 us -> 4.92 us  [local(): pl.pallas_call(functools.partial(apply_kernel, tiles, rows_each, row_coun...]
  transfers between devices with their start and end apart: 7 -> 7, of which waited for: 3 -> 4; matrix products, arithmetic and copies ran while one was open for 0% -> 0% of each run, Pallas kernels for 10% -> 11%
where the time goes in v3:
time: 47 us; the launch traced here: 46.7 us
  Pallas kernels  20.2 us (43%)
  waiting for transfers between devices  13.6 us (29%)
  starting transfers between devices  11.8 us (25%)
  between operations  0.94 us (2%)
    all_to_all x1, waiting for transfers between devices, local(): lax.all_to_all(messages, ('row', 'col'), split_axis=0, concat_axis=0, til...  9.79 us
    all_to_all x1, starting transfers between devices, local(): lax.all_to_all(messages, ('row', 'col'), split_axis=0, concat_axis=0, til...  5.5 us
    pallas_call x1, Pallas kernels, local(): pl.pallas_call(functools.partial(weir_kernel, sections, steps, tiles, cap...  5.31 us
    pallas_call x1, Pallas kernels, local(): pl.pallas_call(functools.partial(apply_kernel, tiles, rows_each, row_coun...  4.92 us
    ppermute x2, starting transfers between devices, exchanged(): lax.ppermute(block, axis, [(i, i ^ 1 << step) for i in range(lax.axis_siz...  3.07 us
    pallas_call x1, Pallas kernels, local(): pl.pallas_call(functools.partial(cell_kernel, tiles, capacity, rows // 8,...  2.6 us
    pallas_call x1, Pallas kernels, local(): pl.pallas_call(functools.partial(solve_kernel, sections), out_shape=(jax....  2.52 us
    ppermute x2, waiting for transfers between devices, swapped(): two = lax.ppermute(jnp.where(odd, last, first), axis, outer)  2.1 us
  transfers between devices with their start and end apart: 7, of which 4 were waited for; matrix products, arithmetic and copies ran while one was open for 0% of the time, Pallas kernels for 11%

profile of v3, /device:TPU:0, one launch (start us, length us, event | category | flops | bytes accessed | tf_op | source)
XLA Modules:
  0.0 46.7 jit_solution(4435466870131617503)
XLA Ops:
  0.6 0.0 copy-start.11
  0.6 2.5 %solve.1 = (f32[16,10,8,128]{3,2,1,0:T(8,128)}, f32[20,8,128]{2,1,0:T(8,128)}, f32[16,1024]{1,0:T(8,128)}, s32[16,1024]{1,0:T(8,128)}, s32[16,1024]{1,0:T(8,128)}, /*index=5*/s32[16,1024]{1,0:T(8,128)}) custom-call(f32[512,128]{1,0:T(8,128)} %bitcast.35, f32[512,128]{1,0:T(8,128)} %bitcast.36, f32[512,128]{1,0:T(8,128)} %bitcast.37, f32[256,128]{1,0:T(8,128)} %bitcast.38, ...), custom_call_target="tpu_custom_call" | custom-call | tf_op jit(solution)/shard_map/solve/pallas_call | solution.py:662
  3.2 0.5 %collective-permute-start = (f32[20,8,128]{2,1,0:T(8,128)}, f32[20,8,128]{2,1,0:T(8,128)S(1)}, u32[]{:S(2)}, u32[]{:S(2)}) collective-permute-start(f32[20,8,128]{2,1,0:T(8,128)} %get-tuple-element.28.own_ref), channel_id=1, source_target_pairs={{0,8},{8,0},{16,24},{24,16},{1,9},{9,1},{17,25},{25,17},{2,10},{10... | collective-permute-start | bytes 245768 | tf_op jit(solution)/shard_map/ppermute | solution.py:606
  3.7 1.9 %rank.1 = (s32[128,128]{1,0:T(8,128)S(1)}, f32[8,32,128]{2,1,0:T(8,128)S(1)}, s32[1]{0:T(128)}, s32[128,128]{1,0:T(8,128)S(1)}) custom-call(s32[128,128]{1,0:T(8,128)S(1)} %bitcast.34), custom_call_target="tpu_custom_call" | custom-call | flops 268435456 | bytes 131072 | tf_op jit(solution)/shard_map/rank/pallas_call | solution.py:694
  5.6 0.0 collective-permute-done.other_ref
  5.6 0.0 copy-start.9
  5.6 0.0 copy-start.10
  5.6 0.7 %merge.1 = (f32[20,8,128]{2,1,0:T(8,128)}, f32[20,8,128]{2,1,0:T(8,128)S(1)}, f32[6,8,128]{2,1,0:T(8,128)S(1)}) custom-call(s32[1]{0:T(128)} %bitcast.position_ref.refs_0_, f32[20,8,128]{2,1,0:T(8,128)S(1)} %copy-done.1, f32[20,8,128]{2,1,0:T(8,128)S(1)} %collective-permute-done.other_ref), custom_call_target="tpu_custom_call" | custom-call | tf_op jit(solution)/shard_map/merge/pallas_call | solution.py:712
  6.3 2.6 %collective-permute-start.1 = (f32[6,8,128]{2,1,0:T(8,128)S(1)}, f32[6,8,128]{2,1,0:T(8,128)S(1)}, u32[]{:S(2)}, u32[]{:S(2)}) collective-permute-start(f32[6,8,128]{2,1,0:T(8,128)S(1)} %get-tuple-element.29.refs_3_.refs_1_), channel_id=1, source_target_pairs={{0,16},{8,24},{16,0},{24,8},{1,17},{9,25},{17,1},{25,9},{2,18},{10... | collective-permute-start | bytes 73736 | tf_op jit(solution)/shard_map/ppermute | solution.py:606
  8.9 0.0 copy-start.8
  8.9 2.6 %cells.1.refs_8_ = f32[256,256]{1,0:T(8,128)S(1)} custom-call(s32[128,128]{1,0:T(8,128)S(1)} %get-tuple-element.35.refs_0_, s32[16,1024]{1,0:T(8,128)S(1)} %copy-done.9, s32[16,1024]{1,0:T(8,128)S(1)} %copy-done.10, f32[6,8,128]{2,1,0:T(8,128)S(1)} %get-tuple-element.29.refs_3_.refs_1_), custom_call_target="tpu_custom_call" | custom-call | flops 2147483648 | bytes 262144 | tf_op jit(solution)/shard_map/cells/pallas_call | solution.py:722
  11.5 0.0 collective-permute-done.1.refs_2_
  11.5 5.3 %weirs.1 = (f32[256,128]{1,0:T(8,128)}, f32[832,128]{1,0:T(8,128)}) custom-call(s32[1]{0:T(128)} %bitcast.position_ref.refs_0_, f32[6,8,128]{2,1,0:T(8,128)S(1)} %get-tuple-element.29.refs_3_.refs_1_, f32[6,8,128]{2,1,0:T(8,128)S(1)} %collective-permute-done.1.refs_2_, f32[20,8,128]{2,1,0:T(8,128)S(1)} %get-tuple-element.30.refs_3_, ...), custom_call_target="tpu_custom_call" | custom-call | tf_op jit(solution)/shard_map/weirs/pallas_call | solution.py:732
  16.9 0.0 copy-start.2
  16.9 0.0 copy-start.3
  16.9 0.0 copy-start.4
  16.9 0.0 copy-start.5
  16.9 0.0 copy-start.6
  16.9 5.5 %all-to-all-start = ((f32[32,26,1,128]{3,2,1,0:T(1,128)}), f32[32,26,1,128]{3,2,1,0:T(1,128)S(1)}, u32[]{:S(2)}, u32[]{:S(2)}) async-start(f32[32,26,1,128]{3,2,1,0:T(1,128)} %bitcast.21), calls=%async_computation | async-start | bytes 851968 | tf_op jit(solution)/shard_map/all_to_all | solution.py:751
  22.5 0.6 %stage.1 = (f32[5,32,512]{2,1,0:T(8,128)S(1)}, f32[8,128]{1,0:T(8,128)S(1)}, f32[8,128]{1,0:T(8,128)S(1)}) custom-call(f32[32,512]{1,0:T(8,128)S(1)} %copy-done.2, f32[32,512]{1,0:T(8,128)S(1)} %copy-done.3, f32[32,512]{1,0:T(8,128)S(1)} %copy-done.4, f32[32,512]{1,0:T(8,128)S(1)} %copy-done.5, s32[32,512]{1,0:T(8,128)S(1)} %copy-done.6, ...), custom_call_target="tpu_custom_call" | custom-call | tf_op jit(solution)/shard_map/stage/pallas_call | solution.py:754
  23.1 1.8 %collective-permute-start.2 = (f32[8,128]{1,0:T(8,128)S(1)}, f32[8,128]{1,0:T(8,128)S(1)}, u32[]{:S(2)}, u32[]{:S(2)}) collective-permute-start(f32[8,128]{1,0:T(8,128)S(1)} %get-tuple-element.59), channel_id=1, source_target_pairs={{0,1},{1,0},{2,3},{3,2},{4,5},{5,4},{6,7},{7,6},{8,9},{9,8},{10,11... | collective-permute-start | bytes 12296 | tf_op jit(solution)/shard_map/ppermute | solution.py:617
  24.9 0.6 %collective-permute-start.3 = (f32[8,128]{1,0:T(8,128)S(1)}, f32[8,128]{1,0:T(8,128)S(1)}, u32[]{:S(2)}, u32[]{:S(2)}) collective-permute-start(f32[8,128]{1,0:T(8,128)S(1)} %get-tuple-element.58), channel_id=1, source_target_pairs={{0,0},{7,7},{1,2},{2,1},{3,4},{4,3},{5,6},{6,5},{8,8},{15,15},{9,1... | collective-permute-start | bytes 12296 | tf_op jit(solution)/shard_map/ppermute | solution.py:616
  25.6 1.3 %collective-permute-done.2 = f32[8,128]{1,0:T(8,128)S(1)} collective-permute-done((f32[8,128]{1,0:T(8,128)S(1)}, f32[8,128]{1,0:T(8,128)S(1)}, u32[]{:S(2)}, u32[]{:S(2)}) %collective-permute-start.2) | collective-permute-done | bytes 4128 | tf_op jit(solution)/shard_map/ppermute | solution.py:617
  26.9 0.0 collective-permute-done.3
  26.9 9.8 %all-to-all-done = f32[32,26,1,128]{3,2,1,0:T(1,128)S(1)} async-done(((f32[32,26,1,128]{3,2,1,0:T(1,128)}), f32[32,26,1,128]{3,2,1,0:T(1,128)S(1)}, u32[]{:S(2)}, u32[]{:S(2)}) %all-to-all-start) | async-done | bytes 426016 | tf_op jit(solution)/shard_map/all_to_all | solution.py:751
  36.7 4.9 %apply.1 = (f32[32,512]{1,0:T(8,128)S(1)}, f32[8,640]{1,0:T(8,128)S(1)}, f32[8,640]{1,0:T(8,128)S(1)}, f32[5,32,128]{2,1,0:T(8,128)S(1)}) custom-call(f32[832,128]{1,0:T(8,128)S(1)} %bitcast.33, f32[5,32,512]{2,1,0:T(8,128)S(1)} %get-tuple-element.42.refs_1_, f32[8,128]{1,0:T(8,128)S(1)} %get-tuple-element.57.refs_2_, f32[8,128]{1,0:T(8,128)S(1)} %get-tuple-element.56.refs_3_), custom_call_target="tpu_custom_call" | custom-call | tf_op jit(solution)/shard_map/apply/pallas_call | solution.py:767
  41.6 0.1 collective-permute-start.4
  41.7 0.6 %collective-permute-start.5 = (f32[8,640]{1,0:T(8,128)S(1)}, f32[8,640]{1,0:T(8,128)S(1)}, u32[]{:S(2)}, u32[]{:S(2)}) collective-permute-start(f32[8,640]{1,0:T(8,128)S(1)} %get-tuple-element.54), channel_id=1, source_target_pairs={{8,16},{16,8},{24,0},{0,24},{9,17},{17,9},{25,1},{1,25},{10,18},{1... | collective-permute-start | bytes 61448 | tf_op jit(solution)/shard_map/ppermute | solution.py:616
  42.3 0.1 pad_add_fusion.refs_0_
  42.4 0.5 collective-permute-done.4
  42.9 2.1 %collective-permute-done.5 = f32[8,640]{1,0:T(8,128)S(1)} collective-permute-done((f32[8,640]{1,0:T(8,128)S(1)}, f32[8,640]{1,0:T(8,128)S(1)}, u32[]{:S(2)}, u32[]{:S(2)}) %collective-permute-start.5) | collective-permute-done | bytes 20512 | tf_op jit(solution)/shard_map/ppermute | solution.py:616
  45.0 1.7 %flood.1 = (f32[32,512]{1,0:T(8,128)}, f32[32,512]{1,0:T(8,128)}, f32[32,512]{1,0:T(8,128)}) custom-call(s32[4]{0:T(128)S(1)} %pad_add_fusion.refs_0_, f32[5,32,512]{2,1,0:T(8,128)S(1)} %get-tuple-element.42.refs_1_, f32[32,512]{1,0:T(8,128)S(1)} %get-tuple-element.45.refs_2_, f32[5,32,128]{2,1,0:T(8,128)S(1)} %get-tuple-element.46.refs_3_, ...), custom_call_target="tpu_custom_call" | custom-call | tf_op jit(solution)/shard_map/flood/pallas_call | solution.py:785
  (19 shorter events, 0.1 us)
Async XLA Ops:
  0.6 3.1 %copy-start.11 = (s32[1,1,16,1024,1]{3,4,2,1,0:T(1,128)S(1)}, s32[1,1,16,1024,1]{3,4,2,1,0:T(1,128)}, u32[]{:S(2)}) copy-start(s32[1,1,16,1024,1]{3,4,2,1,0:T(1,128)} %param.20) | copy-start | bytes 196612
  3.2 2.4 %collective-permute-start = (f32[20,8,128]{2,1,0:T(8,128)}, f32[20,8,128]{2,1,0:T(8,128)S(1)}, u32[]{:S(2)}, u32[]{:S(2)}) collective-permute-start(f32[20,8,128]{2,1,0:T(8,128)} %get-tuple-element.28.own_ref), channel_id=1, source_target_pairs={{0,8},{8,0},{16,24},{24,16},{1,9},{9,1},{17,25},{25,17},{2,10},{10... | collective-permute-start | bytes 245768 | tf_op jit(solution)/shard_map/ppermute | solution.py:606
  3.7 1.9 %copy-start.1 = (f32[20,8,128]{2,1,0:T(8,128)S(1)}, f32[20,8,128]{2,1,0:T(8,128)}, u32[]{:S(2)}) copy-start(f32[20,8,128]{2,1,0:T(8,128)} %get-tuple-element.28.own_ref) | copy-start | bytes 245764
  5.6 3.3 %copy-start.9 = (s32[16,1024]{1,0:T(8,128)S(1)}, s32[16,1024]{1,0:T(8,128)}, u32[]{:S(2)}) copy-start(s32[16,1024]{1,0:T(8,128)} %get-tuple-element.36.refs_1_.refs_11_) | copy-start | bytes 196612
  5.6 3.3 %copy-start.10 = (s32[16,1024]{1,0:T(8,128)S(1)}, s32[16,1024]{1,0:T(8,128)}, u32[]{:S(2)}) copy-start(s32[16,1024]{1,0:T(8,128)} %get-tuple-element.37.refs_2_.refs_12_) | copy-start | bytes 196612
  6.3 5.2 %collective-permute-start.1 = (f32[6,8,128]{2,1,0:T(8,128)S(1)}, f32[6,8,128]{2,1,0:T(8,128)S(1)}, u32[]{:S(2)}, u32[]{:S(2)}) collective-permute-start(f32[6,8,128]{2,1,0:T(8,128)S(1)} %get-tuple-element.29.refs_3_.refs_1_), channel_id=1, source_target_pairs={{0,16},{8,24},{16,0},{24,8},{1,17},{9,25},{17,1},{25,9},{2,18},{10... | collective-permute-start | bytes 73736 | tf_op jit(solution)/shard_map/ppermute | solution.py:606
  8.9 2.6 %copy-start = (f32[16,10,8,128]{3,2,1,0:T(8,128)S(1)}, f32[16,10,8,128]{3,2,1,0:T(8,128)}, u32[]{:S(2)}) copy-start(f32[16,10,8,128]{3,2,1,0:T(8,128)} %get-tuple-element.31.refs_4_) | copy-start | bytes 1966084
  8.9 2.7 %copy-start.7 = (f32[16,1024]{1,0:T(8,128)S(1)}, f32[16,1024]{1,0:T(8,128)}, u32[]{:S(2)}) copy-start(f32[16,1024]{1,0:T(8,128)} %get-tuple-element.38.refs_9_) | copy-start | bytes 196612
  8.9 2.7 %copy-start.8 = (s32[16,1024]{1,0:T(8,128)S(1)}, s32[16,1024]{1,0:T(8,128)}, u32[]{:S(2)}) copy-start(s32[16,1024]{1,0:T(8,128)} %get-tuple-element.39.refs_10_) | copy-start | bytes 196612
  16.9 5.6 %copy-start.2 = (f32[32,512]{1,0:T(8,128)S(1)}, f32[32,512]{1,0:T(8,128)}, u32[]{:S(2)}) copy-start(f32[32,512]{1,0:T(8,128)} %refs_0_.1) | copy-start | bytes 196612
  16.9 5.6 %copy-start.3 = (f32[32,512]{1,0:T(8,128)S(1)}, f32[32,512]{1,0:T(8,128)}, u32[]{:S(2)}) copy-start(f32[32,512]{1,0:T(8,128)} %refs_1_.1) | copy-start | bytes 196612
  16.9 5.6 %copy-start.4 = (f32[32,512]{1,0:T(8,128)S(1)}, f32[32,512]{1,0:T(8,128)}, u32[]{:S(2)}) copy-start(f32[32,512]{1,0:T(8,128)} %refs_2_.1) | copy-start | bytes 196612
  16.9 5.6 %copy-start.5 = (f32[32,512]{1,0:T(8,128)S(1)}, f32[32,512]{1,0:T(8,128)}, u32[]{:S(2)}) copy-start(f32[32,512]{1,0:T(8,128)} %refs_3_.1) | copy-start | bytes 196612
  16.9 5.6 %copy-start.6 = (s32[32,512]{1,0:T(8,128)S(1)}, s32[32,512]{1,0:T(8,128)}, u32[]{:S(2)}) copy-start(s32[32,512]{1,0:T(8,128)} %refs_4_.3) | copy-start | bytes 196612
  16.9 19.8 %all-to-all-start = ((f32[32,26,1,128]{3,2,1,0:T(1,128)}), f32[32,26,1,128]{3,2,1,0:T(1,128)S(1)}, u32[]{:S(2)}, u32[]{:S(2)}) async-start(f32[32,26,1,128]{3,2,1,0:T(1,128)} %bitcast.21), calls=%async_computation | async-start | bytes 851968 | tf_op jit(solution)/shard_map/all_to_all | solution.py:751
  23.1 3.8 %collective-permute-start.2 = (f32[8,128]{1,0:T(8,128)S(1)}, f32[8,128]{1,0:T(8,128)S(1)}, u32[]{:S(2)}, u32[]{:S(2)}) collective-permute-start(f32[8,128]{1,0:T(8,128)S(1)} %get-tuple-element.59), channel_id=1, source_target_pairs={{0,1},{1,0},{2,3},{3,2},{4,5},{5,4},{6,7},{7,6},{8,9},{9,8},{10,11... | collective-permute-start | bytes 12296 | tf_op jit(solution)/shard_map/ppermute | solution.py:617
  24.9 1.9 %collective-permute-start.3 = (f32[8,128]{1,0:T(8,128)S(1)}, f32[8,128]{1,0:T(8,128)S(1)}, u32[]{:S(2)}, u32[]{:S(2)}) collective-permute-start(f32[8,128]{1,0:T(8,128)S(1)} %get-tuple-element.58), channel_id=1, source_target_pairs={{0,0},{7,7},{1,2},{2,1},{3,4},{4,3},{5,6},{6,5},{8,8},{15,15},{9,1... | collective-permute-start | bytes 12296 | tf_op jit(solution)/shard_map/ppermute | solution.py:616
  41.6 1.3 %collective-permute-start.4 = (f32[8,640]{1,0:T(8,128)S(1)}, f32[8,640]{1,0:T(8,128)S(1)}, u32[]{:S(2)}, u32[]{:S(2)}) collective-permute-start(f32[8,640]{1,0:T(8,128)S(1)} %get-tuple-element.55), channel_id=1, source_target_pairs={{0,8},{8,0},{16,24},{24,16},{1,9},{9,1},{17,25},{25,17},{2,10},{10... | collective-permute-start | bytes 61448 | tf_op jit(solution)/shard_map/ppermute | solution.py:617
  41.7 3.3 %collective-permute-start.5 = (f32[8,640]{1,0:T(8,128)S(1)}, f32[8,640]{1,0:T(8,128)S(1)}, u32[]{:S(2)}, u32[]{:S(2)}) collective-permute-start(f32[8,640]{1,0:T(8,128)S(1)} %get-tuple-element.54), channel_id=1, source_target_pairs={{8,16},{16,8},{24,0},{0,24},{9,17},{17,9},{25,1},{1,25},{10,18},{1... | collective-permute-start | bytes 61448 | tf_op jit(solution)/shard_map/ppermute | solution.py:616

commit v4 on v3

--- a/solution.py
+++ b/solution.py
@@ -26,8 +26,9 @@
 VMEM = pl.BlockSpec(memory_space=pltpu.VMEM)
 SMEM = pl.BlockSpec(memory_space=pltpu.SMEM)
 ANY = pl.BlockSpec(memory_space=pl.ANY)
+HBM = pl.BlockSpec(memory_space=pltpu.HBM)
+WIDE = pltpu.CompilerParams(vmem_limit_bytes=60 * 2**20)
 PARAMS = pltpu.CompilerParams(vmem_limit_bytes=40 * 2**20)
-WIDE = pltpu.CompilerParams(vmem_limit_bytes=60 * 2**20)
 
 
 def start_copies(sources, targets, sems):
@@ -196,9 +197,9 @@
     return inverse, mat_vec(inverse, add(head_y, mat_vec(head_left, tail_y)))
 
 
-def merge_kernel(step, first, position_ref, own_ref, other_ref, *refs):
+def merge_kernel(step, first, last, position_ref, own_ref, other_ref, *refs):
     known_ref = None if first else refs[0]
-    group_ref, map_ref, send_ref = refs[-3:]
+    out_ref, map_ref = refs[-2:]
     position = position_ref[0]
     late = ((position >> step) & 1) == 1
 
@@ -245,10 +246,12 @@
                     pick(late, add(value, mat_vec(by_before, tail)), add(value, mat_vec(by_after, head))),
                 ]
             )
-    store_all(group_ref, joined)
     store_all(map_ref, maps[0] + maps[1])
-    later = ((position >> (step + 1)) & 1) == 1
-    store_all(send_ref, [pick(later, joined[0], joined[1]), pick(later, joined[2], joined[5])])
+    if last:
+        later = ((position >> (step + 1)) & 1) == 1
+        store_all(out_ref, [pick(later, joined[0], joined[1]), pick(later, joined[2], joined[5])])
+    else:
+        store_all(out_ref, joined)
 
 
 def rows16(row):
@@ -376,7 +379,7 @@
         out_ref[...] += product(left, right)
         return carry
 
-    lax.fori_loop(0, groups, body, 0, unroll=8)
+    lax.fori_loop(0, groups, body, 0, unroll=16)
 
 
 def weir_kernel(sections, steps, tiles, capacity, row_count, col_count, *refs):
@@ -505,7 +508,7 @@
         total_ref[...] += product(left, right)
         return carry
 
-    lax.fori_loop(0, sources // step, body, 0, unroll=16)
+    lax.fori_loop(0, sources // step, body, 0, unroll=32)
     for n in range(col_count // LOW):
         def summed(v):
             start = 2 * v * high_count + n * row_count
@@ -658,16 +661,15 @@
     blocks = sections // BLOCK
     steps = row_size.bit_length() - 1
     weir_shape = (sections, chains)
-    whole = jax.ShapeDtypeStruct(weir_shape, jnp.int32)
     solved, packed, crest, regime, weir_rows, weir_cols = pl.pallas_call(
         functools.partial(solve_kernel, sections),
         out_shape=(
-            jax.ShapeDtypeStruct((sections, 10, lane_rows, LANES), F32),
-            jax.ShapeDtypeStruct((20, lane_rows, LANES), F32),
-            jax.ShapeDtypeStruct(weir_shape, F32),
-            whole,
-            whole,
-            whole,
+            pltpu.VMEM((sections, 10, lane_rows, LANES), F32),
+            pltpu.VMEM((20, lane_rows, LANES), F32),
+            pltpu.VMEM(weir_shape, F32),
+            pltpu.VMEM(weir_shape, jnp.int32),
+            pltpu.VMEM(weir_shape, jnp.int32),
+            pltpu.VMEM(weir_shape, jnp.int32),
         ),
         in_specs=[ANY] * 8,
         out_specs=(VMEM,) * 6,
@@ -708,16 +710,18 @@
     group, known = packed, ()
     for step in range(steps - 1):
         other = exchanged(group, "row", step)
+        last = step == steps - 2
         twenty = jax.ShapeDtypeStruct((20, lane_rows, LANES), F32)
-        group, own_map, sent = pl.pallas_call(
-            functools.partial(merge_kernel, step, step == 0),
-            out_shape=(twenty, twenty, jax.ShapeDtypeStruct((6, lane_rows, LANES), F32)),
+        group, own_map = pl.pallas_call(
+            functools.partial(merge_kernel, step, step == 0, last),
+            out_shape=(jax.ShapeDtypeStruct((6, lane_rows, LANES), F32) if last else twenty, twenty),
             in_specs=[SMEM] + [VMEM] * (2 + len(known)),
-            out_specs=(VMEM, VMEM, VMEM),
+            out_specs=(VMEM, VMEM),
             compiler_params=PARAMS,
             name="merge",
         )(row_at.reshape(1), group, other, *known)
         known = (own_map,)
+    sent = group
     met = exchanged(sent, "row", steps - 1)
     cells = pl.pallas_call(
         functools.partial(cell_kernel, tiles, capacity, rows // 8, row_count),
@@ -759,7 +763,7 @@
         scratch_shapes=[pltpu.VMEM((row_count, col_count), jnp.int32), pltpu.SemaphoreType.DMA((5,))],
         compiler_params=PARAMS,
         name="stage",
-    )(water_depth, bed_level, flux_first, flux_second, wet_mask, outgoing)
+    )(water_depth, bed_level, flux_first, flux_second, wet_mask, state_rows)
     before, after = swapped(left, right, "col", False)
     tile_out = jax.ShapeDtypeStruct((row_count, col_count), F32)
     edge = jax.ShapeDtypeStruct((8, col_count + LANES), F32)

time: 47 us -> 45.1 us (0.960)
  Pallas kernels: 20.2 us -> 18.1 us
    pallas_call x2, Pallas kernels: 3.2 us -> 1.63 us  [the longest x1 1.59 us: local(): pl.pallas_call(functools.partial(solve_kernel, sections), out_shape=(pltp...]
where the time goes in v4:
time: 45.1 us; the launch traced here: 44.8 us
  Pallas kernels  18.1 us (40%)
  waiting for transfers between devices  13.6 us (30%)
  starting transfers between devices  12.1 us (27%)
  between operations  0.89 us (2%)
    all_to_all x1, waiting for transfers between devices, local(): lax.all_to_all(messages, ('row', 'col'), split_axis=0, concat_axis=0, til...  9.78 us
    all_to_all x1, starting transfers between devices, local(): lax.all_to_all(messages, ('row', 'col'), split_axis=0, concat_axis=0, til...  5.77 us
    pallas_call x1, Pallas kernels, local(): pl.pallas_call(functools.partial(weir_kernel, sections, steps, tiles, cap...  5.38 us
    pallas_call x1, Pallas kernels, local(): pl.pallas_call(functools.partial(apply_kernel, tiles, rows_each, row_coun...  4.54 us
    ppermute x2, starting transfers between devices, exchanged(): lax.ppermute(block, axis, [(i, i ^ 1 << step) for i in range(lax.axis_siz...  3.13 us
    pallas_call x1, Pallas kernels, local(): pl.pallas_call(functools.partial(cell_kernel, tiles, capacity, rows // 8,...  2.36 us
    ppermute x2, waiting for transfers between devices, swapped(): two = lax.ppermute(jnp.where(odd, last, first), axis, outer)  2.1 us
    ppermute x2, starting transfers between devices, swapped(): one = lax.ppermute(jnp.where(odd, first, last), axis, inner)  1.9 us
  transfers between devices with their start and end apart: 7, of which 4 were waited for; matrix products, arithmetic and copies ran while one was open for 0% of the time, Pallas kernels for 11%

profile of v4, /device:TPU:0, one launch (start us, length us, event | category | flops | bytes accessed | tf_op | source)
XLA Modules:
  0.0 44.8 jit_solution(17519765122386606916)
XLA Ops:
  0.6 0.0 copy-start.6
  0.6 1.6 %solve.1 = (f32[16,10,8,128]{3,2,1,0:T(8,128)S(1)}, f32[20,8,128]{2,1,0:T(8,128)S(1)}, f32[16,1024]{1,0:T(8,128)S(1)}, s32[16,1024]{1,0:T(8,128)S(1)}, s32[16,1024]{1,0:T(8,128)S(1)}, /*index=5*/s32[16,1024]{1,0:T(8,128)S(1)}) custom-call(f32[512,128]{1,0:T(8,128)} %bitcast.36, f32[512,128]{1,0:T(8,128)} %bitcast.37, f32[512,128]{1,0:T(8,128)} %bitcast.38, ...), custom_call_target="tpu_custom_call" | custom-call | tf_op jit(solution)/shard_map/solve/pallas_call | solution.py:664
  2.2 0.5 %collective-permute-start = (f32[20,8,128]{2,1,0:T(8,128)S(1)}, f32[20,8,128]{2,1,0:T(8,128)S(1)}, u32[]{:S(2)}, u32[]{:S(2)}) collective-permute-start(f32[20,8,128]{2,1,0:T(8,128)S(1)} %get-tuple-element.28.own_ref), channel_id=1, source_target_pairs={{0,8},{8,0},{16,24},{24,16},{1,9},{9,1},{17,25},{25,17},{2,10},{10... | collective-permute-start | bytes 245768 | tf_op jit(solution)/shard_map/ppermute | solution.py:609
  2.8 0.0 copy-done.6
  2.8 1.9 %rank.1 = (s32[128,128]{1,0:T(8,128)S(1)}, f32[8,32,128]{2,1,0:T(8,128)S(1)}, s32[1]{0:T(128)}, s32[128,128]{1,0:T(8,128)S(1)}) custom-call(s32[128,128]{1,0:T(8,128)S(1)} %bitcast.35), custom_call_target="tpu_custom_call" | custom-call | flops 268435456 | bytes 131072 | tf_op jit(solution)/shard_map/rank/pallas_call | solution.py:696
  4.7 0.0 collective-permute-done.other_ref
  4.7 2.6 %collective-permute-start.1 = (f32[6,8,128]{2,1,0:T(8,128)S(1)}, f32[6,8,128]{2,1,0:T(8,128)S(1)}, u32[]{:S(2)}, u32[]{:S(2)}) collective-permute-start(f32[6,8,128]{2,1,0:T(8,128)S(1)} %get-tuple-element.29.refs_3_.refs_1_), channel_id=1, source_target_pairs={{0,16},{8,24},{16,0},{24,8},{1,17},{9,25},{17,1},{25,9},{2,18},{10... | collective-permute-start | bytes 73736 | tf_op jit(solution)/shard_map/ppermute | solution.py:609
  7.3 2.4 %cells.1.refs_8_ = f32[256,256]{1,0:T(8,128)S(1)} custom-call(s32[128,128]{1,0:T(8,128)S(1)} %get-tuple-element.35.refs_0_, s32[16,1024]{1,0:T(8,128)S(1)} %get-tuple-element.36.refs_1_.refs_11_, s32[16,1024]{1,0:T(8,128)S(1)} %get-tuple-element.37.refs_2_.refs_12_, f32[6,8,128]{2,1,0:T(8,128)S(1)} %get-tuple-element.29.refs_3_.refs_1_), custom_call_target="tpu_custom_call" | custom-call | flops 2147483648 | bytes 262144 | tf_op jit(solution)/shard_map/cells/pallas_call | solution.py:726
  9.7 0.0 collective-permute-done.1.refs_2_
  9.7 5.4 %weirs.1 = (f32[256,128]{1,0:T(8,128)}, f32[832,128]{1,0:T(8,128)}) custom-call(s32[1]{0:T(128)} %bitcast.position_ref.refs_0_, f32[6,8,128]{2,1,0:T(8,128)S(1)} %get-tuple-element.29.refs_3_.refs_1_, f32[6,8,128]{2,1,0:T(8,128)S(1)} %collective-permute-done.1.refs_2_, f32[20,8,128]{2,1,0:T(8,128)S(1)} %get-tuple-element.30.refs_3_, ...), custom_call_target="tpu_custom_call" | custom-call | tf_op jit(solution)/shard_map/weirs/pallas_call | solution.py:736
  15.1 0.0 copy-start
  15.1 0.0 copy-start.1
  15.1 0.0 copy-start.2
  15.1 0.0 copy-start.3
  15.2 0.0 copy-start.4
  15.2 0.0 copy-start.5
  15.2 5.8 %all-to-all-start = ((f32[32,26,1,128]{3,2,1,0:T(1,128)}), f32[32,26,1,128]{3,2,1,0:T(1,128)S(1)}, u32[]{:S(2)}, u32[]{:S(2)}) async-start(f32[32,26,1,128]{3,2,1,0:T(1,128)} %bitcast.21), calls=%async_computation | async-start | bytes 851968 | tf_op jit(solution)/shard_map/all_to_all | solution.py:755
  21.0 0.0 copy-done
  21.0 0.0 copy-done.1
  21.0 0.6 %stage.1 = (f32[5,32,512]{2,1,0:T(8,128)S(1)}, f32[8,128]{1,0:T(8,128)S(1)}, f32[8,128]{1,0:T(8,128)S(1)}) custom-call(f32[32,512]{1,0:T(8,128)S(1)} %copy-done.1, f32[32,512]{1,0:T(8,128)S(1)} %copy-done.2, f32[32,512]{1,0:T(8,128)S(1)} %copy-done.3, f32[32,512]{1,0:T(8,128)S(1)} %copy-done.4, s32[32,512]{1,0:T(8,128)S(1)} %copy-done.5, f32[256,128]{1,0:T(8,128)S(1)} %copy-done), custom_call_target="tpu_custom_call" | custom-call | tf_op jit(solution)/shard_map/stage/pallas_call | solution.py:758
  21.6 1.8 %collective-permute-start.2 = (f32[8,128]{1,0:T(8,128)S(1)}, f32[8,128]{1,0:T(8,128)S(1)}, u32[]{:S(2)}, u32[]{:S(2)}) collective-permute-start(f32[8,128]{1,0:T(8,128)S(1)} %get-tuple-element.59), channel_id=1, source_target_pairs={{0,1},{1,0},{2,3},{3,2},{4,5},{5,4},{6,7},{7,6},{8,9},{9,8},{10,11... | collective-permute-start | bytes 12296 | tf_op jit(solution)/shard_map/ppermute | solution.py:620
  23.5 0.6 %collective-permute-start.3 = (f32[8,128]{1,0:T(8,128)S(1)}, f32[8,128]{1,0:T(8,128)S(1)}, u32[]{:S(2)}, u32[]{:S(2)}) collective-permute-start(f32[8,128]{1,0:T(8,128)S(1)} %get-tuple-element.58), channel_id=1, source_target_pairs={{0,0},{7,7},{1,2},{2,1},{3,4},{4,3},{5,6},{6,5},{8,8},{15,15},{9,1... | collective-permute-start | bytes 12296 | tf_op jit(solution)/shard_map/ppermute | solution.py:619
  24.2 1.3 %collective-permute-done.2 = f32[8,128]{1,0:T(8,128)S(1)} collective-permute-done((f32[8,128]{1,0:T(8,128)S(1)}, f32[8,128]{1,0:T(8,128)S(1)}, u32[]{:S(2)}, u32[]{:S(2)}) %collective-permute-start.2) | collective-permute-done | bytes 4128 | tf_op jit(solution)/shard_map/ppermute | solution.py:620
  25.4 0.0 collective-permute-done.3
  25.4 9.8 %all-to-all-done = f32[32,26,1,128]{3,2,1,0:T(1,128)S(1)} async-done(((f32[32,26,1,128]{3,2,1,0:T(1,128)}), f32[32,26,1,128]{3,2,1,0:T(1,128)S(1)}, u32[]{:S(2)}, u32[]{:S(2)}) %all-to-all-start) | async-done | bytes 426016 | tf_op jit(solution)/shard_map/all_to_all | solution.py:755
  35.2 4.5 %apply.1 = (f32[32,512]{1,0:T(8,128)S(1)}, f32[8,640]{1,0:T(8,128)S(1)}, f32[8,640]{1,0:T(8,128)S(1)}, f32[5,32,128]{2,1,0:T(8,128)S(1)}) custom-call(f32[832,128]{1,0:T(8,128)S(1)} %bitcast.33, f32[5,32,512]{2,1,0:T(8,128)S(1)} %get-tuple-element.41.refs_1_, f32[8,128]{1,0:T(8,128)S(1)} %get-tuple-element.57.refs_2_, f32[8,128]{1,0:T(8,128)S(1)} %get-tuple-element.56.refs_3_), custom_call_target="tpu_custom_call" | custom-call | tf_op jit(solution)/shard_map/apply/pallas_call | solution.py:771
  39.8 0.1 collective-permute-start.4
  39.8 0.6 %collective-permute-start.5 = (f32[8,640]{1,0:T(8,128)S(1)}, f32[8,640]{1,0:T(8,128)S(1)}, u32[]{:S(2)}, u32[]{:S(2)}) collective-permute-start(f32[8,640]{1,0:T(8,128)S(1)} %get-tuple-element.54), channel_id=1, source_target_pairs={{8,16},{16,8},{24,0},{0,24},{9,17},{17,9},{25,1},{1,25},{10,18},{1... | collective-permute-start | bytes 61448 | tf_op jit(solution)/shard_map/ppermute | solution.py:619
  40.5 0.1 pad_add_fusion.refs_0_
  40.6 0.5 %collective-permute-done.4 = f32[8,640]{1,0:T(8,128)S(1)} collective-permute-done((f32[8,640]{1,0:T(8,128)S(1)}, f32[8,640]{1,0:T(8,128)S(1)}, u32[]{:S(2)}, u32[]{:S(2)}) %collective-permute-start.4) | collective-permute-done | bytes 20512 | tf_op jit(solution)/shard_map/ppermute | solution.py:620
  41.0 2.1 %collective-permute-done.5 = f32[8,640]{1,0:T(8,128)S(1)} collective-permute-done((f32[8,640]{1,0:T(8,128)S(1)}, f32[8,640]{1,0:T(8,128)S(1)}, u32[]{:S(2)}, u32[]{:S(2)}) %collective-permute-start.5) | collective-permute-done | bytes 20512 | tf_op jit(solution)/shard_map/ppermute | solution.py:619
  43.1 1.7 %flood.1 = (f32[32,512]{1,0:T(8,128)}, f32[32,512]{1,0:T(8,128)}, f32[32,512]{1,0:T(8,128)}) custom-call(s32[4]{0:T(128)S(1)} %pad_add_fusion.refs_0_, f32[5,32,512]{2,1,0:T(8,128)S(1)} %get-tuple-element.41.refs_1_, f32[32,512]{1,0:T(8,128)S(1)} %get-tuple-element.45.refs_2_, f32[5,32,128]{2,1,0:T(8,128)S(1)} %get-tuple-element.46.refs_3_, ...), custom_call_target="tpu_custom_call" | custom-call | tf_op jit(solution)/shard_map/flood/pallas_call | solution.py:789
  (9 shorter events, 0.1 us)
Async XLA Ops:
  0.6 2.1 %copy-start.6 = (s32[1,1,16,1024,1]{3,4,2,1,0:T(1,128)S(1)}, s32[1,1,16,1024,1]{3,4,2,1,0:T(1,128)}, u32[]{:S(2)}) copy-start(s32[1,1,16,1024,1]{3,4,2,1,0:T(1,128)} %param.20) | copy-start | bytes 196612
  2.2 2.4 %collective-permute-start = (f32[20,8,128]{2,1,0:T(8,128)S(1)}, f32[20,8,128]{2,1,0:T(8,128)S(1)}, u32[]{:S(2)}, u32[]{:S(2)}) collective-permute-start(f32[20,8,128]{2,1,0:T(8,128)S(1)} %get-tuple-element.28.own_ref), channel_id=1, source_target_pairs={{0,8},{8,0},{16,24},{24,16},{1,9},{9,1},{17,25},{25,17},{2,10},{10... | collective-permute-start | bytes 245768 | tf_op jit(solution)/shard_map/ppermute | solution.py:609
  4.7 5.0 %collective-permute-start.1 = (f32[6,8,128]{2,1,0:T(8,128)S(1)}, f32[6,8,128]{2,1,0:T(8,128)S(1)}, u32[]{:S(2)}, u32[]{:S(2)}) collective-permute-start(f32[6,8,128]{2,1,0:T(8,128)S(1)} %get-tuple-element.29.refs_3_.refs_1_), channel_id=1, source_target_pairs={{0,16},{8,24},{16,0},{24,8},{1,17},{9,25},{17,1},{25,9},{2,18},{10... | collective-permute-start | bytes 73736 | tf_op jit(solution)/shard_map/ppermute | solution.py:609
  15.1 5.9 %copy-start = (f32[256,128]{1,0:T(8,128)S(1)}, f32[256,128]{1,0:T(8,128)}, u32[]{:S(2)}) copy-start(f32[256,128]{1,0:T(8,128)} %get-tuple-element.40.refs_5_) | copy-start | bytes 393220
  15.1 5.9 %copy-start.1 = (f32[32,512]{1,0:T(8,128)S(1)}, f32[32,512]{1,0:T(8,128)}, u32[]{:S(2)}) copy-start(f32[32,512]{1,0:T(8,128)} %refs_0_.1) | copy-start | bytes 196612
  15.1 5.9 %copy-start.2 = (f32[32,512]{1,0:T(8,128)S(1)}, f32[32,512]{1,0:T(8,128)}, u32[]{:S(2)}) copy-start(f32[32,512]{1,0:T(8,128)} %refs_1_.1) | copy-start | bytes 196612
  15.1 5.9 %copy-start.3 = (f32[32,512]{1,0:T(8,128)S(1)}, f32[32,512]{1,0:T(8,128)}, u32[]{:S(2)}) copy-start(f32[32,512]{1,0:T(8,128)} %refs_2_.1) | copy-start | bytes 196612
  15.2 5.9 %copy-start.4 = (f32[32,512]{1,0:T(8,128)S(1)}, f32[32,512]{1,0:T(8,128)}, u32[]{:S(2)}) copy-start(f32[32,512]{1,0:T(8,128)} %refs_3_.1) | copy-start | bytes 196612
  15.2 5.9 %copy-start.5 = (s32[32,512]{1,0:T(8,128)S(1)}, s32[32,512]{1,0:T(8,128)}, u32[]{:S(2)}) copy-start(s32[32,512]{1,0:T(8,128)} %refs_4_.3) | copy-start | bytes 196612
  15.2 20.0 %all-to-all-start = ((f32[32,26,1,128]{3,2,1,0:T(1,128)}), f32[32,26,1,128]{3,2,1,0:T(1,128)S(1)}, u32[]{:S(2)}, u32[]{:S(2)}) async-start(f32[32,26,1,128]{3,2,1,0:T(1,128)} %bitcast.21), calls=%async_computation | async-start | bytes 851968 | tf_op jit(solution)/shard_map/all_to_all | solution.py:755
  21.6 3.8 %collective-permute-start.2 = (f32[8,128]{1,0:T(8,128)S(1)}, f32[8,128]{1,0:T(8,128)S(1)}, u32[]{:S(2)}, u32[]{:S(2)}) collective-permute-start(f32[8,128]{1,0:T(8,128)S(1)} %get-tuple-element.59), channel_id=1, source_target_pairs={{0,1},{1,0},{2,3},{3,2},{4,5},{5,4},{6,7},{7,6},{8,9},{9,8},{10,11... | collective-permute-start | bytes 12296 | tf_op jit(solution)/shard_map/ppermute | solution.py:620
  23.5 1.9 %collective-permute-start.3 = (f32[8,128]{1,0:T(8,128)S(1)}, f32[8,128]{1,0:T(8,128)S(1)}, u32[]{:S(2)}, u32[]{:S(2)}) collective-permute-start(f32[8,128]{1,0:T(8,128)S(1)} %get-tuple-element.58), channel_id=1, source_target_pairs={{0,0},{7,7},{1,2},{2,1},{3,4},{4,3},{5,6},{6,5},{8,8},{15,15},{9,1... | collective-permute-start | bytes 12296 | tf_op jit(solution)/shard_map/ppermute | solution.py:619
  39.8 1.3 %collective-permute-start.4 = (f32[8,640]{1,0:T(8,128)S(1)}, f32[8,640]{1,0:T(8,128)S(1)}, u32[]{:S(2)}, u32[]{:S(2)}) collective-permute-start(f32[8,640]{1,0:T(8,128)S(1)} %get-tuple-element.55), channel_id=1, source_target_pairs={{0,8},{8,0},{16,24},{24,16},{1,9},{9,1},{17,25},{25,17},{2,10},{10... | collective-permute-start | bytes 61448 | tf_op jit(solution)/shard_map/ppermute | solution.py:620
  39.8 3.3 %collective-permute-start.5 = (f32[8,640]{1,0:T(8,128)S(1)}, f32[8,640]{1,0:T(8,128)S(1)}, u32[]{:S(2)}, u32[]{:S(2)}) collective-permute-start(f32[8,640]{1,0:T(8,128)S(1)} %get-tuple-element.54), channel_id=1, source_target_pairs={{8,16},{16,8},{24,0},{0,24},{9,17},{17,9},{25,1},{1,25},{10,18},{1... | collective-permute-start | bytes 61448 | tf_op jit(solution)/shard_map/ppermute | solution.py:619

commit v5 on v4

--- a/solution.py
+++ b/solution.py
@@ -59,7 +59,7 @@
     return [[m[1][1] * scale, -m[0][1] * scale], [-m[1][0] * scale, m[0][0] * scale]]
 
 
-def rank_kernel(tiles, capacity, blocks, tile_ref, slot_ref, base_ref, flag_ref, whole_ref):
+def rank_kernel(tiles, capacity, blocks, tile_ref, slot_ref, base_ref, flag_ref):
     table = lax.broadcasted_iota(jnp.int32, (tiles, LANES), 0)
     first_slot = table.astype(F32) * capacity
     row_at = lax.broadcasted_iota(jnp.int32, (LANES, 2 * LANES), 0)
@@ -67,33 +67,26 @@
     earlier = jnp.where(row_at < col_at, 1.0, 0.0).astype(BF16)
 
     def body(b, carry):
-        rank, most = carry
-        base = jnp.floor(rank * (1.0 / LOW))
+        offset, most = carry
+        base = jnp.floor((offset - first_slot) * (1.0 / LOW))
         base_ref[b] = base
-        offset = first_slot + (rank - base * LOW)
-        start = offset
         for n in range(BLOCK):
             g = b * BLOCK + n
             ids = tile_ref[pl.ds((g // 8) * 64 + g % 8, 8, stride=8), :]
             hits = [ids[r : r + 1, :] == table for r in range(8)]
             hot = jnp.concatenate([jnp.where(h, 1.0, 0.0).astype(BF16) for h in hits], 0)
             counts = jnp.dot(hot, earlier, preferred_element_type=F32)
-            rows, bases = [], []
+            rows = []
             for r in range(8):
                 part = counts[r * tiles : (r + 1) * tiles]
                 place = jnp.where(hits[r], part[:, :LANES] + offset, 0.0)
                 rows.append(jnp.sum(place, axis=0, keepdims=True))
-                bases.append(jnp.sum(jnp.where(hits[r], base * LOW, 0.0), axis=0, keepdims=True))
                 offset = offset + part[:, LANES:]
-            slots = jnp.concatenate(rows, 0)
-            at = pl.ds(pl.multiple_of(g * 8, 8), 8)
-            slot_ref[at, :] = slots.astype(jnp.int32)
-            whole_ref[at, :] = (slots + jnp.concatenate(bases, 0)).astype(jnp.int32)
-        last = jnp.floor((offset - first_slot - 1.0) * (1.0 / LOW))
-        return rank + (offset - start), jnp.maximum(most, last)
-
-    nothing = jnp.zeros((tiles, LANES), F32)
-    most = lax.fori_loop(0, blocks, body, (nothing, nothing), unroll=8)[1]
+            slot_ref[pl.ds(pl.multiple_of(g * 8, 8), 8), :] = jnp.concatenate(rows, 0).astype(jnp.int32)
+        last = jnp.floor((offset - first_slot - 1.0) * (1.0 / LOW)) - base
+        return offset, jnp.maximum(most, last)
+
+    most = lax.fori_loop(0, blocks, body, (first_slot, jnp.zeros((tiles, LANES), F32)), unroll=8)[1]
     flag_ref[0] = jnp.max(most).astype(jnp.int32)
 
 
@@ -295,65 +288,74 @@
     return (pl.ds(over, 8), pl.ds(along, LANES))
 
 
-def fill_slots(tiles, capacity, start, stop, most, slot_ref, base_ref, flag_ref, values, total_ref, side=None):
+def fill_slots(tiles, capacity, blocks, slot_ref, base_ref, flag_ref, values, total_ref, side_code, side_ref):
     windows = capacity // LOW
-    taken = min(most, windows)
-    window_table = table16(taken * tiles)
+    taken = min(2, windows)
     low_table = table16(LOW)
-    if side is not None:
-        side_code, side_ref = side
-        tile_table = table16(tiles)
-        side_table = table16(LANES)
-        side_ref[...] = jnp.zeros_like(side_ref)
-
-    def block_values(b):
-        groups = [values(b * BLOCK + n) for n in range(BLOCK)]
-        return [jnp.concatenate([g[v] for g in groups], 0) for v in range(len(groups[0]))]
-
-    def add_block(b, first, with_side):
+    side_table = table16(LANES)
+    first_window = lax.broadcasted_iota(jnp.int32, (tiles, LANES), 0).astype(F32) * windows
+    one = jnp.ones((), BF16)
+    zero = jnp.zeros((), BF16)
+    total_ref[...] = jnp.zeros_like(total_ref)
+    side_ref[...] = jnp.zeros_like(side_ref)
+
+    def add_block(b, first):
         rows = pl.ds(pl.multiple_of(b * (8 * BLOCK), 8 * BLOCK), 8 * BLOCK)
         slot = slot_ref[rows, :]
-        value = block_values(b)
-        tile = slot // capacity
-        window = slot % capacity // LOW - first
-        code = jnp.where((window >= 0) & (window < taken), window * tiles + tile, -1)
-        left, right = one_hots(code.astype(F32), (slot % LOW).astype(F32), value, window_table, low_table)
-        found = product(left, right)
+        window = (slot // LOW).astype(F32)
+        low = (slot % LOW).astype(F32)
+        place = jnp.concatenate([side_code(b * BLOCK + n) for n in range(BLOCK)], 0).astype(F32)
+        groups = [values(b * BLOCK + n) for n in range(BLOCK)]
+        value = [jnp.concatenate([g[v] for g in groups], 0) for v in range(len(groups[0]))]
         base = base_ref[b] + first
+        covered = [jnp.where(base + i < windows, first_window + (base + i), -1.0) for i in range(taken)]
+        window_table = jnp.concatenate(covered, 0).astype(BF16).reshape(taken * tiles // 16, 16, LANES)
+        left, right, side_left, side_right = [], [], [], []
+        for r in range(8 * BLOCK):
+            hit = window_table == rows16(window[r : r + 1])[None]
+            parts = [jnp.where(hit, rows16(v[r : r + 1])[None], zero).reshape(-1, LANES) for v in value]
+            left.append(jnp.concatenate(parts, 0))
+            if taken == 2:
+                parts = [p[:tiles] + p[tiles:] for p in parts]
+            side_left.append(jnp.concatenate(parts, 0))
+            hit = low_table == rows16(low[r : r + 1])[None]
+            right.append(jnp.where(hit, one, zero).reshape(-1, LANES))
+            hit = side_table == rows16(place[r : r + 1])[None]
+            side_right.append(jnp.where(hit, one, zero).reshape(-1, LANES))
+        found = product(jnp.concatenate(left, 1), jnp.concatenate(right, 1))
         base = jnp.concatenate([base, base], 1)
-        for v in range(len(value)):
-            parts = [found[(v * taken + i) * tiles : (v * taken + i + 1) * tiles] for i in range(taken)]
+        for v in range(len(value) // 2):
+            parts = []
+            for i in range(taken):
+                high, rest = (((2 * v + n) * taken + i) * tiles for n in range(2))
+                parts.append(found[high : high + tiles] + found[rest : rest + tiles])
             for q in range(windows):
                 put = jnp.where(base == q, parts[0], 0.0)
                 for i in range(1, taken):
                     put = jnp.where(base == q - i, parts[i], put)
                 total_ref[pl.ds((v * windows + q) * tiles, tiles), :] += put
-        if with_side:
-            code = jnp.concatenate([side_code(b * BLOCK + n) for n in range(BLOCK)], 0)
-            left, right = one_hots(tile.astype(F32), code.astype(F32), value, tile_table, side_table)
-            side_ref[...] += product(left, right)
+        side_ref[...] += product(jnp.concatenate(side_left, 1), jnp.concatenate(side_right, 1))
 
     def body(b, carry):
-        add_block(b, 0, side is not None)
+        add_block(b, 0)
         return carry
 
-    lax.fori_loop(start, stop, body, 0, unroll=4)
+    lax.fori_loop(0, blocks, body, 0, unroll=4)
     for first in range(taken, windows, taken):
 
         @pl.when(flag_ref[0] >= first)
         def _(first=first):
             def rest(b, carry):
-                add_block(b, first, False)
+                add_block(b, first)
                 return carry
 
-            lax.fori_loop(start, stop, rest, 0)
-
-
-def store_slots(tiles, capacity, total_ref, part, scale, out_ref, pitch, row):
+            lax.fori_loop(0, blocks, rest, 0)
+
+
+def store_slots(tiles, capacity, window_of, out_ref, pitch, row):
     windows = capacity // LOW
     for q in range(windows):
-        first = total_ref[pl.ds((part * windows + q) * tiles, tiles), :]
-        value = first * scale + total_ref[pl.ds(((part + 1) * windows + q) * tiles, tiles), :]
+        value = window_of(q)
         for j in range(LOW // LANES):
             at = pl.ds(row + j * windows + q, tiles, stride=pitch)
             out_ref[at, :] = value[:, j * LANES : (j + 1) * LANES]
@@ -437,19 +439,22 @@
         place = jnp.where(col < 2, col, jnp.where(col >= col_count - 2, col - (col_count - 4), -1))
         return jnp.where(place >= 0, place * row_count + row_ref[group_at(g)], -1)
 
-    total_ref[...] = jnp.zeros_like(total_ref)
-    side = (side_code, side_ref)
-    fill_slots(tiles, capacity, 0, sections // BLOCK, 2, slot_ref, base_ref, flag_ref, values, total_ref, side)
+    blocks = sections // BLOCK
+    fill_slots(tiles, capacity, blocks, slot_ref, base_ref, flag_ref, values, total_ref, side_code, side_ref)
+    windows = capacity // LOW
     rows_each = capacity // LANES
     pitch = 3 * rows_each + 2
     at = lax.broadcasted_iota(jnp.int32, (tiles, LANES), 1)
     first_cols = at < 2 * row_count
     for v in range(2):
-        store_slots(tiles, capacity, total_ref, 2 * v, 1.0, out_ref, pitch, v * rows_each)
+        window_of = lambda q: total_ref[pl.ds((v * windows + q) * tiles, tiles), :]
+        store_slots(tiles, capacity, window_of, out_ref, pitch, v * rows_each)
         sums = side_ref[pl.ds(2 * v * tiles, tiles), :] + side_ref[pl.ds((2 * v + 1) * tiles, tiles), :]
         beside = jnp.where(first_cols, pltpu.roll(sums, tiles - 1, 0), pltpu.roll(sums, 1, 0))
         out_ref[pl.ds(3 * rows_each + v, tiles, stride=pitch), :] = beside
-    store_slots(tiles, capacity, cells_ref, 0, float(LOW), out_ref, pitch, 2 * rows_each)
+    cell_part = lambda n, q: cells_ref[pl.ds((n * windows + q) * tiles, tiles), :]
+    window_of = lambda q: cell_part(0, q) * float(LOW) + cell_part(1, q)
+    store_slots(tiles, capacity, window_of, out_ref, pitch, 2 * rows_each)
     state_copy.wait()
 
 
@@ -693,16 +698,15 @@
         weir_row,
         weir_col,
     )
-    *places, whole_slots = pl.pallas_call(
+    places = pl.pallas_call(
         functools.partial(rank_kernel, tiles, capacity, blocks),
         out_shape=(
             jax.ShapeDtypeStruct((rows, LANES), jnp.int32),
             jax.ShapeDtypeStruct((blocks, tiles, LANES), F32),
             jax.ShapeDtypeStruct((1,), jnp.int32),
-            jax.ShapeDtypeStruct((rows, LANES), jnp.int32),
         ),
         in_specs=[VMEM],
-        out_specs=(VMEM, VMEM, SMEM, VMEM),
+        out_specs=(VMEM, VMEM, SMEM),
         compiler_params=PARAMS,
         cost_estimate=pl.CostEstimate(flops=2 * tiles * weirs * LOW, bytes_accessed=2**17, transcendentals=0),
         name="rank",
@@ -731,7 +735,7 @@
         compiler_params=PARAMS,
         cost_estimate=pl.CostEstimate(flops=4 * high_count * LOW * weirs, bytes_accessed=2**18, transcendentals=0),
         name="cells",
-    )(whole_slots, weir_rows, weir_cols, sent)
+    )(places[0], weir_rows, weir_cols, sent)
     state_shape = jax.ShapeDtypeStruct((sections * lane_rows * 2, LANES), F32)
     state_rows, outgoing = pl.pallas_call(
         functools.partial(weir_kernel, sections, steps, tiles, capacity, row_count, col_count),
@@ -741,7 +745,7 @@
         scratch_shapes=[
             pltpu.VMEM(state_shape.shape, F32),
             pltpu.VMEM((rows, LANES), F32),
-            pltpu.VMEM((4 * high_count, LOW), F32),
+            pltpu.VMEM((2 * high_count, LOW), F32),
             pltpu.VMEM((4 * tiles, LANES), F32),
             pltpu.SemaphoreType.DMA((1,)),
         ],

time: 45.1 us -> 44.6 us (0.989)
  Pallas kernels: 18.1 us -> 17.6 us
  transfers between devices with their start and end apart: 7 -> 7, of which waited for: 4 -> 4; matrix products, arithmetic and copies ran while one was open for 0% -> 0% of each run, Pallas kernels for 11% -> 10%
where the time goes in v5:
time: 44.6 us; the launch traced here: 44.3 us
  Pallas kernels  17.6 us (39%)
  waiting for transfers between devices  13.6 us (30%)
  starting transfers between devices  12.1 us (27%)
  between operations  0.89 us (2%)
    all_to_all x1, waiting for transfers between devices, local(): lax.all_to_all(messages, ('row', 'col'), split_axis=0, concat_axis=0, til...  9.78 us
    all_to_all x1, starting transfers between devices, local(): lax.all_to_all(messages, ('row', 'col'), split_axis=0, concat_axis=0, til...  5.77 us
    pallas_call x1, Pallas kernels, local(): pl.pallas_call(functools.partial(weir_kernel, sections, steps, tiles, cap...  5.28 us
    pallas_call x1, Pallas kernels, local(): pl.pallas_call(functools.partial(apply_kernel, tiles, rows_each, row_coun...  4.54 us
    ppermute x2, starting transfers between devices, exchanged(): lax.ppermute(block, axis, [(i, i ^ 1 << step) for i in range(lax.axis_siz...  3.13 us
    pallas_call x1, Pallas kernels, local(): pl.pallas_call(functools.partial(cell_kernel, tiles, capacity, rows // 8,...  2.37 us
    ppermute x2, waiting for transfers between devices, swapped(): two = lax.ppermute(jnp.where(odd, last, first), axis, outer)  2.1 us
    ppermute x2, starting transfers between devices, swapped(): one = lax.ppermute(jnp.where(odd, first, last), axis, inner)  1.9 us
  transfers between devices with their start and end apart: 7, of which 4 were waited for; matrix products, arithmetic and copies ran while one was open for 0% of the time, Pallas kernels for 10%

profile of v5, /device:TPU:0, one launch (start us, length us, event | category | flops | bytes accessed | tf_op | source)
XLA Modules:
  0.0 44.3 jit_solution(15573916423666423566)
XLA Ops:
  0.6 0.0 copy-start.6
  0.6 1.6 %solve.1 = (f32[16,10,8,128]{3,2,1,0:T(8,128)S(1)}, f32[20,8,128]{2,1,0:T(8,128)S(1)}, f32[16,1024]{1,0:T(8,128)S(1)}, s32[16,1024]{1,0:T(8,128)S(1)}, s32[16,1024]{1,0:T(8,128)S(1)}, /*index=5*/s32[16,1024]{1,0:T(8,128)S(1)}) custom-call(f32[512,128]{1,0:T(8,128)} %bitcast.36, f32[512,128]{1,0:T(8,128)} %bitcast.37, f32[512,128]{1,0:T(8,128)} %bitcast.38, ...), custom_call_target="tpu_custom_call" | custom-call | tf_op jit(solution)/shard_map/solve/pallas_call | solution.py:669
  2.2 0.5 %collective-permute-start = (f32[20,8,128]{2,1,0:T(8,128)S(1)}, f32[20,8,128]{2,1,0:T(8,128)S(1)}, u32[]{:S(2)}, u32[]{:S(2)}) collective-permute-start(f32[20,8,128]{2,1,0:T(8,128)S(1)} %get-tuple-element.27.own_ref), channel_id=1, source_target_pairs={{0,8},{8,0},{16,24},{24,16},{1,9},{9,1},{17,25},{25,17},{2,10},{10... | collective-permute-start | bytes 245768 | tf_op jit(solution)/shard_map/ppermute | solution.py:614
  2.8 0.0 copy-done.6
  2.8 1.5 %rank.1 = (s32[128,128]{1,0:T(8,128)S(1)}, f32[8,32,128]{2,1,0:T(8,128)S(1)}, s32[1]{0:T(128)}) custom-call(s32[128,128]{1,0:T(8,128)S(1)} %bitcast.35), custom_call_target="tpu_custom_call" | custom-call | flops 268435456 | bytes 131072 | tf_op jit(solution)/shard_map/rank/pallas_call | solution.py:701
  4.3 0.0 collective-permute-done.other_ref
  4.3 2.6 %collective-permute-start.1 = (f32[6,8,128]{2,1,0:T(8,128)S(1)}, f32[6,8,128]{2,1,0:T(8,128)S(1)}, u32[]{:S(2)}, u32[]{:S(2)}) collective-permute-start(f32[6,8,128]{2,1,0:T(8,128)S(1)} %get-tuple-element.28.refs_3_.refs_1_), channel_id=1, source_target_pairs={{0,16},{8,24},{16,0},{24,8},{1,17},{9,25},{17,1},{25,9},{2,18},{10... | collective-permute-start | bytes 73736 | tf_op jit(solution)/shard_map/ppermute | solution.py:614
  6.9 2.4 %cells.1.refs_8_ = f32[256,256]{1,0:T(8,128)S(1)} custom-call(s32[128,128]{1,0:T(8,128)S(1)} %get-tuple-element.31.refs_0_.refs_5_, s32[16,1024]{1,0:T(8,128)S(1)} %get-tuple-element.34.refs_1_.refs_11_, s32[16,1024]{1,0:T(8,128)S(1)} %get-tuple-element.35.refs_2_.refs_12_, f32[6,8,128]{2,1,0:T(8,128)S(1)} %get-tuple-element.28.refs_3_.refs_1_), custom_call_target="tpu_custom_call" | custom-call | flops 2147483648 | bytes 262144 | tf_op jit(solution)/shard_map/cells/pallas_call | solution.py:730
  9.3 0.0 collective-permute-done.1.refs_2_
  9.3 5.3 %weirs.1 = (f32[256,128]{1,0:T(8,128)}, f32[832,128]{1,0:T(8,128)}) custom-call(s32[1]{0:T(128)} %bitcast.position_ref.refs_0_, f32[6,8,128]{2,1,0:T(8,128)S(1)} %get-tuple-element.28.refs_3_.refs_1_, f32[6,8,128]{2,1,0:T(8,128)S(1)} %collective-permute-done.1.refs_2_, f32[20,8,128]{2,1,0:T(8,128)S(1)} %get-tuple-element.29.refs_3_, ...), custom_call_target="tpu_custom_call" | custom-call | tf_op jit(solution)/shard_map/weirs/pallas_call | solution.py:740
  14.6 0.0 copy-start
  14.6 0.0 copy-start.1
  14.6 0.0 copy-start.2
  14.6 0.0 copy-start.3
  14.7 0.0 copy-start.4
  14.7 0.0 copy-start.5
  14.7 5.8 %all-to-all-start = ((f32[32,26,1,128]{3,2,1,0:T(1,128)}), f32[32,26,1,128]{3,2,1,0:T(1,128)S(1)}, u32[]{:S(2)}, u32[]{:S(2)}) async-start(f32[32,26,1,128]{3,2,1,0:T(1,128)} %bitcast.21), calls=%async_computation | async-start | bytes 851968 | tf_op jit(solution)/shard_map/all_to_all | solution.py:759
  20.5 0.0 copy-done
  20.5 0.0 copy-done.1
  20.5 0.6 %stage.1 = (f32[5,32,512]{2,1,0:T(8,128)S(1)}, f32[8,128]{1,0:T(8,128)S(1)}, f32[8,128]{1,0:T(8,128)S(1)}) custom-call(f32[32,512]{1,0:T(8,128)S(1)} %copy-done.1, f32[32,512]{1,0:T(8,128)S(1)} %copy-done.2, f32[32,512]{1,0:T(8,128)S(1)} %copy-done.3, f32[32,512]{1,0:T(8,128)S(1)} %copy-done.4, s32[32,512]{1,0:T(8,128)S(1)} %copy-done.5, f32[256,128]{1,0:T(8,128)S(1)} %copy-done), custom_call_target="tpu_custom_call" | custom-call | tf_op jit(solution)/shard_map/stage/pallas_call | solution.py:762
  21.1 1.8 %collective-permute-start.2 = (f32[8,128]{1,0:T(8,128)S(1)}, f32[8,128]{1,0:T(8,128)S(1)}, u32[]{:S(2)}, u32[]{:S(2)}) collective-permute-start(f32[8,128]{1,0:T(8,128)S(1)} %get-tuple-element.57), channel_id=1, source_target_pairs={{0,1},{1,0},{2,3},{3,2},{4,5},{5,4},{6,7},{7,6},{8,9},{9,8},{10,11... | collective-permute-start | bytes 12296 | tf_op jit(solution)/shard_map/ppermute | solution.py:625
  23.0 0.6 %collective-permute-start.3 = (f32[8,128]{1,0:T(8,128)S(1)}, f32[8,128]{1,0:T(8,128)S(1)}, u32[]{:S(2)}, u32[]{:S(2)}) collective-permute-start(f32[8,128]{1,0:T(8,128)S(1)} %get-tuple-element.56), channel_id=1, source_target_pairs={{0,0},{7,7},{1,2},{2,1},{3,4},{4,3},{5,6},{6,5},{8,8},{15,15},{9,1... | collective-permute-start | bytes 12296 | tf_op jit(solution)/shard_map/ppermute | solution.py:624
  23.7 1.3 %collective-permute-done.2 = f32[8,128]{1,0:T(8,128)S(1)} collective-permute-done((f32[8,128]{1,0:T(8,128)S(1)}, f32[8,128]{1,0:T(8,128)S(1)}, u32[]{:S(2)}, u32[]{:S(2)}) %collective-permute-start.2) | collective-permute-done | bytes 4128 | tf_op jit(solution)/shard_map/ppermute | solution.py:625
  24.9 0.0 collective-permute-done.3
  24.9 9.8 %all-to-all-done = f32[32,26,1,128]{3,2,1,0:T(1,128)S(1)} async-done(((f32[32,26,1,128]{3,2,1,0:T(1,128)}), f32[32,26,1,128]{3,2,1,0:T(1,128)S(1)}, u32[]{:S(2)}, u32[]{:S(2)}) %all-to-all-start) | async-done | bytes 426016 | tf_op jit(solution)/shard_map/all_to_all | solution.py:759
  34.7 4.5 %apply.1 = (f32[32,512]{1,0:T(8,128)S(1)}, f32[8,640]{1,0:T(8,128)S(1)}, f32[8,640]{1,0:T(8,128)S(1)}, f32[5,32,128]{2,1,0:T(8,128)S(1)}) custom-call(f32[832,128]{1,0:T(8,128)S(1)} %bitcast.33, f32[5,32,512]{2,1,0:T(8,128)S(1)} %get-tuple-element.39.refs_1_, f32[8,128]{1,0:T(8,128)S(1)} %get-tuple-element.55.refs_2_, f32[8,128]{1,0:T(8,128)S(1)} %get-tuple-element.54.refs_3_), custom_call_target="tpu_custom_call" | custom-call | tf_op jit(solution)/shard_map/apply/pallas_call | solution.py:775
  39.3 0.1 collective-permute-start.4
  39.3 0.6 %collective-permute-start.5 = (f32[8,640]{1,0:T(8,128)S(1)}, f32[8,640]{1,0:T(8,128)S(1)}, u32[]{:S(2)}, u32[]{:S(2)}) collective-permute-start(f32[8,640]{1,0:T(8,128)S(1)} %get-tuple-element.52), channel_id=1, source_target_pairs={{8,16},{16,8},{24,0},{0,24},{9,17},{17,9},{25,1},{1,25},{10,18},{1... | collective-permute-start | bytes 61448 | tf_op jit(solution)/shard_map/ppermute | solution.py:624
  40.0 0.1 pad_add_fusion.refs_0_
  40.1 0.5 %collective-permute-done.4 = f32[8,640]{1,0:T(8,128)S(1)} collective-permute-done((f32[8,640]{1,0:T(8,128)S(1)}, f32[8,640]{1,0:T(8,128)S(1)}, u32[]{:S(2)}, u32[]{:S(2)}) %collective-permute-start.4) | collective-permute-done | bytes 20512 | tf_op jit(solution)/shard_map/ppermute | solution.py:625
  40.5 2.1 %collective-permute-done.5 = f32[8,640]{1,0:T(8,128)S(1)} collective-permute-done((f32[8,640]{1,0:T(8,128)S(1)}, f32[8,640]{1,0:T(8,128)S(1)}, u32[]{:S(2)}, u32[]{:S(2)}) %collective-permute-start.5) | collective-permute-done | bytes 20512 | tf_op jit(solution)/shard_map/ppermute | solution.py:624
  42.6 1.7 %flood.1 = (f32[32,512]{1,0:T(8,128)}, f32[32,512]{1,0:T(8,128)}, f32[32,512]{1,0:T(8,128)}) custom-call(s32[4]{0:T(128)S(1)} %pad_add_fusion.refs_0_, f32[5,32,512]{2,1,0:T(8,128)S(1)} %get-tuple-element.39.refs_1_, f32[32,512]{1,0:T(8,128)S(1)} %get-tuple-element.43.refs_2_, f32[5,32,128]{2,1,0:T(8,128)S(1)} %get-tuple-element.44.refs_3_, ...), custom_call_target="tpu_custom_call" | custom-call | tf_op jit(solution)/shard_map/flood/pallas_call | solution.py:793
  (9 shorter events, 0.1 us)
Async XLA Ops:
  0.6 2.1 %copy-start.6 = (s32[1,1,16,1024,1]{3,4,2,1,0:T(1,128)S(1)}, s32[1,1,16,1024,1]{3,4,2,1,0:T(1,128)}, u32[]{:S(2)}) copy-start(s32[1,1,16,1024,1]{3,4,2,1,0:T(1,128)} %param.20) | copy-start | bytes 196612
  2.2 2.0 %collective-permute-start = (f32[20,8,128]{2,1,0:T(8,128)S(1)}, f32[20,8,128]{2,1,0:T(8,128)S(1)}, u32[]{:S(2)}, u32[]{:S(2)}) collective-permute-start(f32[20,8,128]{2,1,0:T(8,128)S(1)} %get-tuple-element.27.own_ref), channel_id=1, source_target_pairs={{0,8},{8,0},{16,24},{24,16},{1,9},{9,1},{17,25},{25,17},{2,10},{10... | collective-permute-start | bytes 245768 | tf_op jit(solution)/shard_map/ppermute | solution.py:614
  4.3 5.0 %collective-permute-start.1 = (f32[6,8,128]{2,1,0:T(8,128)S(1)}, f32[6,8,128]{2,1,0:T(8,128)S(1)}, u32[]{:S(2)}, u32[]{:S(2)}) collective-permute-start(f32[6,8,128]{2,1,0:T(8,128)S(1)} %get-tuple-element.28.refs_3_.refs_1_), channel_id=1, source_target_pairs={{0,16},{8,24},{16,0},{24,8},{1,17},{9,25},{17,1},{25,9},{2,18},{10... | collective-permute-start | bytes 73736 | tf_op jit(solution)/shard_map/ppermute | solution.py:614
  14.6 5.9 %copy-start = (f32[256,128]{1,0:T(8,128)S(1)}, f32[256,128]{1,0:T(8,128)}, u32[]{:S(2)}) copy-start(f32[256,128]{1,0:T(8,128)} %get-tuple-element.38.refs_5_) | copy-start | bytes 393220
  14.6 5.9 %copy-start.1 = (f32[32,512]{1,0:T(8,128)S(1)}, f32[32,512]{1,0:T(8,128)}, u32[]{:S(2)}) copy-start(f32[32,512]{1,0:T(8,128)} %refs_0_.1) | copy-start | bytes 196612
  14.6 5.9 %copy-start.2 = (f32[32,512]{1,0:T(8,128)S(1)}, f32[32,512]{1,0:T(8,128)}, u32[]{:S(2)}) copy-start(f32[32,512]{1,0:T(8,128)} %refs_1_.1) | copy-start | bytes 196612
  14.6 5.9 %copy-start.3 = (f32[32,512]{1,0:T(8,128)S(1)}, f32[32,512]{1,0:T(8,128)}, u32[]{:S(2)}) copy-start(f32[32,512]{1,0:T(8,128)} %refs_2_.1) | copy-start | bytes 196612
  14.7 5.9 %copy-start.4 = (f32[32,512]{1,0:T(8,128)S(1)}, f32[32,512]{1,0:T(8,128)}, u32[]{:S(2)}) copy-start(f32[32,512]{1,0:T(8,128)} %refs_3_.1) | copy-start | bytes 196612
  14.7 5.9 %copy-start.5 = (s32[32,512]{1,0:T(8,128)S(1)}, s32[32,512]{1,0:T(8,128)}, u32[]{:S(2)}) copy-start(s32[32,512]{1,0:T(8,128)} %refs_4_.3) | copy-start | bytes 196612
  14.7 20.0 %all-to-all-start = ((f32[32,26,1,128]{3,2,1,0:T(1,128)}), f32[32,26,1,128]{3,2,1,0:T(1,128)S(1)}, u32[]{:S(2)}, u32[]{:S(2)}) async-start(f32[32,26,1,128]{3,2,1,0:T(1,128)} %bitcast.21), calls=%async_computation | async-start | bytes 851968 | tf_op jit(solution)/shard_map/all_to_all | solution.py:759
  21.1 3.8 %collective-permute-start.2 = (f32[8,128]{1,0:T(8,128)S(1)}, f32[8,128]{1,0:T(8,128)S(1)}, u32[]{:S(2)}, u32[]{:S(2)}) collective-permute-start(f32[8,128]{1,0:T(8,128)S(1)} %get-tuple-element.57), channel_id=1, source_target_pairs={{0,1},{1,0},{2,3},{3,2},{4,5},{5,4},{6,7},{7,6},{8,9},{9,8},{10,11... | collective-permute-start | bytes 12296 | tf_op jit(solution)/shard_map/ppermute | solution.py:625
  23.0 1.9 %collective-permute-start.3 = (f32[8,128]{1,0:T(8,128)S(1)}, f32[8,128]{1,0:T(8,128)S(1)}, u32[]{:S(2)}, u32[]{:S(2)}) collective-permute-start(f32[8,128]{1,0:T(8,128)S(1)} %get-tuple-element.56), channel_id=1, source_target_pairs={{0,0},{7,7},{1,2},{2,1},{3,4},{4,3},{5,6},{6,5},{8,8},{15,15},{9,1... | collective-permute-start | bytes 12296 | tf_op jit(solution)/shard_map/ppermute | solution.py:624
  39.3 1.3 %collective-permute-start.4 = (f32[8,640]{1,0:T(8,128)S(1)}, f32[8,640]{1,0:T(8,128)S(1)}, u32[]{:S(2)}, u32[]{:S(2)}) collective-permute-start(f32[8,640]{1,0:T(8,128)S(1)} %get-tuple-element.53), channel_id=1, source_target_pairs={{0,8},{8,0},{16,24},{24,16},{1,9},{9,1},{17,25},{25,17},{2,10},{10... | collective-permute-start | bytes 61448 | tf_op jit(solution)/shard_map/ppermute | solution.py:625
  39.3 3.3 %collective-permute-start.5 = (f32[8,640]{1,0:T(8,128)S(1)}, f32[8,640]{1,0:T(8,128)S(1)}, u32[]{:S(2)}, u32[]{:S(2)}) collective-permute-start(f32[8,640]{1,0:T(8,128)S(1)} %get-tuple-element.52), channel_id=1, source_target_pairs={{8,16},{16,8},{24,0},{0,24},{9,17},{17,9},{25,1},{1,25},{10,18},{1... | collective-permute-start | bytes 61448 | tf_op jit(solution)/shard_map/ppermute | solution.py:624

commit v6 on v5

--- a/solution.py
+++ b/solution.py
@@ -91,15 +91,13 @@
 
 
 def solve_kernel(sections, *refs):
-    inputs, later = refs[:4], refs[4:8]
-    solved_ref, packed_ref = refs[8:10]
-    fetched = refs[10:14]
-    lower_ref, main_ref, upper_ref, rhs_ref, sems, later_sems = refs[14:]
+    inputs = refs[:4]
+    solved_ref, packed_ref = refs[4:6]
+    lower_ref, main_ref, upper_ref, rhs_ref, sems = refs[6:]
     pieces = []
     for n in range(4):
-        parts = [[r.at[pl.ds(n * r.shape[0] // 4, r.shape[0] // 4)] for r in group] for group in (inputs, refs[14:18])]
+        parts = [[r.at[pl.ds(n * r.shape[0] // 4, r.shape[0] // 4)] for r in group] for group in (inputs, refs[6:10])]
         pieces.append(start_copies(*parts, sems.at[n]))
-    copies = start_copies(later, fetched, later_sems)
 
     def block(ref, k):
         return [[ref[pl.ds(k * 32 + i * 16 + j, 8, stride=2), :] for j in range(2)] for i in range(2)]
@@ -152,8 +150,6 @@
             packed_ref[8 + 2 * i + j] = tail[1][i][j]
             packed_ref[12 + 2 * i + j] = spike[i][j]
             packed_ref[16 + 2 * i + j] = tail[2][i][j]
-    for copy in copies:
-        copy.wait()
 
 
 def load_pair(ref, n):
@@ -352,12 +348,12 @@
             lax.fori_loop(0, blocks, rest, 0)
 
 
-def store_slots(tiles, capacity, window_of, out_ref, pitch, row):
+def store_slots(capacity, first, count, window_of, out_ref, pitch, row):
     windows = capacity // LOW
     for q in range(windows):
         value = window_of(q)
         for j in range(LOW // LANES):
-            at = pl.ds(row + j * windows + q, tiles, stride=pitch)
+            at = pl.ds(first * pitch + row + j * windows + q, count, stride=pitch)
             out_ref[at, :] = value[:, j * LANES : (j + 1) * LANES]
 
 
@@ -388,7 +384,7 @@
     position_ref, own_ref, other_ref, map_ref = refs[:4]
     solved_ref, slot_ref, base_ref, flag_ref, cells_ref = refs[4:9]
     crest_ref, regime_ref, row_ref, col_ref = refs[9:13]
-    state_out, out_ref, state_ref, phase_ref, total_ref, side_ref, sems = refs[13:]
+    state_out, out_ref, state_ref, phase_ref, total_ref, side_ref, message_ref, sems = refs[13:]
     late = ((position_ref[0] >> (steps - 1)) & 1) == 1
     own = [load_pair(own_ref, 0), load_square(own_ref, 2)]
     other = [load_pair(other_ref, 0), load_square(other_ref, 2)]
@@ -446,15 +442,26 @@
     pitch = 3 * rows_each + 2
     at = lax.broadcasted_iota(jnp.int32, (tiles, LANES), 1)
     first_cols = at < 2 * row_count
+    beside = []
     for v in range(2):
-        window_of = lambda q: total_ref[pl.ds((v * windows + q) * tiles, tiles), :]
-        store_slots(tiles, capacity, window_of, out_ref, pitch, v * rows_each)
         sums = side_ref[pl.ds(2 * v * tiles, tiles), :] + side_ref[pl.ds((2 * v + 1) * tiles, tiles), :]
-        beside = jnp.where(first_cols, pltpu.roll(sums, tiles - 1, 0), pltpu.roll(sums, 1, 0))
-        out_ref[pl.ds(3 * rows_each + v, tiles, stride=pitch), :] = beside
-    cell_part = lambda n, q: cells_ref[pl.ds((n * windows + q) * tiles, tiles), :]
-    window_of = lambda q: cell_part(0, q) * float(LOW) + cell_part(1, q)
-    store_slots(tiles, capacity, window_of, out_ref, pitch, 2 * rows_each)
+        beside.append(jnp.where(first_cols, pltpu.roll(sums, tiles - 1, 0), pltpu.roll(sums, 1, 0)))
+    count = tiles // 4
+    copies = []
+    for first in range(0, tiles, count):
+        for v in range(2):
+            window_of = lambda q: total_ref[pl.ds((v * windows + q) * tiles + first, count), :]
+            store_slots(capacity, first, count, window_of, message_ref, pitch, v * rows_each)
+            at = pl.ds(first * pitch + 3 * rows_each + v, count, stride=pitch)
+            message_ref[at, :] = beside[v][first : first + count]
+        cell_part = lambda n, q: cells_ref[pl.ds((n * windows + q) * tiles + first, count), :]
+        window_of = lambda q: cell_part(0, q) * float(LOW) + cell_part(1, q)
+        store_slots(capacity, first, count, window_of, message_ref, pitch, 2 * rows_each)
+        rows = pl.ds(first * pitch, count * pitch)
+        copies.append(pltpu.make_async_copy(message_ref.at[rows], out_ref.at[rows], sems.at[1 + len(copies)]))
+        copies[-1].start()
+    for copy in copies:
+        copy.wait()
     state_copy.wait()
 
 
@@ -665,26 +672,20 @@
     river_block = pltpu.VMEM((sections * 4 * lane_rows, LANES), F32)
     blocks = sections // BLOCK
     steps = row_size.bit_length() - 1
-    weir_shape = (sections, chains)
-    solved, packed, crest, regime, weir_rows, weir_cols = pl.pallas_call(
+    solved, packed = pl.pallas_call(
         functools.partial(solve_kernel, sections),
         out_shape=(
             pltpu.VMEM((sections, 10, lane_rows, LANES), F32),
             pltpu.VMEM((20, lane_rows, LANES), F32),
-            pltpu.VMEM(weir_shape, F32),
-            pltpu.VMEM(weir_shape, jnp.int32),
-            pltpu.VMEM(weir_shape, jnp.int32),
-            pltpu.VMEM(weir_shape, jnp.int32),
         ),
-        in_specs=[ANY] * 8,
-        out_specs=(VMEM,) * 6,
+        in_specs=[ANY] * 4,
+        out_specs=(VMEM,) * 2,
         scratch_shapes=[
             river_block,
             river_block,
             river_block,
             pltpu.VMEM((sections * 2 * lane_rows, LANES), F32),
             pltpu.SemaphoreType.DMA((4, 4)),
-            pltpu.SemaphoreType.DMA((4,)),
         ],
         compiler_params=WIDE,
         name="solve",
@@ -693,10 +694,6 @@
         block_rows(river_main),
         block_rows(river_upper),
         rhs_rows,
-        weir_crest,
-        weir_regime,
-        weir_row,
-        weir_col,
     )
     places = pl.pallas_call(
         functools.partial(rank_kernel, tiles, capacity, blocks),
@@ -735,23 +732,24 @@
         compiler_params=PARAMS,
         cost_estimate=pl.CostEstimate(flops=4 * high_count * LOW * weirs, bytes_accessed=2**18, transcendentals=0),
         name="cells",
-    )(places[0], weir_rows, weir_cols, sent)
+    )(places[0], weir_row, weir_col, sent)
     state_shape = jax.ShapeDtypeStruct((sections * lane_rows * 2, LANES), F32)
     state_rows, outgoing = pl.pallas_call(
         functools.partial(weir_kernel, sections, steps, tiles, capacity, row_count, col_count),
         out_shape=(state_shape, jax.ShapeDtypeStruct((tiles * pitch, LANES), F32)),
         in_specs=[SMEM] + [VMEM] * 5 + [VMEM, SMEM] + [VMEM] * 5,
-        out_specs=(ANY, VMEM),
+        out_specs=(ANY, ANY),
         scratch_shapes=[
             pltpu.VMEM(state_shape.shape, F32),
             pltpu.VMEM((rows, LANES), F32),
             pltpu.VMEM((2 * high_count, LOW), F32),
             pltpu.VMEM((4 * tiles, LANES), F32),
-            pltpu.SemaphoreType.DMA((1,)),
+            pltpu.VMEM((tiles * pitch, LANES), F32),
+            pltpu.SemaphoreType.DMA((5,)),
         ],
         compiler_params=PARAMS,
         name="weirs",
-    )(row_at.reshape(1), sent, met, own_map, solved, *places, cells, crest, regime, weir_rows, weir_cols)
+    )(row_at.reshape(1), sent, met, own_map, solved, *places, cells, weir_crest, weir_regime, weir_row, weir_col)
     river_state = (
         state_rows.reshape(sections, lane_rows, 2, LANES).transpose(0, 2, 1, 3).reshape(sections, 2, chains)
     )

time: 44.6 us -> 44.6 us (level)
  waiting for transfers between devices: 13.6 us -> 10.8 us
  starting transfers between devices: 12.1 us -> 14.8 us
    all_to_all x1, waiting for transfers between devices: 9.78 us -> 6.72 us  [local(): lax.all_to_all(messages, ('row', 'col'), split_axis=0, concat_axis=0, til...]
    ppermute x2, starting transfers between devices: 1.9 us -> 4.73 us  [swapped(): one = lax.ppermute(jnp.where(odd, first, last), axis, inner)]
  transfers between devices with their start and end apart: 7 -> 7, of which waited for: 4 -> 3; matrix products, arithmetic and copies ran while one was open for 0% -> 0% of each run, Pallas kernels for 10% -> 10%
where the time goes in v6:
time: 44.6 us; the launch traced here: 44.3 us
  Pallas kernels  17.6 us (39%)
  starting transfers between devices  14.8 us (33%)
  waiting for transfers between devices  10.8 us (24%)
  between operations  0.89 us (2%)
    all_to_all x1, waiting for transfers between devices, local(): lax.all_to_all(messages, ('row', 'col'), split_axis=0, concat_axis=0, til...  6.72 us
    all_to_all x1, starting transfers between devices, local(): lax.all_to_all(messages, ('row', 'col'), split_axis=0, concat_axis=0, til...  5.74 us
    pallas_call x1, Pallas kernels, local(): pl.pallas_call(functools.partial(weir_kernel, sections, steps, tiles, cap...  5.31 us
    ppermute x2, starting transfers between devices, swapped(): one = lax.ppermute(jnp.where(odd, first, last), axis, inner)  4.73 us
    pallas_call x1, Pallas kernels, local(): pl.pallas_call(functools.partial(apply_kernel, tiles, rows_each, row_coun...  4.54 us
    ppermute x2, starting transfers between devices, exchanged(): lax.ppermute(block, axis, [(i, i ^ 1 << step) for i in range(lax.axis_siz...  3.13 us
    ppermute x2, waiting for transfers between devices, swapped(): two = lax.ppermute(jnp.where(odd, last, first), axis, outer)  2.48 us
    pallas_call x1, Pallas kernels, local(): pl.pallas_call(functools.partial(cell_kernel, tiles, capacity, rows // 8,...  2.37 us
  transfers between devices with their start and end apart: 7, of which 3 were waited for; matrix products, arithmetic and copies ran while one was open for 0% of the time, Pallas kernels for 10%

profile of v6, /device:TPU:0, one launch (start us, length us, event | category | flops | bytes accessed | tf_op | source)
XLA Modules:
  0.0 44.3 jit_solution(3265687081350542427)
XLA Ops:
  0.6 1.5 %solve.1 = (f32[16,10,8,128]{3,2,1,0:T(8,128)S(1)}, f32[20,8,128]{2,1,0:T(8,128)S(1)}) custom-call(f32[512,128]{1,0:T(8,128)} %bitcast.36, f32[512,128]{1,0:T(8,128)} %bitcast.37, f32[512,128]{1,0:T(8,128)} %bitcast.38, f32[256,128]{1,0:T(8,128)} %bitcast.39), custom_call_target="tpu_custom_call" | custom-call | tf_op jit(solution)/shard_map/solve/pallas_call | solution.py:675
  2.2 0.5 %collective-permute-start = (f32[20,8,128]{2,1,0:T(8,128)S(1)}, f32[20,8,128]{2,1,0:T(8,128)S(1)}, u32[]{:S(2)}, u32[]{:S(2)}) collective-permute-start(f32[20,8,128]{2,1,0:T(8,128)S(1)} %get-tuple-element.23.own_ref), channel_id=1, source_target_pairs={{0,8},{8,0},{16,24},{24,16},{1,9},{9,1},{17,25},{25,17},{2,10},{10... | collective-permute-start | bytes 245768 | tf_op jit(solution)/shard_map/ppermute | solution.py:621
  2.7 1.5 %rank.1 = (s32[128,128]{1,0:T(8,128)S(1)}, f32[8,32,128]{2,1,0:T(8,128)S(1)}, s32[1]{0:T(128)}) custom-call(s32[128,128]{1,0:T(8,128)S(1)} %bitcast.35), custom_call_target="tpu_custom_call" | custom-call | flops 268435456 | bytes 131072 | tf_op jit(solution)/shard_map/rank/pallas_call | solution.py:698
  4.2 0.0 collective-permute-done.other_ref
  4.2 0.0 copy-start.1
  4.2 0.0 copy-start.2
  4.3 2.6 %collective-permute-start.1 = (f32[6,8,128]{2,1,0:T(8,128)S(1)}, f32[6,8,128]{2,1,0:T(8,128)S(1)}, u32[]{:S(2)}, u32[]{:S(2)}) collective-permute-start(f32[6,8,128]{2,1,0:T(8,128)S(1)} %get-tuple-element.24.refs_3_.refs_1_), channel_id=1, source_target_pairs={{0,16},{8,24},{16,0},{24,8},{1,17},{9,25},{17,1},{25,9},{2,18},{10... | collective-permute-start | bytes 73736 | tf_op jit(solution)/shard_map/ppermute | solution.py:621
  6.9 0.0 copy-done.2
  6.9 2.4 %cells.1.refs_8_ = f32[256,256]{1,0:T(8,128)S(1)} custom-call(s32[128,128]{1,0:T(8,128)S(1)} %get-tuple-element.27.refs_0_.refs_5_, s32[16,1024]{1,0:T(8,128)S(1)} %copy-done.1, s32[16,1024]{1,0:T(8,128)S(1)} %copy-done.2, f32[6,8,128]{2,1,0:T(8,128)S(1)} %get-tuple-element.24.refs_3_.refs_1_), custom_call_target="tpu_custom_call" | custom-call | flops 2147483648 | bytes 262144 | tf_op jit(solution)/shard_map/cells/pallas_call | solution.py:727
  9.3 0.0 collective-permute-done.1.refs_2_
  9.3 0.0 copy-done.3
  9.3 5.3 %weirs.1 = (f32[256,128]{1,0:T(8,128)}, f32[832,128]{1,0:T(8,128)}) custom-call(s32[1]{0:T(128)} %bitcast.position_ref.refs_0_, f32[6,8,128]{2,1,0:T(8,128)S(1)} %get-tuple-element.24.refs_3_.refs_1_, f32[6,8,128]{2,1,0:T(8,128)S(1)} %collective-permute-done.1.refs_2_, f32[20,8,128]{2,1,0:T(8,128)S(1)} %get-tuple-element.25.refs_3_, ...), custom_call_target="tpu_custom_call" | custom-call | tf_op jit(solution)/shard_map/weirs/pallas_call | solution.py:737
  14.6 0.0 copy-start
  14.6 0.0 copy-start.5
  14.7 0.0 copy-start.6
  14.7 0.0 copy-start.7
  14.7 0.0 copy-start.8
  14.7 0.0 copy-start.9
  14.7 5.7 %all-to-all-start = ((f32[32,26,1,128]{3,2,1,0:T(1,128)}), f32[32,26,1,128]{3,2,1,0:T(1,128)S(1)}, u32[]{:S(2)}, u32[]{:S(2)}) async-start(f32[32,26,1,128]{3,2,1,0:T(1,128)} %bitcast.21), calls=%async_computation | async-start | bytes 851968 | tf_op jit(solution)/shard_map/all_to_all | solution.py:757
  20.5 0.6 %stage.1 = (f32[5,32,512]{2,1,0:T(8,128)S(1)}, f32[8,128]{1,0:T(8,128)S(1)}, f32[8,128]{1,0:T(8,128)S(1)}) custom-call(f32[32,512]{1,0:T(8,128)S(1)} %copy-done.5, f32[32,512]{1,0:T(8,128)S(1)} %copy-done.6, f32[32,512]{1,0:T(8,128)S(1)} %copy-done.7, f32[32,512]{1,0:T(8,128)S(1)} %copy-done.8, s32[32,512]{1,0:T(8,128)S(1)} %copy-done.9, f32[256,128]{1,0:T(8,128)S(1)} %copy-done), custom_call_target="tpu_custom_call" | custom-call | tf_op jit(solution)/shard_map/stage/pallas_call | solution.py:760
  21.1 0.7 %collective-permute-start.3 = (f32[8,128]{1,0:T(8,128)S(1)}, f32[8,128]{1,0:T(8,128)S(1)}, u32[]{:S(2)}, u32[]{:S(2)}) collective-permute-start(f32[8,128]{1,0:T(8,128)S(1)} %get-tuple-element.48), channel_id=1, source_target_pairs={{0,0},{7,7},{1,2},{2,1},{3,4},{4,3},{5,6},{6,5},{8,8},{15,15},{9,1... | collective-permute-start | bytes 12296 | tf_op jit(solution)/shard_map/ppermute | solution.py:631
  21.8 4.5 %collective-permute-start.2 = (f32[8,128]{1,0:T(8,128)S(1)}, f32[8,128]{1,0:T(8,128)S(1)}, u32[]{:S(2)}, u32[]{:S(2)}) collective-permute-start(f32[8,128]{1,0:T(8,128)S(1)} %get-tuple-element.49), channel_id=1, source_target_pairs={{0,1},{1,0},{2,3},{3,2},{4,5},{5,4},{6,7},{7,6},{8,9},{9,8},{10,11... | collective-permute-start | bytes 12296 | tf_op jit(solution)/shard_map/ppermute | solution.py:632
  26.3 0.0 collective-permute-done.3
  26.3 1.6 %collective-permute-done.2 = f32[8,128]{1,0:T(8,128)S(1)} collective-permute-done((f32[8,128]{1,0:T(8,128)S(1)}, f32[8,128]{1,0:T(8,128)S(1)}, u32[]{:S(2)}, u32[]{:S(2)}) %collective-permute-start.2) | collective-permute-done | bytes 4128 | tf_op jit(solution)/shard_map/ppermute | solution.py:632
  28.0 6.7 %all-to-all-done = f32[32,26,1,128]{3,2,1,0:T(1,128)S(1)} async-done(((f32[32,26,1,128]{3,2,1,0:T(1,128)}), f32[32,26,1,128]{3,2,1,0:T(1,128)S(1)}, u32[]{:S(2)}, u32[]{:S(2)}) %all-to-all-start) | async-done | bytes 426016 | tf_op jit(solution)/shard_map/all_to_all | solution.py:757
  34.7 4.5 %apply.1 = (f32[32,512]{1,0:T(8,128)S(1)}, f32[8,640]{1,0:T(8,128)S(1)}, f32[8,640]{1,0:T(8,128)S(1)}, f32[5,32,128]{2,1,0:T(8,128)S(1)}) custom-call(f32[832,128]{1,0:T(8,128)S(1)} %bitcast.33, f32[5,32,512]{2,1,0:T(8,128)S(1)} %get-tuple-element.31.refs_1_, f32[8,128]{1,0:T(8,128)S(1)} %get-tuple-element.47.refs_2_, f32[8,128]{1,0:T(8,128)S(1)} %get-tuple-element.46.refs_3_), custom_call_target="tpu_custom_call" | custom-call | tf_op jit(solution)/shard_map/apply/pallas_call | solution.py:773
  39.2 0.5 %collective-permute-start.5 = (f32[8,640]{1,0:T(8,128)S(1)}, f32[8,640]{1,0:T(8,128)S(1)}, u32[]{:S(2)}, u32[]{:S(2)}) collective-permute-start(f32[8,640]{1,0:T(8,128)S(1)} %get-tuple-element.44), channel_id=1, source_target_pairs={{8,16},{16,8},{24,0},{0,24},{9,17},{17,9},{25,1},{1,25},{10,18},{1... | collective-permute-start | bytes 61448 | tf_op jit(solution)/shard_map/ppermute | solution.py:631
  39.8 0.2 collective-permute-start.4
  40.0 0.1 pad_add_fusion.refs_0_
  40.0 2.5 %collective-permute-done.5 = f32[8,640]{1,0:T(8,128)S(1)} collective-permute-done((f32[8,640]{1,0:T(8,128)S(1)}, f32[8,640]{1,0:T(8,128)S(1)}, u32[]{:S(2)}, u32[]{:S(2)}) %collective-permute-start.5) | collective-permute-done | bytes 20512 | tf_op jit(solution)/shard_map/ppermute | solution.py:631
  42.5 0.0 collective-permute-done.4
  42.5 1.7 %flood.1 = (f32[32,512]{1,0:T(8,128)}, f32[32,512]{1,0:T(8,128)}, f32[32,512]{1,0:T(8,128)}) custom-call(s32[4]{0:T(128)S(1)} %pad_add_fusion.refs_0_, f32[5,32,512]{2,1,0:T(8,128)S(1)} %get-tuple-element.31.refs_1_, f32[32,512]{1,0:T(8,128)S(1)} %get-tuple-element.35.refs_2_, f32[5,32,128]{2,1,0:T(8,128)S(1)} %get-tuple-element.36.refs_3_, ...), custom_call_target="tpu_custom_call" | custom-call | tf_op jit(solution)/shard_map/flood/pallas_call | solution.py:791
  (17 shorter events, 0.1 us)
Async XLA Ops:
  0.6 2.1 %copy-start.10 = (s32[1,1,16,1024,1]{3,4,2,1,0:T(1,128)S(1)}, s32[1,1,16,1024,1]{3,4,2,1,0:T(1,128)}, u32[]{:S(2)}) copy-start(s32[1,1,16,1024,1]{3,4,2,1,0:T(1,128)} %param.20) | copy-start | bytes 196612
  2.2 2.0 %collective-permute-start = (f32[20,8,128]{2,1,0:T(8,128)S(1)}, f32[20,8,128]{2,1,0:T(8,128)S(1)}, u32[]{:S(2)}, u32[]{:S(2)}) collective-permute-start(f32[20,8,128]{2,1,0:T(8,128)S(1)} %get-tuple-element.23.own_ref), channel_id=1, source_target_pairs={{0,8},{8,0},{16,24},{24,16},{1,9},{9,1},{17,25},{25,17},{2,10},{10... | collective-permute-start | bytes 245768 | tf_op jit(solution)/shard_map/ppermute | solution.py:621
  4.2 2.7 %copy-start.1 = (s32[16,1024]{1,0:T(8,128)S(1)}, s32[16,1024]{1,0:T(8,128)}, u32[]{:S(2)}) copy-start(s32[16,1024]{1,0:T(8,128)} %refs_11_.1) | copy-start | bytes 196612
  4.2 2.7 %copy-start.2 = (s32[16,1024]{1,0:T(8,128)S(1)}, s32[16,1024]{1,0:T(8,128)}, u32[]{:S(2)}) copy-start(s32[16,1024]{1,0:T(8,128)} %refs_12_.1) | copy-start | bytes 196612
  4.3 5.0 %collective-permute-start.1 = (f32[6,8,128]{2,1,0:T(8,128)S(1)}, f32[6,8,128]{2,1,0:T(8,128)S(1)}, u32[]{:S(2)}, u32[]{:S(2)}) collective-permute-start(f32[6,8,128]{2,1,0:T(8,128)S(1)} %get-tuple-element.24.refs_3_.refs_1_), channel_id=1, source_target_pairs={{0,16},{8,24},{16,0},{24,8},{1,17},{9,25},{17,1},{25,9},{2,18},{10... | collective-permute-start | bytes 73736 | tf_op jit(solution)/shard_map/ppermute | solution.py:621
  6.9 2.4 %copy-start.3 = (f32[16,1024]{1,0:T(8,128)S(1)}, f32[16,1024]{1,0:T(8,128)}, u32[]{:S(2)}) copy-start(f32[16,1024]{1,0:T(8,128)} %refs_9_.1) | copy-start | bytes 196612
  6.9 2.4 %copy-start.4 = (s32[16,1024]{1,0:T(8,128)S(1)}, s32[16,1024]{1,0:T(8,128)}, u32[]{:S(2)}) copy-start(s32[16,1024]{1,0:T(8,128)} %refs_10_.1) | copy-start | bytes 196612
  14.6 5.8 %copy-start = (f32[256,128]{1,0:T(8,128)S(1)}, f32[256,128]{1,0:T(8,128)}, u32[]{:S(2)}) copy-start(f32[256,128]{1,0:T(8,128)} %get-tuple-element.30.refs_5_) | copy-start | bytes 393220
  14.6 5.8 %copy-start.5 = (f32[32,512]{1,0:T(8,128)S(1)}, f32[32,512]{1,0:T(8,128)}, u32[]{:S(2)}) copy-start(f32[32,512]{1,0:T(8,128)} %refs_0_.1) | copy-start | bytes 196612
  14.7 5.8 %copy-start.6 = (f32[32,512]{1,0:T(8,128)S(1)}, f32[32,512]{1,0:T(8,128)}, u32[]{:S(2)}) copy-start(f32[32,512]{1,0:T(8,128)} %refs_1_.3) | copy-start | bytes 196612
  14.7 5.8 %copy-start.7 = (f32[32,512]{1,0:T(8,128)S(1)}, f32[32,512]{1,0:T(8,128)}, u32[]{:S(2)}) copy-start(f32[32,512]{1,0:T(8,128)} %refs_2_.3) | copy-start | bytes 196612
  14.7 5.8 %copy-start.8 = (f32[32,512]{1,0:T(8,128)S(1)}, f32[32,512]{1,0:T(8,128)}, u32[]{:S(2)}) copy-start(f32[32,512]{1,0:T(8,128)} %refs_3_.1) | copy-start | bytes 196612
  14.7 5.8 %copy-start.9 = (s32[32,512]{1,0:T(8,128)S(1)}, s32[32,512]{1,0:T(8,128)}, u32[]{:S(2)}) copy-start(s32[32,512]{1,0:T(8,128)} %refs_4_.1) | copy-start | bytes 196612
  14.7 20.0 %all-to-all-start = ((f32[32,26,1,128]{3,2,1,0:T(1,128)}), f32[32,26,1,128]{3,2,1,0:T(1,128)S(1)}, u32[]{:S(2)}, u32[]{:S(2)}) async-start(f32[32,26,1,128]{3,2,1,0:T(1,128)} %bitcast.21), calls=%async_computation | async-start | bytes 851968 | tf_op jit(solution)/shard_map/all_to_all | solution.py:757
  21.1 5.2 %collective-permute-start.3 = (f32[8,128]{1,0:T(8,128)S(1)}, f32[8,128]{1,0:T(8,128)S(1)}, u32[]{:S(2)}, u32[]{:S(2)}) collective-permute-start(f32[8,128]{1,0:T(8,128)S(1)} %get-tuple-element.48), channel_id=1, source_target_pairs={{0,0},{7,7},{1,2},{2,1},{3,4},{4,3},{5,6},{6,5},{8,8},{15,15},{9,1... | collective-permute-start | bytes 12296 | tf_op jit(solution)/shard_map/ppermute | solution.py:631
  21.8 6.2 %collective-permute-start.2 = (f32[8,128]{1,0:T(8,128)S(1)}, f32[8,128]{1,0:T(8,128)S(1)}, u32[]{:S(2)}, u32[]{:S(2)}) collective-permute-start(f32[8,128]{1,0:T(8,128)S(1)} %get-tuple-element.49), channel_id=1, source_target_pairs={{0,1},{1,0},{2,3},{3,2},{4,5},{5,4},{6,7},{7,6},{8,9},{9,8},{10,11... | collective-permute-start | bytes 12296 | tf_op jit(solution)/shard_map/ppermute | solution.py:632
  39.2 3.3 %collective-permute-start.5 = (f32[8,640]{1,0:T(8,128)S(1)}, f32[8,640]{1,0:T(8,128)S(1)}, u32[]{:S(2)}, u32[]{:S(2)}) collective-permute-start(f32[8,640]{1,0:T(8,128)S(1)} %get-tuple-element.44), channel_id=1, source_target_pairs={{8,16},{16,8},{24,0},{0,24},{9,17},{17,9},{25,1},{1,25},{10,18},{1... | collective-permute-start | bytes 61448 | tf_op jit(solution)/shard_map/ppermute | solution.py:631
  39.8 2.7 %collective-permute-start.4 = (f32[8,640]{1,0:T(8,128)S(1)}, f32[8,640]{1,0:T(8,128)S(1)}, u32[]{:S(2)}, u32[]{:S(2)}) collective-permute-start(f32[8,640]{1,0:T(8,128)S(1)} %get-tuple-element.45), channel_id=1, source_target_pairs={{0,8},{8,0},{16,24},{24,16},{1,9},{9,1},{17,25},{25,17},{2,10},{10... | collective-permute-start | bytes 61448 | tf_op jit(solution)/shard_map/ppermute | solution.py:632
